TPU v7x, 32 devices: a whole 2x2x4 slice. The times are simulated.
32 devices in a mesh: groups: 2 (over y), feat: 8 (over z, x), pair: 2 (over core).
Axes of the slice: x: 2, y: 2, z: 4, core: 2. Of those that a mesh axis runs over, the one named last changes fastest.
Arguments:
- codes: bfloat16 [2048, 2, 8192], P(('groups', 'feat')), parts along dimension 0, may hold values from 0 to 2
- block_ids: int32 [2048, 2], P(('groups', 'feat')), parts along dimension 0, may hold values from 0 to 3, all different within a row; in each aligned block of 128 rows (0 to 127, 128 to 255, ...) at most 128 rows name the same one
- decoder: bfloat16 [65536, 4096], P('feat', 'pair'), may hold values from -0.046875 to 0.046875
- targets: bfloat16 [2048, 2, 4096], P(('groups', 'feat'), None, 'pair'), parts along dimension 0, may hold values from -6 to 6
Outputs:
- reconstruction: bfloat16 [2048, 2, 4096], P(('groups', 'feat'), None, 'pair'), parts along dimension 0
- code_grad: bfloat16 [2048, 2, 8192], P(('groups', 'feat')), parts along dimension 0
- weight_grad: bfloat16 [131072, 4096], P(('groups', 'feat'), 'pair'), parts along dimension 0
There are 2 independent parts, one for each index of `groups`. A program takes and returns all parts, laid end to end along the dimension named above; an argument that names none is the same for every part. Nothing has to cross between parts.
Inputs may be any that keep to these rules, and one draw needn't show every extreme that they name: `block_ids`: each token names 2 different blocks. The 128 tokens of one index of feat name one block at most 128 times, and in every draw some block is named exactly 128 times by the tokens of some index.
All inputs are finite; a program needn't handle non-finite values.
Results may differ from a plain program's by a relative error of at most 0.006.
Values may be sent and summed in bfloat16 or wider, within the bound.
No kernel may reach another device: no remote copies, remote signals or barrier semaphores. Data moves between devices by JAX's collectives and lax.ppermute only.
A program may use at most 256 MiB of HBM per device.

v0:
```python
import jax
import jax.numpy as jnp
from jax import lax
from jax.sharding import PartitionSpec as P

PAIRS = 2


error_scale = 0.125


def local(codes, block_ids, decoder, targets):
    tok_rows, per_token, block_width = codes.shape
    half_width = decoder.shape[1]
    owners = lax.axis_size("feat")
    blocks = owners // PAIRS
    capacity = 2 * tok_rows * per_token // blocks
    flat_ids = block_ids.reshape(-1)
    matches = (flat_ids[:, None] == jnp.arange(blocks, dtype=jnp.int32)[None, :]).astype(jnp.int32)
    ranking = jnp.sum((jnp.cumsum(matches, axis=0) - 1) * matches, axis=1)
    slot_lists = [(target * blocks + flat_ids) * capacity + ranking for target in range(PAIRS)]
    values = codes.reshape(-1, block_width)
    outgoing = jnp.zeros((owners * capacity, values.shape[1]), jnp.bfloat16)
    for slot_index in slot_lists:
        outgoing = outgoing.at[slot_index].set(values)
    outgoing = outgoing.reshape(owners, capacity, values.shape[1])
    arrived = lax.all_to_all(outgoing, "feat", split_axis=0, concat_axis=0, tiled=True)
    partial_rows = jnp.einsum("snb,bd->snd", arrived, decoder, preferred_element_type=jnp.float32)
    sent_back = lax.all_to_all(
        partial_rows.astype(jnp.bfloat16), "feat", split_axis=0, concat_axis=0, tiled=True
    )
    returned = sent_back
    returned_flat = returned.reshape(owners * capacity, half_width)
    rebuilt = jnp.stack(
        [
            jnp.sum(
                returned_flat[slot_index]
                .astype(jnp.float32)
                .reshape(tok_rows, per_token, half_width),
                axis=1,
            )
            for slot_index in slot_lists
        ],
        axis=1,
    )
    error_grad = ((rebuilt - targets.astype(jnp.float32)) * error_scale).astype(jnp.bfloat16)
    grad_out = jnp.zeros((owners * capacity, half_width), jnp.bfloat16)
    for target in range(PAIRS):
        grad_out = grad_out.at[slot_lists[target]].set(
            jnp.repeat(error_grad[:, target], per_token, axis=0)
        )
    grad_out = grad_out.reshape(owners, capacity, half_width)
    arrived_grad = lax.all_to_all(grad_out, "feat", split_axis=0, concat_axis=0, tiled=True)
    summed = jnp.einsum("snd,bd->snb", arrived_grad, decoder, preferred_element_type=jnp.float32)
    summed = lax.psum(summed, "pair")
    sent_back = lax.all_to_all(
        summed.astype(jnp.bfloat16), "feat", split_axis=0, concat_axis=0, tiled=True
    )
    weight_grad = lax.dot_general(
        arrived.reshape(-1, block_width),
        arrived_grad.reshape(-1, half_width),
        (((0,), (0,)), ((), ())),
        preferred_element_type=jnp.float32,
    ).astype(jnp.bfloat16)
    code_flat = sent_back.reshape(owners * capacity, sent_back.shape[2])
    code_total = code_flat[slot_lists[0]].astype(jnp.float32)
    for slot_index in slot_lists[1:]:
        code_total = code_total + code_flat[slot_index].astype(jnp.float32)
    code_grad = code_total.astype(jnp.bfloat16).reshape(tok_rows, per_token, sent_back.shape[2])
    return (rebuilt.astype(jnp.bfloat16), code_grad, weight_grad)


def solution(mesh):
    return jax.shard_map(
        local,
        mesh=mesh,
        in_specs=(
            P(("groups", "feat"), None, None),
            P(("groups", "feat"), None),
            P("feat", "pair"),
            P(("groups", "feat"), None, "pair"),
        ),
        out_specs=(
            P(("groups", "feat"), None, "pair"),
            P(("groups", "feat"), None, None),
            P(("groups", "feat"), "pair"),
        ),
        check_vma=False,
    )
```

profile of v0, /device:TPU:9, one launch (start us, length us, event | category | flops | bytes accessed | tf_op | source)
XLA Modules:
  0.0 1250.9 jit_solution(13048977734132695825)
XLA Ops:
  0.6 0.7 add_multiply_fusion
  1.3 0.8 copy.11
  2.1 0.1 eq.29
  2.2 0.1 eq.25
  2.4 0.1 copy.15
  2.5 0.1 mul.39
  2.7 1.2 reduce-window.6
  3.9 0.1 slice.24
  4.0 0.1 copy.13
  4.1 0.1 copy.14
  4.2 0.1 add_bitcast_fusion
  4.3 0.1 copy.10
  4.4 0.1 mul.36
  4.5 7.2 reshape.179
  11.7 17.3 %scatter_custom_fusion = bf16[1024,8192]{1,0:T(8,128)(2,1)} fusion(s32[256]{0:T(256)S(1)} %bitcast.50, bf16[256,8192]{1,0:T(8,128)(2,1)} %reshape.179, bf16[]{:T(256)} %constant.8.clone.1), kind=kCustom, calls=%fused_computation.14 | custom fusion | bytes 16777728 | tf_op jit(solution)/shard_map/scatter | solution.py:25
  29.1 23.3 %scatter_fusion = bf16[1024,8192]{1,0:T(8,128)(2,1)} fusion(bf16[1024,8192]{1,0:T(8,128)(2,1)} %scatter_custom_fusion, s32[256]{0:T(256)S(1)} %bitcast.47, bf16[256,8192]{1,0:T(8,128)(2,1)} %reshape.179), kind=kCustom, calls=%fused_computation.5 | custom fusion | bytes 12583936 | tf_op jit(solution)/shard_map/scatter | solution.py:25
  52.3 369.0 %all_to_all.20 = bf16[8,128,8192]{2,1,0:T(8,128)(2,1)} all-to-all(bf16[8,128,8192]{2,1,0:T(8,128)(2,1)} %bitcast.41), channel_id=1, replica_groups=mesh['groups'=2,'feat'=8,'pair'=2] {'feat'}, dimensions={0} | all-to-all | bytes 33554432 | tf_op jit(solution)/shard_map/all_to_all | solution.py:27
  421.3 44.4 %fusion.6 = bf16[8,128,2048]{2,1,0:T(8,128)(2,1)} fusion(bf16[8,128,8192]{2,1,0:T(8,128)(2,1)} %all_to_all.20, bf16[8192,2048]{1,0:T(8,128)(2,1)} %param.6), kind=kOutput, calls=%fused_computation.16 | convolution fusion | flops 34361835520 | bytes 54525952 | tf_op jit(solution)/shard_map/snb,bd->snd/dot_general | solution.py:28
  465.7 5.9 all-to-all-start.1
  471.6 0.0 copy-start.3
  471.6 0.0 copy-start.2
  471.6 91.4 %all-to-all-done.1 = bf16[8,128,2048]{2,1,0:T(8,128)(2,1)} async-done(((bf16[8,128,2048]{2,1,0:T(8,128)(2,1)}), bf16[8,128,2048]{2,1,0:T(8,128)(2,1)}, u32[]{:S(2)}, u32[]{:S(2)}) %all-to-all-start.1) | async-done | bytes 4194336 | tf_op jit(solution)/shard_map/all_to_all | solution.py:29
  563.0 0.0 copy-done.3
  563.0 5.1 gather_fusion.1
  568.1 1.3 reshape.134
  569.4 0.0 copy-done.2
  569.5 5.1 gather_fusion
  574.6 2.5 reshape.133
  577.1 2.8 reduce_sum.32
  579.8 4.1 reduce_sum.31
  584.0 1.9 multiply_convert_fusion
  585.8 0.9 slice_bitcast_fusion
  586.7 0.6 broadcast_in_dim.10
  587.3 1.2 reshape.187
  588.5 0.0 copy-start.1
  588.5 5.6 scatter_custom_fusion.2
  594.1 0.0 copy-done.1
  594.1 1.6 broadcast_in_dim.11
  595.7 1.8 reshape.195
  597.6 7.1 scatter_fusion.1
  604.6 97.0 %all_to_all.21 = bf16[8,128,2048]{2,1,0:T(8,128)(2,1)S(1)} all-to-all(bf16[8,128,2048]{2,1,0:T(8,128)(2,1)} %bitcast.42), channel_id=1, replica_groups=mesh['groups'=2,'feat'=8,'pair'=2] {'feat'}, dimensions={0} | all-to-all | bytes 8388608 | tf_op jit(solution)/shard_map/all_to_all | solution.py:53
  701.6 0.0 copy-start
  701.6 2.0 copy-done
  703.7 40.5 %fusion = f32[8,128,8192]{2,1,0:T(8,128)} fusion(bf16[8,128,2048]{2,1,0:T(8,128)(2,1)S(1)} %all_to_all.21, bf16[8192,2048]{1,0:T(8,128)(2,1)} %param.6), kind=kOutput, calls=%fused_computation.9 | convolution fusion | flops 34359738368 | bytes 71303168 | tf_op jit(solution)/shard_map/snd,bd->snb/dot_general | solution.py:54
  744.2 89.8 %all-reduce.1 = bf16[8,128,8192]{2,1,0:T(8,128)(2,1)} all-reduce(f32[8,128,8192]{2,1,0:T(8,128)} %fusion), channel_id=1, replica_groups=mesh['groups'=2,'feat'=8,'pair'=2] {'pair'}, use_global_device_ids=true, to_apply=%region_9.10 | all-reduce | flops 8388608 | bytes 50331648 | tf_op jit(solution)/shard_map/psum | solution.py:55
  834.0 6.5 all-to-all-start.3
  840.5 0.1 fusion.11
  840.6 2.0 copy.18
  842.7 45.5 %bitcast_convert_fusion = bf16[8192,2048]{1,0:T(8,128)(2,1)} fusion(bf16[8,128,8192]{2,1,0:T(8,128)(2,1)} %all_to_all.20, bf16[8,128,2048]{2,1,0:T(8,128)(2,1)} %copy-done), kind=kOutput, calls=%fused_computation.8 | convolution fusion | flops 34376515584 | bytes 54525952 | tf_op jit(solution)/shard_map/dot_general | solution.py:59
  888.2 313.4 %all-to-all-done.3 = bf16[8,128,8192]{2,1,0:T(8,128)(2,1)} async-done(((bf16[8,128,8192]{2,1,0:T(8,128)(2,1)}), bf16[8,128,8192]{2,1,0:T(8,128)(2,1)}, u32[]{:S(2)}, u32[]{:S(2)}) %all-to-all-start.3) | async-done | bytes 16777248 | tf_op jit(solution)/shard_map/all_to_all | solution.py:56
  1201.6 17.1 %gather_fusion.3 = bf16[256,8192]{1,0:T(8,128)(2,1)} fusion(bf16[1024,8192]{1,0:T(8,128)(2,1)} %bitcast.13, s32[1024]{0:T(1024)} %copy-done.3), kind=kCustom, calls=%fused_computation.3 | custom fusion | bytes 8389632 | tf_op jit(solution)/shard_map/gather | solution.py:68
  1218.6 17.2 %gather_fusion.2 = bf16[256,8192]{1,0:T(8,128)(2,1)} fusion(bf16[1024,8192]{1,0:T(8,128)(2,1)} %bitcast.13, s32[1024]{0:T(1024)} %copy-done.2), kind=kCustom, calls=%fused_computation.2 | custom fusion | bytes 8389632 | tf_op jit(solution)/shard_map/gather | solution.py:66
  1235.9 7.0 add_convert_fusion
  1242.8 7.6 convert_element_type.67
  (7 shorter events, 0.1 us)
Async XLA Ops:
  465.7 97.3 %all-to-all-start.1 = ((bf16[8,128,2048]{2,1,0:T(8,128)(2,1)}), bf16[8,128,2048]{2,1,0:T(8,128)(2,1)}, u32[]{:S(2)}, u32[]{:S(2)}) async-start(bf16[8,128,2048]{2,1,0:T(8,128)(2,1)} %fusion.6), calls=%async_computation.1 | async-start | bytes 8388608 | tf_op jit(solution)/shard_map/all_to_all | solution.py:29
  471.6 91.4 %copy-start.3 = (s32[1024]{0:T(1024)}, s32[1024]{0:T(1024)S(1)}, u32[]{:S(2)}) copy-start(s32[1024]{0:T(1024)S(1)} %pad_clamp_fusion) | copy-start | bytes 12292
  471.6 97.8 %copy-start.2 = (s32[1024]{0:T(1024)}, s32[1024]{0:T(1024)S(1)}, u32[]{:S(2)}) copy-start(s32[1024]{0:T(1024)S(1)} %pad_clamp_fusion.1) | copy-start | bytes 12292
  588.5 5.6 copy-start.1
  701.6 2.0 copy-start
  834.0 367.6 %all-to-all-start.3 = ((bf16[8,128,8192]{2,1,0:T(8,128)(2,1)}), bf16[8,128,8192]{2,1,0:T(8,128)(2,1)}, u32[]{:S(2)}, u32[]{:S(2)}) async-start(bf16[8,128,8192]{2,1,0:T(8,128)(2,1)} %all-reduce.1), calls=%async_computation.3 | async-start | bytes 33554432 | tf_op jit(solution)/shard_map/all_to_all | solution.py:56
where the time goes:
time: 1260 us; the launch traced here: 1250 us
  blocking collectives  556 us (44%)
  waiting for transfers between devices  405 us (32%)
  matrix products  130 us (10%)
  local copies, waits for them, and re-layouts  128 us (10%)
  other arithmetic  17.9 us (1%)
    all_to_all x1, blocking collectives, local(): lax.all_to_all(outgoing, 'feat', split_axis=0, concat_axis=0, tiled=True)  369 us
    all_to_all x1, waiting for transfers between devices, local(): lax.all_to_all(summed.astype(jnp.bfloat16), 'feat', split_axis=0, concat_...  313 us
    all_to_all x1, blocking collectives, local(): lax.all_to_all(grad_out, 'feat', split_axis=0, concat_axis=0, tiled=True)  97 us
    all_to_all x1, waiting for transfers between devices, local(): lax.all_to_all(partial_rows.astype(jnp.bfloat16), 'feat', split_axis=0, c...  91.4 us
    psum x1, blocking collectives, local(): summed = lax.psum(summed, 'pair')  89.8 us
    dot_general x1, matrix products, local(): lax.dot_general(arrived.reshape(-1, block_width), arrived_grad.reshape(-1...  45.5 us
    dot_general x1, matrix products, local(): jnp.einsum('snb,bd->snd', arrived, decoder, preferred_element_type=jnp.fl...  44.4 us
    scatter x2, local copies, waits for them, and re-layouts, local(): outgoing = outgoing.at[slot_index].set(values)  40.6 us
  transfers between devices with their start and end apart: 2, of which 2 were waited for; matrix products, arithmetic and copies ran while one was open for 4% of the time, Pallas kernels for 0%

commit v1 on v0

--- a/solution.py
+++ b/solution.py
@@ -1,15 +1,20 @@
 import jax
 import jax.numpy as jnp
 from jax import lax
+from jax.experimental import pallas as pl
+from jax.experimental.pallas import tpu as pltpu
 from jax.sharding import PartitionSpec as P
 
 PAIRS = 2
+SPLIT = (1, 1)
+STRIP = 1024
+VMEM_LIMIT = 48 * 1024 * 1024
 
 
 error_scale = 0.125
 
 
-def local(codes, block_ids, decoder, targets):
+def slotted(codes, block_ids, decoder, targets):
     tok_rows, per_token, block_width = codes.shape
     half_width = decoder.shape[1]
     owners = lax.axis_size("feat")
@@ -29,8 +34,7 @@
     sent_back = lax.all_to_all(
         partial_rows.astype(jnp.bfloat16), "feat", split_axis=0, concat_axis=0, tiled=True
     )
-    returned = sent_back
-    returned_flat = returned.reshape(owners * capacity, half_width)
+    returned_flat = sent_back.reshape(owners * capacity, half_width)
     rebuilt = jnp.stack(
         [
             jnp.sum(
@@ -70,9 +74,518 @@
     return (rebuilt.astype(jnp.bfloat16), code_grad, weight_grad)
 
 
+def add(*terms):
+    return sum(term.astype(jnp.float32) for term in terms).astype(jnp.bfloat16)
+
+
+def call(kernel, core, operands, specs, grid, outs, out_specs, scratch, flops, moved, alias={}):
+    return pl.pallas_call(
+        kernel,
+        grid_spec=pltpu.PrefetchScalarGridSpec(
+            num_scalar_prefetch=1,
+            grid=(grid,),
+            in_specs=specs,
+            out_specs=out_specs,
+            scratch_shapes=scratch,
+        ),
+        out_shape=outs,
+        input_output_aliases=alias,
+        compiler_params=pltpu.CompilerParams(
+            vmem_limit_bytes=VMEM_LIMIT, dimension_semantics=("arbitrary",)
+        ),
+        cost_estimate=pl.CostEstimate(flops=flops, bytes_accessed=moved, transcendentals=0),
+    )(core, *operands)
+
+
+def rebuild(core, own, other, decoder):
+    rows, half = own.shape
+    depth = decoder.shape[1]
+    strips = half // min(STRIP, half)
+    kept = rows // 2
+
+    def kernel(core_ref, own_ref, other_ref, decoder_ref, *rest):
+        upper_ref, lower_ref, total = rest[-3:]
+        step = pl.program_id(0)
+
+        @pl.when(step == 0)
+        def _():
+            total[...] = jnp.zeros_like(total)
+
+        @pl.when(step < strips)
+        def _():
+            total[...] += jnp.dot(
+                own_ref[...], decoder_ref[...], preferred_element_type=jnp.float32
+            )
+
+        @pl.when(step >= strips)
+        def _():
+            total[...] += jnp.dot(
+                other_ref[...], decoder_ref[...], preferred_element_type=jnp.float32
+            )
+
+        @pl.when(step == 2 * strips - 1)
+        def _():
+            upper_ref[...] = total[:kept].astype(jnp.bfloat16)
+            lower_ref[...] = total[kept:].astype(jnp.bfloat16)
+
+    def strip(step, core_ref):
+        side = jnp.where(step < strips, core_ref[0], 1 - core_ref[0])
+        return side * strips + lax.rem(step, strips), 0
+
+    out = jax.ShapeDtypeStruct((kept, depth), jnp.bfloat16)
+    return call(
+        kernel,
+        core,
+        [own, other, decoder],
+        [
+            pl.BlockSpec((rows, STRIP), lambda i, c: (0, jnp.minimum(i, strips - 1))),
+            pl.BlockSpec((rows, STRIP), lambda i, c: (0, jnp.maximum(i - strips, 0))),
+            pl.BlockSpec((STRIP, depth), strip),
+        ],
+        2 * strips,
+        [out, out],
+        [pl.BlockSpec((kept, depth), lambda i, c: (0, 0))] * 2,
+        [pltpu.VMEM((rows, depth), jnp.float32)],
+        4 * rows * half * depth,
+        4 * half * depth,
+    )
+
+
+def code_terms(core, upper, lower, decoder):
+    kept, depth = upper.shape
+    half = decoder.shape[0] // 2
+    strips = half // min(STRIP, half)
+    rows = 2 * kept
+
+    def kernel(core_ref, upper_ref, lower_ref, decoder_ref, give_ref, keep_ref, grads):
+        step = pl.program_id(0)
+
+        @pl.when(step == 0)
+        def _():
+            grads[:kept, :] = upper_ref[...]
+            grads[kept:, :] = lower_ref[...]
+
+        product = lax.dot_general(
+            grads[...],
+            decoder_ref[...],
+            (((1,), (1,)), ((), ())),
+            preferred_element_type=jnp.float32,
+        ).astype(jnp.bfloat16)
+
+        @pl.when(step < strips)
+        def _():
+            give_ref[...] = product
+
+        @pl.when(step >= strips)
+        def _():
+            keep_ref[...] = product
+
+    def strip(step, core_ref):
+        side = jnp.where(step < strips, 1 - core_ref[0], core_ref[0])
+        return side * strips + lax.rem(step, strips), 0
+
+    out = jax.ShapeDtypeStruct((rows, half), jnp.bfloat16)
+    return call(
+        kernel,
+        core,
+        [upper, lower, decoder],
+        [pl.BlockSpec((kept, depth), lambda i, c: (0, 0))] * 2
+        + [pl.BlockSpec((STRIP, depth), strip)],
+        2 * strips,
+        [out, out],
+        [
+            pl.BlockSpec((rows, STRIP), lambda i, c: (0, jnp.minimum(i, strips - 1))),
+            pl.BlockSpec((rows, STRIP), lambda i, c: (0, jnp.maximum(i - strips, 0))),
+        ],
+        [pltpu.VMEM((rows, depth), jnp.bfloat16)],
+        4 * rows * half * depth,
+        4 * half * depth,
+    )
+
+
+def weight_half(side, rows, grads, base=None):
+    half = rows[0].shape[1]
+    depth = grads[0].shape[1]
+    strips = half // min(STRIP, half)
+    sizes = [piece.shape[0] for piece in grads]
+    total = sum(sizes)
+    pieces = len(rows)
+
+    def kernel(side_ref, *refs):
+        row_refs, grad_refs = refs[:pieces], refs[pieces : pieces + len(grads)]
+        out_ref, stacked = refs[-2:]
+
+        @pl.when(pl.program_id(0) == 0)
+        def _():
+            at = 0
+            for size, ref in zip(sizes, grad_refs):
+                stacked[at : at + size, :] = ref[...]
+                at += size
+
+        left = jnp.concatenate([ref[...] for ref in row_refs], axis=0)
+        out_ref[...] = lax.dot_general(
+            left, stacked[...], (((0,), (0,)), ((), ())), preferred_element_type=jnp.float32
+        ).astype(jnp.bfloat16)
+
+    operands = rows + grads
+    specs = [pl.BlockSpec((piece.shape[0], STRIP), lambda i, c: (0, i)) for piece in rows]
+    specs += [pl.BlockSpec(piece.shape, lambda i, c: (0, 0)) for piece in grads]
+    alias = {}
+    if base is not None:
+        alias = {1 + len(operands): 0}
+        operands = operands + [base]
+        specs = specs + [pl.BlockSpec(memory_space=pl.ANY)]
+    return call(
+        kernel,
+        side,
+        operands,
+        specs,
+        strips,
+        jax.ShapeDtypeStruct((2 * half, depth), jnp.bfloat16),
+        pl.BlockSpec((STRIP, depth), lambda i, c: (c[0] * strips + i, 0)),
+        [pltpu.VMEM((total, depth), jnp.bfloat16)],
+        2 * total * half * depth,
+        2 * half * (depth + total),
+        alias,
+    )
+
+
+NEAR, FAR = 0, 1
+
+
+class Bag:
+    def __init__(self):
+        self.heres, self.theres, self.waits, self.ys = ([None, None] for _ in range(4))
+
+
+def dense(codes, block_ids, decoder, targets):
+    tok_rows, per_token, width = codes.shape
+    half = width // 2
+    me = lax.axis_index("feat")
+    core = lax.axis_index("pair")
+    core_at = core.astype(jnp.int32).reshape(1)
+    layer = me // 2
+    target = layer // 2
+    inner = (layer == 1) | (layer == 2)
+    block = me % 4
+    sibling = block ^ 1
+    unit = tok_rows // sum(SPLIT)
+    starts = (0, SPLIT[0] * unit)
+    counts = (SPLIT[0] * unit, tok_rows - SPLIT[0] * unit)
+
+    def over_layers(pairs):
+        return [(a * 2 + x, b * 2 + x) for a, b in pairs for x in range(2)]
+
+    def feat(value, perm):
+        return lax.ppermute(value, "feat", perm)
+
+    NEIGHBOUR = over_layers([(0, 1), (1, 0), (2, 3), (3, 2)])
+    MIDDLE = over_layers([(1, 2), (2, 1)])
+    OUTWARD = over_layers([(1, 0), (2, 3)])
+    INWARD = over_layers([(0, 1), (3, 2)])
+    MIRROR = over_layers([(0, 3), (3, 0), (1, 2), (2, 1)])
+    ACROSS = over_layers([(0, 2), (2, 0), (1, 3), (3, 1)])
+    COLUMN = [(i, i ^ 1) for i in range(8)]
+
+    def other_core(value):
+        return lax.ppermute(value, "pair", [(0, 1), (1, 0)])
+
+    def pick(value, ids, wanted):
+        hits = (ids == wanted)[:, :, None]
+        return jnp.where(hits[:, 0], value[0], jnp.where(hits[:, 1], value[1], 0))
+
+    def stack(*values):
+        return jnp.concatenate(values, axis=0)
+
+    def part_of(value, i):
+        return value[starts[i] : starts[i] + counts[i]]
+
+    def error(rebuilt, wanted):
+        gap = rebuilt.astype(jnp.float32) - wanted.astype(jnp.float32)
+        return (gap * error_scale).astype(jnp.bfloat16)
+
+    parts = (Bag(), Bag())
+    kinds = tuple((Bag(), Bag()) for kind in (NEAR, FAR))
+    token = []
+
+    def gate(*values):
+        out = lax.optimization_barrier((*values, *token))[: len(values)]
+        return out[0] if len(values) == 1 else out
+
+    def done(*values):
+        token[:] = values
+
+    def prep(i):
+        source = codes if i == 0 else gate(codes)
+        own = lax.dynamic_slice(source, (starts[i], 0, core * half), (counts[i], per_token, half))
+        own = jnp.swapaxes(own, 0, 1)
+        parts[i].own = own
+        if i == 0:
+            parts[i].near = feat(own, NEIGHBOUR)
+            parts[i].mid = feat(own, MIDDLE)
+        done(own)
+
+    def ids(i):
+        parts[i].near, parts[i].mid, mine = gate(parts[i].near, parts[i].mid, block_ids)
+        near, mirror, across = feat(mine, NEIGHBOUR), feat(mine, MIRROR), feat(mine, ACROSS)
+        parts[0].slots = [
+            block_ids,
+            near,
+            jnp.where(inner, mirror, across),
+            jnp.where(inner, across, mirror),
+        ]
+        done(mine)
+
+    def aims(i):
+        wanted = part_of(gate(targets), i)
+        kinds[NEAR][i].aim = lax.dynamic_index_in_dim(wanted, target, 1, keepdims=False)
+        far = lax.dynamic_index_in_dim(wanted, 1 - target, 1, keepdims=False)
+        kinds[FAR][i].aim = feat(far, MIRROR)
+        done(far, kinds[NEAR][i].aim)
+
+    def named(i, slot):
+        return part_of(parts[0].slots[slot], i)
+
+    def in1(i):
+        near, mid = gate(parts[i].near, parts[i].mid)
+        parts[i].in_end = feat(mid, OUTWARD)
+        parts[i].out_mid = feat(near, MIDDLE)
+        parts[i].near, parts[i].mid = near, mid
+        done(near, mid)
+
+    def in1x(i):
+        own, near = gate(parts[i].own, parts[i].near)
+        a, b = named(i, 0), named(i, 1)
+        crossing = stack(pick(own, a, sibling), pick(near, b, sibling))
+        kinds[NEAR][i].crossed = feat(crossing, COLUMN)
+        kinds[NEAR][i].kept = stack(pick(own, a, block), pick(near, b, block))
+        done(crossing, kinds[NEAR][i].kept)
+
+    def in2(i):
+        in_end, out_mid, mid = gate(parts[i].in_end, parts[i].out_mid, parts[i].mid)
+        parts[i].out_end = feat(out_mid, OUTWARD)
+        parts[i].out_mid = out_mid
+        if i == 0:
+            parts[1].mid = feat(gate(parts[1].own), MIDDLE)
+        far_in = jnp.where(inner, mid, in_end)
+        crossing = pick(far_in, named(i, 2), sibling)
+        parts[i].in_crossed = feat(crossing, COLUMN)
+        parts[i].in_kept = pick(far_in, named(i, 2), block)
+        done(crossing, parts[i].in_kept)
+
+    def in3(i):
+        kept, crossed = gate(kinds[NEAR][i].kept, kinds[NEAR][i].crossed)
+        rows = stack(kept, crossed)
+        kinds[NEAR][i].rows = rows
+        kinds[NEAR][i].rows_other = other_core(rows)
+        done(rows)
+
+    def in4(i):
+        out_end, out_mid = gate(parts[i].out_end, parts[i].out_mid)
+        if i == 0:
+            parts[1].near = feat(gate(parts[1].own), NEIGHBOUR)
+        far_out = jnp.where(inner, out_mid, out_end)
+        crossing = pick(far_out, named(i, 3), sibling)
+        parts[i].out_crossed = feat(crossing, COLUMN)
+        parts[i].out_kept = pick(far_out, named(i, 3), block)
+        done(crossing, parts[i].out_kept)
+
+    def in5(i):
+        rows = stack(*gate(parts[i].in_kept, parts[i].out_kept, parts[i].in_crossed, parts[i].out_crossed))
+        kinds[FAR][i].rows = rows
+        kinds[FAR][i].rows_other = other_core(rows)
+        done(rows)
+
+    def sums(kind):
+        def step(i):
+            own, other = gate(kinds[kind][i].rows, kinds[kind][i].rows_other)
+            upper, lower = rebuild(core_at, own, other, decoder)
+            kinds[kind][i].rows, kinds[kind][i].rows_other = own, other
+            kinds[kind][i].upper = upper
+            kinds[kind][i].lower = feat(lower, COLUMN)
+            done(upper, lower)
+
+        return step
+
+    def err1(kind):
+        def step(i):
+            total = add(*gate(kinds[kind][i].upper, kinds[kind][i].lower))
+            first, second = total[: counts[i]], total[counts[i] :]
+            keep, send = first, second
+            if kind == FAR:
+                keep, send = jnp.where(inner, first, second), jnp.where(inner, second, first)
+            kinds[kind][i].keep = keep
+            kinds[kind][i].sent = feat(send, NEIGHBOUR)
+            done(keep, send)
+
+        return step
+
+    def err2(kind):
+        def step(i):
+            rebuilt = add(*gate(kinds[kind][i].keep, kinds[kind][i].sent))
+            grad = error(rebuilt, gate(kinds[kind][i].aim))
+            kinds[kind][i].rebuilt = rebuilt
+            kinds[kind][i].grad = grad
+            kinds[kind][i].grad_sent = feat(grad, NEIGHBOUR)
+            done(grad)
+
+        return step
+
+    def err3(kind):
+        def step(i):
+            grad, sent = gate(kinds[kind][i].grad, kinds[kind][i].grad_sent)
+            if kind == FAR:
+                grad, sent = jnp.where(inner, grad, sent), jnp.where(inner, sent, grad)
+            grads = stack(grad, sent)
+            kinds[kind][i].grads = grads
+            kinds[kind][i].grads_other = feat(grads, COLUMN)
+            done(grads)
+
+        return step
+
+    def terms(kind):
+        def step(i):
+            upper, lower = gate(kinds[kind][i].grads, kinds[kind][i].grads_other)
+            give, keep = code_terms(core_at, upper, lower, decoder)
+            kinds[kind][i].grads, kinds[kind][i].grads_other = upper, lower
+            kinds[kind][i].terms = keep
+            kinds[kind][i].given = other_core(give)
+            done(keep, give)
+
+        return step
+
+    def out1(kind):
+        def step(i):
+            total = add(*gate(kinds[kind][i].terms, kinds[kind][i].given))
+            n = counts[i]
+            kinds[kind][i].heres[0], kinds[kind][i].heres[1] = total[:n], total[n : 2 * n]
+            kinds[kind][i].waits[0] = total[2 * n : 3 * n]
+            kinds[kind][i].theres[1] = feat(total[3 * n :], COLUMN)
+            done(total)
+
+        return step
+
+    def out1b(kind):
+        def step(i):
+            give = gate(kinds[kind][i].waits[0])
+            kinds[kind][i].theres[0] = feat(give, COLUMN)
+            done(give)
+
+        return step
+
+    def out2(kind, slot):
+        def step(i):
+            here, there = gate(kinds[kind][i].heres[slot], kinds[kind][i].theres[slot])
+            name = named(i, slot + 2 * kind)
+            out = jnp.stack(
+                [
+                    jnp.where(
+                        name[:, k : k + 1] == block,
+                        here,
+                        jnp.where(name[:, k : k + 1] == sibling, there, 0),
+                    )
+                    for k in range(per_token)
+                ]
+            )
+            kinds[kind][i].ys[slot] = out
+            if kind == FAR:
+                sent = feat(out, INWARD)
+                if slot:
+                    parts[i].out_sent = sent
+                else:
+                    parts[i].in_sent = sent
+            done(out)
+
+        return step
+
+    def out3(i):
+        y_out = add(*gate(kinds[FAR][i].ys[1], parts[i].out_sent))
+        parts[i].out_sent = feat(y_out, MIDDLE)
+        done(y_out)
+
+    def out3b(i):
+        y_in = add(*gate(kinds[FAR][i].ys[0], parts[i].in_sent))
+        parts[i].in_sent = feat(y_in, MIDDLE)
+        done(y_in)
+
+    def out4(i):
+        y_near = add(*gate(kinds[NEAR][i].ys[1], parts[i].out_sent))
+        kinds[NEAR][i].sent = feat(y_near, NEIGHBOUR)
+        done(y_near)
+
+    def out5(i):
+        own = add(*gate(kinds[NEAR][i].ys[0], kinds[NEAR][i].sent, parts[i].in_sent))
+        parts[i].sum = own
+        parts[i].sum_other = other_core(own)
+        done(own)
+
+    def out6(i):
+        own, other = gate(parts[i].sum, parts[i].sum_other)
+        first = core == 0
+        whole = jnp.concatenate(
+            [jnp.where(first, own, other), jnp.where(first, other, own)], axis=2
+        )
+        parts[i].code_grad = jnp.swapaxes(whole, 0, 1)
+        done(parts[i].code_grad)
+
+    def weights(i):
+        base = None
+        rows, grads = [], []
+        for part in range(2):
+            for kind in (NEAR, FAR):
+                rows.append((kinds[kind][part].rows_other if i else kinds[kind][part].rows))
+                grads += [kinds[kind][part].grads, kinds[kind][part].grads_other]
+        rows[0] = gate(rows[0])
+        if i:
+            base = parts[0].weight_grad
+        parts[i].weight_grad = weight_half(1 - core_at if i else core_at, rows, grads, base)
+        done(parts[i].weight_grad)
+
+    def recon1(i):
+        far = gate(kinds[FAR][i].rebuilt)
+        kinds[FAR][i].done = feat(far, MIRROR)
+        done(far)
+
+    def recon2(i):
+        own = stack(kinds[NEAR][0].rebuilt, kinds[NEAR][1].rebuilt)
+        far = gate(stack(kinds[FAR][0].done, kinds[FAR][1].done))
+        first = target == 0
+        parts[0].recon = jnp.stack([jnp.where(first, own, far), jnp.where(first, far, own)], axis=1)
+        done(parts[0].recon)
+
+    sums_near, sums_far = sums(NEAR), sums(FAR)
+    err1_near, err1_far = err1(NEAR), err1(FAR)
+    err2_near, err2_far = err2(NEAR), err2(FAR)
+    err3_near, err3_far = err3(NEAR), err3(FAR)
+    terms_near, terms_far = terms(NEAR), terms(FAR)
+    out1_near, out1_far = out1(NEAR), out1(FAR)
+    out1b_near, out1b_far = out1b(NEAR), out1b(FAR)
+    out2_mine, out2_next = out2(NEAR, 0), out2(NEAR, 1)
+    out2_in, out2_out = out2(FAR, 0), out2(FAR, 1)
+    order = (
+        (prep, 0), (prep, 1), (ids, 0), (in1, 0), (in1x, 0), (in2, 0), (in3, 0), (sums_near, 0),
+        (in4, 0), (in5, 0), (in1, 1), (in1x, 1), (sums_far, 0), (in2, 1), (aims, 0), (in3, 1),
+        (err1_far, 0), (sums_near, 1), (in4, 1), (err1_near, 0), (err1_near, 1), (err2_far, 0),
+        (aims, 1), (in5, 1), (err3_far, 0), (err2_near, 0), (err2_near, 1), (err3_near, 0),
+        (sums_far, 1), (terms_far, 0), (err3_near, 1), (err1_far, 1), (out1_far, 0),
+        (err2_far, 1), (recon1, 0), (err3_far, 1), (out1b_far, 0), (out2_out, 0), (terms_far, 1),
+        (out2_in, 0), (out3, 0), (recon1, 1), (out1_far, 1), (terms_near, 0), (out2_out, 1),
+        (out1_near, 0), (out3b, 0), (out1b_far, 1), (terms_near, 1), (out2_next, 0), (out4, 0),
+        (out2_in, 1), (out3, 1), (out1_near, 1), (out1b_near, 0), (out1b_near, 1), (weights, 0),
+        (out2_mine, 0), (out5, 0), (out3b, 1), (out2_next, 1), (out4, 1), (weights, 1),
+        (out6, 0), (recon2, 0), (out2_mine, 1), (out5, 1), (out6, 1),
+    )
+    for step, i in order:
+        step(i)
+    code_grad = stack(parts[0].code_grad, parts[1].code_grad)
+    return parts[0].recon, code_grad, parts[1].weight_grad
+
+
 def solution(mesh):
+    owners = mesh.shape["feat"]
+    plan = dense if owners // PAIRS == 4 and mesh.shape["pair"] == 2 else slotted
     return jax.shard_map(
-        local,
+        plan,
         mesh=mesh,
         in_specs=(
             P(("groups", "feat"), None, None),

time: 1260 us -> 522 us (0.41)
  blocking collectives: 556 us -> 0 us
  waiting for transfers between devices: 405 us -> 164 us
  Pallas kernels: 0 us -> 178 us
  matrix products: 130 us -> 0 us
  local copies, waits for them, and re-layouts: 128 us -> 30.7 us
  starting transfers between devices: 12.4 us -> 105 us
  other arithmetic: 17.9 us -> 32 us
    all_to_all x2 -> x0, blocking collectives: 466 us -> none  [the longest x1 369 us: local(): lax.all_to_all(outgoing, 'feat', split_axis=0, concat_axis=0, tiled=True)]
    all_to_all x2 -> x0, waiting for transfers between devices: 405 us -> none  [the longest x1 313 us: local(): lax.all_to_all(summed.astype(jnp.bfloat16), 'feat', split_axis=0, concat_...]
    pallas_call x0 -> x10, Pallas kernels: none -> 178 us  [call(): pl.pallas_call(kernel, grid_spec=pltpu.PrefetchScalarGridSpec(num_scalar_...]
    ppermute x0 -> x67, waiting for transfers between devices: none -> 164 us  [the longest x57 161 us: feat(): return lax.ppermute(value, 'feat', perm)]
    dot_general x3 -> x0, matrix products: 130 us -> none  [the longest x1 45.5 us: local(): lax.dot_general(arrived.reshape(-1, block_width), arrived_grad.reshape(-1...]
    ppermute x0 -> x67, starting transfers between devices: none -> 105 us  [the longest x57 77.6 us: feat(): return lax.ppermute(value, 'feat', perm)]
    psum x1 -> x0, blocking collectives: 89.8 us -> none  [local(): summed = lax.psum(summed, 'pair')]
    scatter x4 -> x0, local copies, waits for them, and re-layouts: 53.2 us -> none  [the longest x2 40.6 us: local(): outgoing = outgoing.at[slot_index].set(values)]
  transfers between devices with their start and end apart: 2 -> 67, of which waited for: 2 -> 26; matrix products, arithmetic and copies ran while one was open for 4% -> 9% of each run, Pallas kernels for 0% -> 32%
where the time goes in v1:
time: 522 us; the launch traced here: 512 us
  Pallas kernels  178 us (34%)
  waiting for transfers between devices  164 us (31%)
  starting transfers between devices  105 us (20%)
  other arithmetic  32 us (6%)
  local copies, waits for them, and re-layouts  30.7 us (6%)
    pallas_call x10, Pallas kernels, call(): pl.pallas_call(kernel, grid_spec=pltpu.PrefetchScalarGridSpec(num_scalar_...  178 us
    ppermute x57, waiting for transfers between devices, feat(): return lax.ppermute(value, 'feat', perm)  161 us
    ppermute x57, starting transfers between devices, feat(): return lax.ppermute(value, 'feat', perm)  77.6 us
    ppermute x10, starting transfers between devices, other_core(): return lax.ppermute(value, 'pair', [(0, 1), (1, 0)])  27.4 us
    convert_element_type x16, other arithmetic, add(): sum((term.astype(jnp.float32) for term in terms)).astype(jnp.bfloat16)  16.8 us
    unnamed x55, local copies, waits for them, and re-layouts  14.4 us
  transfers between devices with their start and end apart: 67, of which 26 were waited for; matrix products, arithmetic and copies ran while one was open for 9% of the time, Pallas kernels for 32%

profile of v1, /device:TPU:9, one launch (start us, length us, event | category | flops | bytes accessed | tf_op | source)
XLA Modules:
  0.0 512.3 jit_solution(10050512006343342339)
XLA Ops:
  0.6 2.1 constant_dynamic-slice_fusion
  3.4 3.2 collective-permute-start.1
  6.7 6.9 %copy.13 = bf16[128,2,8192]{2,0,1:T(8,128)(2,1)} copy(bf16[128,2,8192]{2,1,0:T(2,128)(2,1)} %param.4) | data formatting | bytes 8388608 | tf_op jit(solution)/shard_map/optimization_barrier | solution.py:312
  15.0 14.4 %collective-permute-done.1 = bf16[2,64,4096]{2,1,0:T(8,128)(2,1)} collective-permute-done((bf16[2,64,4096]{2,1,0:T(8,128)(2,1)S(1)}, bf16[2,64,4096]{2,1,0:T(8,128)(2,1)}, u32[]{:S(2)}, u32[]{:S(2)}) %collective-permute-start.1) | collective-permute-done | bytes 1048608 | tf_op jit(solution)/shard_map/ppermute | solution.py:280
  31.9 2.1 collective-permute-start.2
  34.0 2.1 collective-permute-start.7
  39.6 18.3 %collective-permute-done.7 = bf16[2,64,4096]{2,1,0:T(8,128)(2,1)S(1)} collective-permute-done((bf16[2,64,4096]{2,1,0:T(8,128)(2,1)S(1)}, bf16[2,64,4096]{2,1,0:T(8,128)(2,1)S(1)}, u32[]{:S(2)}, u32[]{:S(2)}) %collective-permute-start.7) | collective-permute-done | bytes 1048608 | tf_op jit(solution)/shard_map/ppermute | solution.py:280
  63.5 3.5 collective-permute-start.8
  67.1 1.5 collective-permute-start.12
  71.0 17.3 %shard_map.67 = (bf16[128,2048]{1,0:T(8,128)(2,1)S(1)}, bf16[128,2048]{1,0:T(8,128)(2,1)S(1)}) custom-call(s32[1]{0:T(128)} %bitcast.core_ref.side_ref, bf16[256,4096]{1,0:T(8,128)(2,1)} %constant_dynamic-update-slice_fusion.own_ref.refs_0_, bf16[256,4096]{1,0:T(8,128)(2,1)S(1)} %collective-permute-done.8.other_ref.refs_0_, bf16[8192,2048]{1,0:T(8,128)(2,1)} %decoder_ref.15), custom_call_target="tpu_custom_call" | custom-call | flops 8589934592 | bytes 33554432 | tf_op jit(solution)/shard_map/pallas_call | solution.py:82
  88.4 3.0 collective-permute-done.12
  93.0 3.1 collective-permute-start.11
  96.3 8.2 %collective-permute-done.14 = bf16[64,4096]{1,0:T(8,128)(2,1)S(1)} collective-permute-done((bf16[64,4096]{1,0:T(8,128)(2,1)S(1)}, bf16[64,4096]{1,0:T(8,128)(2,1)S(1)}, u32[]{:S(2)}, u32[]{:S(2)}) %collective-permute-start.14) | collective-permute-done | bytes 524320 | tf_op jit(solution)/shard_map/ppermute | solution.py:280
  104.7 1.7 collective-permute-start.17
  106.4 12.1 %collective-permute-done.11 = bf16[2,64,4096]{2,1,0:T(8,128)(2,1)S(1)} collective-permute-done((bf16[2,64,4096]{2,1,0:T(8,128)(2,1)S(1)}, bf16[2,64,4096]{2,1,0:T(8,128)(2,1)S(1)}, u32[]{:S(2)}, u32[]{:S(2)}) %collective-permute-start.11) | collective-permute-done | bytes 1048608 | tf_op jit(solution)/shard_map/ppermute | solution.py:280
  119.6 2.1 collective-permute-start.16
  121.7 1.6 collective-permute-start.15
  124.3 16.9 %shard_map.68 = (bf16[128,2048]{1,0:T(8,128)(2,1)S(1)}, bf16[128,2048]{1,0:T(8,128)(2,1)S(1)}) custom-call(s32[1]{0:T(128)} %bitcast.core_ref.side_ref, bf16[256,4096]{1,0:T(8,128)(2,1)S(1)} %constant_dynamic-update-slice_fusion.2.own_ref.refs_1_, bf16[256,4096]{1,0:T(8,128)(2,1)S(1)} %collective-permute-done.17.other_ref.refs_1_, ...), custom_call_target="tpu_custom_call" | custom-call | flops 8589934592 | bytes 33554432 | tf_op jit(solution)/shard_map/pallas_call | solution.py:82
  141.2 2.6 collective-permute-done.16
  146.2 3.5 collective-permute-start.20
  152.8 10.4 %collective-permute-done.21 = bf16[128,2048]{1,0:T(8,128)(2,1)S(1)} collective-permute-done((bf16[128,2048]{1,0:T(8,128)(2,1)S(1)}, bf16[128,2048]{1,0:T(8,128)(2,1)S(1)}, u32[]{:S(2)}, u32[]{:S(2)}) %collective-permute-start.21) | collective-permute-done | bytes 524320 | tf_op jit(solution)/shard_map/ppermute | solution.py:280
  163.3 2.7 collective-permute-start.18
  166.3 16.8 %shard_map.69 = (bf16[128,2048]{1,0:T(8,128)(2,1)S(1)}, bf16[128,2048]{1,0:T(8,128)(2,1)S(1)}) custom-call(s32[1]{0:T(128)} %bitcast.core_ref.side_ref, bf16[256,4096]{1,0:T(8,128)(2,1)S(1)} %constant_dynamic-update-slice_fusion.6.own_ref.refs_2_, bf16[256,4096]{1,0:T(8,128)(2,1)S(1)} %collective-permute-done.20.other_ref.refs_2_, ...), custom_call_target="tpu_custom_call" | custom-call | flops 8589934592 | bytes 33554432 | tf_op jit(solution)/shard_map/pallas_call | solution.py:82
  183.1 4.0 collective-permute-done.18
  189.2 7.3 %collective-permute-done.24 = bf16[128,2048]{1,0:T(8,128)(2,1)S(1)} collective-permute-done((bf16[128,2048]{1,0:T(8,128)(2,1)S(1)}, bf16[128,2048]{1,0:T(8,128)(2,1)S(1)}, u32[]{:S(2)}, u32[]{:S(2)}) %collective-permute-start.24) | collective-permute-done | bytes 524320 | tf_op jit(solution)/shard_map/ppermute | solution.py:280
  196.4 2.2 collective-permute-start.22
  201.6 6.1 %collective-permute-done.28 = bf16[64,4096]{1,0:T(8,128)(2,1)S(1)} collective-permute-done((bf16[64,4096]{1,0:T(8,128)(2,1)S(1)}, bf16[64,4096]{1,0:T(8,128)(2,1)S(1)}, u32[]{:S(2)}, u32[]{:S(2)}) %collective-permute-start.28) | collective-permute-done | bytes 524320 | tf_op jit(solution)/shard_map/ppermute | solution.py:280
  207.9 5.0 collective-permute-start.30
  213.1 2.3 collective-permute-start.31
  216.5 5.8 %collective-permute-done.31 = bf16[64,2048]{1,0:T(8,128)(2,1)S(1)} collective-permute-done((bf16[64,2048]{1,0:T(8,128)(2,1)S(1)}, bf16[64,2048]{1,0:T(8,128)(2,1)S(1)}, u32[]{:S(2)}, u32[]{:S(2)}) %collective-permute-start.31) | collective-permute-done | bytes 262176 | tf_op jit(solution)/shard_map/ppermute | solution.py:280
  222.4 16.9 %shard_map.70 = (bf16[128,2048]{1,0:T(8,128)(2,1)S(1)}, bf16[128,2048]{1,0:T(8,128)(2,1)S(1)}) custom-call(s32[1]{0:T(128)} %bitcast.core_ref.side_ref, bf16[256,4096]{1,0:T(8,128)(2,1)S(1)} %constant_dynamic-update-slice_fusion.8.own_ref.refs_3_, bf16[256,4096]{1,0:T(8,128)(2,1)S(1)} %collective-permute-done.30.other_ref.refs_3_, ...), custom_call_target="tpu_custom_call" | custom-call | flops 8589934592 | bytes 33554432 | tf_op jit(solution)/shard_map/pallas_call | solution.py:82
  239.3 16.5 %shard_map.71 = (bf16[256,4096]{1,0:T(8,128)(2,1)S(1)}, bf16[256,4096]{1,0:T(8,128)(2,1)S(1)}) custom-call(s32[1]{0:T(128)} %bitcast.core_ref.side_ref, bf16[128,2048]{1,0:T(8,128)(2,1)S(1)} %pad_maximum_fusion.14.upper_ref.refs_6_, bf16[128,2048]{1,0:T(8,128)(2,1)S(1)} %collective-permute-done.34.lower_ref.refs_7_, bf16[8192,2048]{1,0:T(8,128)(2,1)} %decoder_ref.15), custom_call_target="tpu_custom_call" | custom-call | flops 8589934592 | bytes 33554432 | tf_op jit(solution)/shard_map/pallas_call | solution.py:82
  255.9 2.0 collective-permute-start.36
  257.9 1.5 collective-permute-start.33
  262.3 3.6 collective-permute-done.33
  265.9 6.8 %collective-permute-done.32 = bf16[128,2048]{1,0:T(8,128)(2,1)S(1)} collective-permute-done((bf16[128,2048]{1,0:T(8,128)(2,1)S(1)}, bf16[128,2048]{1,0:T(8,128)(2,1)S(1)}, u32[]{:S(2)}, u32[]{:S(2)}) %collective-permute-start.32) | collective-permute-done | bytes 524320 | tf_op jit(solution)/shard_map/ppermute | solution.py:280
  273.7 5.0 collective-permute-done.35
  281.4 3.7 collective-permute-done.40
  286.7 6.1 %collective-permute-done.39 = bf16[64,4096]{1,0:T(8,128)(2,1)S(1)} collective-permute-done((bf16[64,4096]{1,0:T(8,128)(2,1)S(1)}, bf16[64,4096]{1,0:T(8,128)(2,1)S(1)}, u32[]{:S(2)}, u32[]{:S(2)}) %collective-permute-start.39) | collective-permute-done | bytes 524320 | tf_op jit(solution)/shard_map/ppermute | solution.py:280
  293.1 12.3 %collective-permute-start.41 = (bf16[2,64,4096]{2,1,0:T(8,128)(2,1)S(1)}, bf16[2,64,4096]{2,1,0:T(8,128)(2,1)S(1)}, u32[]{:S(2)}, u32[]{:S(2)}) collective-permute-start(bf16[2,64,4096]{2,1,0:T(8,128)(2,1)S(1)} %pad_maximum_fusion.5), channel_id=1, source_target_pairs={{0,4},{2,6},{12,8},{14,10},{1,5},{3,7},{13,9},{15,11},{16,20},{18,... | collective-permute-start | bytes 3145736 | tf_op jit(solution)/shard_map/ppermute | solution.py:280
  305.4 16.4 %shard_map.72 = (bf16[256,4096]{1,0:T(8,128)(2,1)S(1)}, bf16[256,4096]{1,0:T(8,128)(2,1)S(1)}) custom-call(s32[1]{0:T(128)} %bitcast.core_ref.side_ref, bf16[128,2048]{1,0:T(8,128)(2,1)S(1)} %pad_maximum_fusion.16.upper_ref.refs_10_, bf16[128,2048]{1,0:T(8,128)(2,1)S(1)} %collective-permute-done.43.lower_ref.refs_11_, bf16[8192,2048]{1,0:T(8,128)(2,1)} %decoder_ref.15), custom_call_target="tpu_custom_call" | custom-call | flops 8589934592 | bytes 33554432 | tf_op jit(solution)/shard_map/pallas_call | solution.py:82
  321.7 6.7 %collective-permute-start.46 = (bf16[256,4096]{1,0:T(8,128)(2,1)S(1)}, bf16[256,4096]{1,0:T(8,128)(2,1)S(1)}, u32[]{:S(2)}, u32[]{:S(2)}) collective-permute-start(bf16[256,4096]{1,0:T(8,128)(2,1)S(1)} %get-tuple-element.251), channel_id=1, source_target_pairs={{0,1},{1,0},{2,3},{3,2},{4,5},{5,4},{6,7},{7,6},{8,9},{9,8},{10,11... | collective-permute-start | bytes 6291464 | tf_op jit(solution)/shard_map/ppermute | solution.py:291
  334.6 17.3 %shard_map.73 = (bf16[256,4096]{1,0:T(8,128)(2,1)}, bf16[256,4096]{1,0:T(8,128)(2,1)S(1)}) custom-call(s32[1]{0:T(128)} %bitcast.core_ref.side_ref, bf16[128,2048]{1,0:T(8,128)(2,1)S(1)} %constant_dynamic-update-slice_fusion.12.upper_ref.refs_4_, bf16[128,2048]{1,0:T(8,128)(2,1)S(1)} %collective-permute-done.45.lower_ref.refs_5_, bf16[8192,2048]{1,0:T(8,128)(2,1)} %decoder_ref.15), custom_call_target="tpu_custom_call" | custom-call | flops 8589934592 | bytes 33554432 | tf_op jit(solution)/shard_map/pallas_call | solution.py:82
  356.6 2.1 collective-permute-start.55
  359.8 1.6 select_bitcast_fusion.13
  363.0 2.4 add_convert_fusion.1
  365.4 17.3 %collective-permute-done.50 = bf16[2,64,4096]{2,1,0:T(8,128)(2,1)S(1)} collective-permute-done((bf16[2,64,4096]{2,1,0:T(8,128)(2,1)}, bf16[2,64,4096]{2,1,0:T(8,128)(2,1)S(1)}, u32[]{:S(2)}, u32[]{:S(2)}) %collective-permute-start.50) | collective-permute-done | bytes 1048608 | tf_op jit(solution)/shard_map/ppermute | solution.py:280
  383.8 2.9 collective-permute-start.58
  389.3 16.3 %shard_map.74 = (bf16[256,4096]{1,0:T(8,128)(2,1)S(1)}, bf16[256,4096]{1,0:T(8,128)(2,1)S(1)}) custom-call(s32[1]{0:T(128)} %bitcast.core_ref.side_ref, bf16[128,2048]{1,0:T(8,128)(2,1)S(1)} %constant_dynamic-update-slice_fusion.14.upper_ref.refs_8_, bf16[128,2048]{1,0:T(8,128)(2,1)S(1)} %collective-permute-done.49.lower_ref.refs_9_, ...), custom_call_target="tpu_custom_call" | custom-call | flops 8589934592 | bytes 33554432 | tf_op jit(solution)/shard_map/pallas_call | solution.py:82
  405.7 4.6 collective-permute-done.54
  410.3 2.2 collective-permute-start.51
  412.8 2.5 add_convert_fusion.9
  418.2 2.3 collective-permute-start.62
  422.6 22.1 %shard_map.75.refs_12_ = bf16[8192,2048]{1,0:T(8,128)(2,1)} custom-call(s32[1]{0:T(128)} %bitcast.core_ref.side_ref, bf16[256,4096]{1,0:T(8,128)(2,1)} %constant_dynamic-update-slice_fusion.own_ref.refs_0_, bf16[256,4096]{1,0:T(8,128)(2,1)} %copy-done.5, bf16[256,4096]{1,0:T(8,128)(2,1)} %copy-done.4, bf16[256,4096]{1,0:T(8,128)(2,1)} %copy-done.6, ...), custom_call_target="tpu_custom_call" | custom-call | flops 17179869184 | bytes 25165824 | tf_op jit(solution)/shard_map/pallas_call | solution.py:82
  446.6 2.0 add_convert_fusion.7
  448.6 14.3 %collective-permute-done.61 = bf16[2,64,4096]{2,1,0:T(8,128)(2,1)} collective-permute-done((bf16[2,64,4096]{2,1,0:T(8,128)(2,1)S(1)}, bf16[2,64,4096]{2,1,0:T(8,128)(2,1)}, u32[]{:S(2)}, u32[]{:S(2)}) %collective-permute-start.61) | collective-permute-done | bytes 1048608 | tf_op jit(solution)/shard_map/ppermute | solution.py:280
  464.4 4.8 collective-permute-done.60
  469.4 1.5 add_convert_fusion.5
  470.9 2.5 collective-permute-start.64
  473.4 2.5 collective-permute-start.65
  475.9 2.0 collective-permute-start.59
  477.9 22.1 %shard_map.76 = bf16[8192,2048]{1,0:T(8,128)(2,1)} custom-call(s32[1]{0:T(128)S(6)} %sub.33.side_ref, bf16[256,4096]{1,0:T(8,128)(2,1)} %copy-done, bf16[256,4096]{1,0:T(8,128)(2,1)} %copy-done.1, bf16[256,4096]{1,0:T(8,128)(2,1)} %copy-done.2, bf16[256,4096]{1,0:T(8,128)(2,1)} %copy-done.3, ...), custom_call_target="tpu_custom_call", output_to_operand_aliasing={{}: (13, {})} | custom-call | flops 17179869184 | bytes 25165824 | tf_op jit(solution)/shard_map/pallas_call | solution.py:82
  502.4 2.0 copy.16
  505.6 6.4 %copy.17 = bf16[128,2,8192]{2,1,0:T(2,128)(2,1)} copy(bf16[128,2,8192]{2,0,1:T(8,128)(2,1)S(1)} %pad_maximum_fusion) | data formatting | bytes 8388608
  (242 shorter events, 69.9 us)
Async XLA Ops:
  3.4 26.0 %collective-permute-start.1 = (bf16[2,64,4096]{2,1,0:T(8,128)(2,1)S(1)}, bf16[2,64,4096]{2,1,0:T(8,128)(2,1)}, u32[]{:S(2)}, u32[]{:S(2)}) collective-permute-start(bf16[2,64,4096]{2,1,0:T(8,128)(2,1)S(1)} %bitcast.302), channel_id=1, source_target_pairs={{4,8},{6,10},{8,4},{10,6},{5,9},{7,11},{9,5},{11,7},{20,24},{22,26... | collective-permute-start | bytes 3145736 | tf_op jit(solution)/shard_map/ppermute | solution.py:280
  6.6 23.9 %collective-permute-start = (bf16[2,64,4096]{2,1,0:T(8,128)(2,1)S(1)}, bf16[2,64,4096]{2,1,0:T(8,128)(2,1)S(1)}, u32[]{:S(2)}, u32[]{:S(2)}) collective-permute-start(bf16[2,64,4096]{2,1,0:T(8,128)(2,1)S(1)} %bitcast.303), channel_id=1, source_target_pairs={{0,4},{2,6},{4,0},{6,2},{8,12},{10,14},{12,8},{14,10},{1,5},{3,7},... | collective-permute-start | bytes 3145736 | tf_op jit(solution)/shard_map/ppermute | solution.py:280
  30.5 8.9 %collective-permute-start.5 = (s32[128,2]{0,1:T(2,128)S(1)}, s32[128,2]{0,1:T(2,128)S(1)}, u32[]{:S(2)}, u32[]{:S(2)}) collective-permute-start(s32[128,2]{0,1:T(2,128)S(1)} %copy-done.20), channel_id=1, source_target_pairs={{0,8},{2,10},{8,0},{10,2},{4,12},{6,14},{12,4},{14,6},{1,9},{3,11}... | collective-permute-start | bytes 3080 | tf_op jit(solution)/shard_map/ppermute | solution.py:280
  31.4 8.1 %collective-permute-start.4 = (s32[128,2]{0,1:T(2,128)S(1)}, s32[128,2]{0,1:T(2,128)S(1)}, u32[]{:S(2)}, u32[]{:S(2)}) collective-permute-start(s32[128,2]{0,1:T(2,128)S(1)} %copy-done.20), channel_id=1, source_target_pairs={{0,12},{2,14},{12,0},{14,2},{4,8},{6,10},{8,4},{10,6},{1,13},{3,15... | collective-permute-start | bytes 3080 | tf_op jit(solution)/shard_map/ppermute | solution.py:280
  34.0 23.9 %collective-permute-start.7 = (bf16[2,64,4096]{2,1,0:T(8,128)(2,1)S(1)}, bf16[2,64,4096]{2,1,0:T(8,128)(2,1)S(1)}, u32[]{:S(2)}, u32[]{:S(2)}) collective-permute-start(bf16[2,64,4096]{2,1,0:T(8,128)(2,1)S(1)} %collective-permute-done), channel_id=1, source_target_pairs={{4,8},{6,10},{8,4},{10,6},{5,9},{7,11},{9,5},{11,7},{20,24},{22,26... | collective-permute-start | bytes 3145736 | tf_op jit(solution)/shard_map/ppermute | solution.py:280
  36.1 22.8 %collective-permute-start.6 = (bf16[2,64,4096]{2,1,0:T(8,128)(2,1)}, bf16[2,64,4096]{2,1,0:T(8,128)(2,1)S(1)}, u32[]{:S(2)}, u32[]{:S(2)}) collective-permute-start(bf16[2,64,4096]{2,1,0:T(8,128)(2,1)} %collective-permute-done.1), channel_id=1, source_target_pairs={{4,0},{6,2},{8,12},{10,14},{5,1},{7,3},{9,13},{11,15},{20,16},{22,... | collective-permute-start | bytes 3145736 | tf_op jit(solution)/shard_map/ppermute | solution.py:280
  38.1 23.3 %collective-permute-start.3 = (bf16[128,4096]{1,0:T(8,128)(2,1)S(1)}, bf16[128,4096]{1,0:T(8,128)(2,1)S(1)}, u32[]{:S(2)}, u32[]{:S(2)}) collective-permute-start(bf16[128,4096]{1,0:T(8,128)(2,1)S(1)} %pad_maximum_fusion.2), channel_id=1, source_target_pairs={{0,2},{2,0},{4,6},{6,4},{8,10},{10,8},{12,14},{14,12},{1,3},{3,1},... | collective-permute-start | bytes 3145736 | tf_op jit(solution)/shard_map/ppermute | solution.py:280
  63.5 7.5 %collective-permute-start.8 = (bf16[256,4096]{1,0:T(8,128)(2,1)}, bf16[256,4096]{1,0:T(8,128)(2,1)S(1)}, u32[]{:S(2)}, u32[]{:S(2)}) collective-permute-start(bf16[256,4096]{1,0:T(8,128)(2,1)} %constant_dynamic-update-slice_fusion.own_ref.refs_0_), channel_id=1, source_target_pairs={{0,1},{1,0},{2,3},{3,2},{4,5},{5,4},{6,7},{7,6},{8,9},{9,8},{10,11... | collective-permute-start | bytes 6291464 | tf_op jit(solution)/shard_map/ppermute | solution.py:291
  67.1 24.4 %collective-permute-start.12 = (bf16[2,64,4096]{2,1,0:T(8,128)(2,1)}, bf16[2,64,4096]{2,1,0:T(8,128)(2,1)S(1)}, u32[]{:S(2)}, u32[]{:S(2)}) collective-permute-start(bf16[2,64,4096]{2,1,0:T(8,128)(2,1)} %copy-done.16), channel_id=1, source_target_pairs={{4,0},{6,2},{8,12},{10,14},{5,1},{7,3},{9,13},{11,15},{20,16},{22,... | collective-permute-start | bytes 3145736 | tf_op jit(solution)/shard_map/ppermute | solution.py:280
  68.6 27.7 %collective-permute-start.13 = (bf16[64,4096]{1,0:T(8,128)(2,1)}, bf16[64,4096]{1,0:T(8,128)(2,1)S(1)}, u32[]{:S(2)}, u32[]{:S(2)}) collective-permute-start(bf16[64,4096]{1,0:T(8,128)(2,1)} %get-tuple-element.372), channel_id=1, source_target_pairs={{0,2},{2,0},{4,6},{6,4},{8,10},{10,8},{12,14},{14,12},{1,3},{3,1},... | collective-permute-start | bytes 1572872 | tf_op jit(solution)/shard_map/ppermute | solution.py:280
  91.7 12.7 %collective-permute-start.14 = (bf16[64,4096]{1,0:T(8,128)(2,1)S(1)}, bf16[64,4096]{1,0:T(8,128)(2,1)S(1)}, u32[]{:S(2)}, u32[]{:S(2)}) collective-permute-start(bf16[64,4096]{1,0:T(8,128)(2,1)S(1)} %get-tuple-element.369), channel_id=1, source_target_pairs={{0,2},{2,0},{4,6},{6,4},{8,10},{10,8},{12,14},{14,12},{1,3},{3,1},... | collective-permute-start | bytes 1572872 | tf_op jit(solution)/shard_map/ppermute | solution.py:280
  93.0 25.5 %collective-permute-start.11 = (bf16[2,64,4096]{2,1,0:T(8,128)(2,1)S(1)}, bf16[2,64,4096]{2,1,0:T(8,128)(2,1)S(1)}, u32[]{:S(2)}, u32[]{:S(2)}) collective-permute-start(bf16[2,64,4096]{2,1,0:T(8,128)(2,1)S(1)} %dynamic-slice_bitcast_fusion), channel_id=1, source_target_pairs={{4,8},{6,10},{8,4},{10,6},{5,9},{7,11},{9,5},{11,7},{20,24},{22,26... | collective-permute-start | bytes 3145736 | tf_op jit(solution)/shard_map/ppermute | solution.py:280
  96.2 23.4 %collective-permute-start.10 = (bf16[2,64,4096]{2,1,0:T(8,128)(2,1)S(1)}, bf16[2,64,4096]{2,1,0:T(8,128)(2,1)S(1)}, u32[]{:S(2)}, u32[]{:S(2)}) collective-permute-start(bf16[2,64,4096]{2,1,0:T(8,128)(2,1)S(1)} %dynamic-slice_bitcast_fusion), channel_id=1, source_target_pairs={{0,4},{2,6},{4,0},{6,2},{8,12},{10,14},{12,8},{14,10},{1,5},{3,7},... | collective-permute-start | bytes 3145736 | tf_op jit(solution)/shard_map/ppermute | solution.py:280
  104.7 19.6 %collective-permute-start.17 = (bf16[256,4096]{1,0:T(8,128)(2,1)S(1)}, bf16[256,4096]{1,0:T(8,128)(2,1)S(1)}, u32[]{:S(2)}, u32[]{:S(2)}) collective-permute-start(bf16[256,4096]{1,0:T(8,128)(2,1)S(1)} %constant_dynamic-update-slice_fusion.2.own_ref.refs_1_), channel_id=1, source_target_pairs={{0,1},{1,0},{2,3},{3,2},{4,5},{5,4},{6,7},{7,6},{8,9},{9,8},{10,11... | collective-permute-start | bytes 6291464 | tf_op jit(solution)/shard_map/ppermute | solution.py:291
  119.6 24.3 %collective-permute-start.16 = (bf16[2,64,4096]{2,1,0:T(8,128)(2,1)S(1)}, bf16[2,64,4096]{2,1,0:T(8,128)(2,1)S(1)}, u32[]{:S(2)}, u32[]{:S(2)}) collective-permute-start(bf16[2,64,4096]{2,1,0:T(8,128)(2,1)S(1)} %collective-permute-done.10), channel_id=1, source_target_pairs={{4,8},{6,10},{8,4},{10,6},{5,9},{7,11},{9,5},{11,7},{20,24},{22,26... | collective-permute-start | bytes 3145736 | tf_op jit(solution)/shard_map/ppermute | solution.py:280
  121.7 22.1 %collective-permute-start.15 = (bf16[2,64,4096]{2,1,0:T(8,128)(2,1)S(1)}, bf16[2,64,4096]{2,1,0:T(8,128)(2,1)S(1)}, u32[]{:S(2)}, u32[]{:S(2)}) collective-permute-start(bf16[2,64,4096]{2,1,0:T(8,128)(2,1)S(1)} %collective-permute-done.11), channel_id=1, source_target_pairs={{4,0},{6,2},{8,12},{10,14},{5,1},{7,3},{9,13},{11,15},{20,16},{22,... | collective-permute-start | bytes 3145736 | tf_op jit(solution)/shard_map/ppermute | solution.py:280
  123.8 22.2 %collective-permute-start.19 = (bf16[128,4096]{1,0:T(8,128)(2,1)S(1)}, bf16[128,4096]{1,0:T(8,128)(2,1)S(1)}, u32[]{:S(2)}, u32[]{:S(2)}) collective-permute-start(bf16[128,4096]{1,0:T(8,128)(2,1)S(1)} %pad_maximum_fusion.3), channel_id=1, source_target_pairs={{0,2},{2,0},{4,6},{6,4},{8,10},{10,8},{12,14},{14,12},{1,3},{3,1},... | collective-permute-start | bytes 3145736 | tf_op jit(solution)/shard_map/ppermute | solution.py:280
  146.2 20.0 %collective-permute-start.20 = (bf16[256,4096]{1,0:T(8,128)(2,1)S(1)}, bf16[256,4096]{1,0:T(8,128)(2,1)S(1)}, u32[]{:S(2)}, u32[]{:S(2)}) collective-permute-start(bf16[256,4096]{1,0:T(8,128)(2,1)S(1)} %constant_dynamic-update-slice_fusion.6.own_ref.refs_2_), channel_id=1, source_target_pairs={{0,1},{1,0},{2,3},{3,2},{4,5},{5,4},{6,7},{7,6},{8,9},{9,8},{10,11... | collective-permute-start | bytes 6291464 | tf_op jit(solution)/shard_map/ppermute | solution.py:291
  149.8 13.5 %collective-permute-start.21 = (bf16[128,2048]{1,0:T(8,128)(2,1)S(1)}, bf16[128,2048]{1,0:T(8,128)(2,1)S(1)}, u32[]{:S(2)}, u32[]{:S(2)}) collective-permute-start(bf16[128,2048]{1,0:T(8,128)(2,1)S(1)} %get-tuple-element.188), channel_id=1, source_target_pairs={{0,2},{2,0},{4,6},{6,4},{8,10},{10,8},{12,14},{14,12},{1,3},{3,1},... | collective-permute-start | bytes 1572872 | tf_op jit(solution)/shard_map/ppermute | solution.py:280
  150.0 37.7 %collective-permute-start.9 = (bf16[128,2048]{1,0:T(8,128)(2,1)S(1)}, bf16[128,2048]{1,0:T(8,128)(2,1)S(1)}, u32[]{:S(2)}, u32[]{:S(2)}) collective-permute-start(bf16[128,2048]{1,0:T(8,128)(2,1)S(1)} %get-tuple-element.171), channel_id=1, source_target_pairs={{0,2},{2,0},{4,6},{6,4},{8,10},{10,8},{12,14},{14,12},{1,3},{3,1},... | collective-permute-start | bytes 1572872 | tf_op jit(solution)/shard_map/ppermute | solution.py:280
  151.3 50.3 %collective-permute-start.27 = (bf16[64,4096]{1,0:T(8,128)(2,1)S(1)}, bf16[64,4096]{1,0:T(8,128)(2,1)S(1)}, u32[]{:S(2)}, u32[]{:S(2)}) collective-permute-start(bf16[64,4096]{1,0:T(8,128)(2,1)S(1)} %get-tuple-element.364), channel_id=1, source_target_pairs={{0,2},{2,0},{4,6},{6,4},{8,10},{10,8},{12,14},{14,12},{1,3},{3,1},... | collective-permute-start | bytes 1572872 | tf_op jit(solution)/shard_map/ppermute | solution.py:280
  151.6 47.2 %collective-permute-start.25 = (bf16[64,2048]{1,0:T(8,128)(2,1)S(1)}, bf16[64,2048]{1,0:T(8,128)(2,1)S(1)}, u32[]{:S(2)}, u32[]{:S(2)}) collective-permute-start(bf16[64,2048]{1,0:T(8,128)(2,1)S(1)} %get-tuple-element.392), channel_id=1, source_target_pairs={{0,12},{2,14},{12,0},{14,2},{4,8},{6,10},{8,4},{10,6},{1,13},{3,15... | collective-permute-start | bytes 786440 | tf_op jit(solution)/shard_map/ppermute | solution.py:280
  163.3 23.8 %collective-permute-start.18 = (bf16[2,64,4096]{2,1,0:T(8,128)(2,1)S(1)}, bf16[2,64,4096]{2,1,0:T(8,128)(2,1)S(1)}, u32[]{:S(2)}, u32[]{:S(2)}) collective-permute-start(bf16[2,64,4096]{2,1,0:T(8,128)(2,1)S(1)} %collective-permute-done.16), channel_id=1, source_target_pairs={{4,0},{6,2},{8,12},{10,14},{5,1},{7,3},{9,13},{11,15},{20,16},{22,... | collective-permute-start | bytes 3145736 | tf_op jit(solution)/shard_map/ppermute | solution.py:280
  166.2 32.6 %collective-permute-start.23 = (bf16[64,2048]{1,0:T(8,128)(2,1)S(1)}, bf16[64,2048]{1,0:T(8,128)(2,1)S(1)}, u32[]{:S(2)}, u32[]{:S(2)}) collective-permute-start(bf16[64,2048]{1,0:T(8,128)(2,1)S(1)} %get-tuple-element.389), channel_id=1, source_target_pairs={{0,4},{2,6},{4,0},{6,2},{8,12},{10,14},{12,8},{14,10},{1,5},{3,7},... | collective-permute-start | bytes 786440 | tf_op jit(solution)/shard_map/ppermute | solution.py:280
  187.1 9.4 %collective-permute-start.24 = (bf16[128,2048]{1,0:T(8,128)(2,1)S(1)}, bf16[128,2048]{1,0:T(8,128)(2,1)S(1)}, u32[]{:S(2)}, u32[]{:S(2)}) collective-permute-start(bf16[128,2048]{1,0:T(8,128)(2,1)S(1)} %get-tuple-element.200), channel_id=1, source_target_pairs={{0,2},{2,0},{4,6},{6,4},{8,10},{10,8},{12,14},{14,12},{1,3},{3,1},... | collective-permute-start | bytes 1572872 | tf_op jit(solution)/shard_map/ppermute | solution.py:280
  187.7 20.0 %collective-permute-start.28 = (bf16[64,4096]{1,0:T(8,128)(2,1)S(1)}, bf16[64,4096]{1,0:T(8,128)(2,1)S(1)}, u32[]{:S(2)}, u32[]{:S(2)}) collective-permute-start(bf16[64,4096]{1,0:T(8,128)(2,1)S(1)} %get-tuple-element.362), channel_id=1, source_target_pairs={{0,2},{2,0},{4,6},{6,4},{8,10},{10,8},{12,14},{14,12},{1,3},{3,1},... | collective-permute-start | bytes 1572872 | tf_op jit(solution)/shard_map/ppermute | solution.py:280
  196.4 16.5 %collective-permute-start.22 = (bf16[64,2048]{1,0:T(8,128)(2,1)S(1)}, bf16[64,2048]{1,0:T(8,128)(2,1)S(1)}, u32[]{:S(2)}, u32[]{:S(2)}) collective-permute-start(bf16[64,2048]{1,0:T(8,128)(2,1)S(1)} %get-tuple-element.387), channel_id=1, source_target_pairs={{0,4},{2,6},{4,0},{6,2},{8,12},{10,14},{12,8},{14,10},{1,5},{3,7},... | collective-permute-start | bytes 786440 | tf_op jit(solution)/shard_map/ppermute | solution.py:280
  199.7 13.2 %collective-permute-start.26 = (bf16[64,2048]{1,0:T(8,128)(2,1)S(1)}, bf16[64,2048]{1,0:T(8,128)(2,1)S(1)}, u32[]{:S(2)}, u32[]{:S(2)}) collective-permute-start(bf16[64,2048]{1,0:T(8,128)(2,1)S(1)} %get-tuple-element.215), channel_id=1, source_target_pairs={{0,4},{2,6},{4,0},{6,2},{8,12},{10,14},{12,8},{14,10},{1,5},{3,7},... | collective-permute-start | bytes 786440 | tf_op jit(solution)/shard_map/ppermute | solution.py:280
  199.7 16.0 %collective-permute-start.29 = (bf16[64,2048]{1,0:T(8,128)(2,1)S(1)}, bf16[64,2048]{1,0:T(8,128)(2,1)S(1)}, u32[]{:S(2)}, u32[]{:S(2)}) collective-permute-start(bf16[64,2048]{1,0:T(8,128)(2,1)S(1)} %get-tuple-element.385), channel_id=1, source_target_pairs={{0,4},{2,6},{4,0},{6,2},{8,12},{10,14},{12,8},{14,10},{1,5},{3,7},... | collective-permute-start | bytes 786440 | tf_op jit(solution)/shard_map/ppermute | solution.py:280
  207.9 14.5 %collective-permute-start.30 = (bf16[256,4096]{1,0:T(8,128)(2,1)S(1)}, bf16[256,4096]{1,0:T(8,128)(2,1)S(1)}, u32[]{:S(2)}, u32[]{:S(2)}) collective-permute-start(bf16[256,4096]{1,0:T(8,128)(2,1)S(1)} %constant_dynamic-update-slice_fusion.8.own_ref.refs_3_), channel_id=1, source_target_pairs={{0,1},{1,0},{2,3},{3,2},{4,5},{5,4},{6,7},{7,6},{8,9},{9,8},{10,11... | collective-permute-start | bytes 6291464 | tf_op jit(solution)/shard_map/ppermute | solution.py:291
  213.1 9.2 %collective-permute-start.31 = (bf16[64,2048]{1,0:T(8,128)(2,1)S(1)}, bf16[64,2048]{1,0:T(8,128)(2,1)S(1)}, u32[]{:S(2)}, u32[]{:S(2)}) collective-permute-start(bf16[64,2048]{1,0:T(8,128)(2,1)S(1)} %get-tuple-element.223), channel_id=1, source_target_pairs={{0,4},{2,6},{4,0},{6,2},{8,12},{10,14},{12,8},{14,10},{1,5},{3,7},... | collective-permute-start | bytes 786440 | tf_op jit(solution)/shard_map/ppermute | solution.py:280
  215.4 23.9 %collective-permute-start.34 = (bf16[128,2048]{1,0:T(8,128)(2,1)S(1)}, bf16[128,2048]{1,0:T(8,128)(2,1)S(1)}, u32[]{:S(2)}, u32[]{:S(2)}) collective-permute-start(bf16[128,2048]{1,0:T(8,128)(2,1)S(1)} %pad_maximum_fusion.14.upper_ref.refs_6_), channel_id=1, source_target_pairs={{0,2},{2,0},{4,6},{6,4},{8,10},{10,8},{12,14},{14,12},{1,3},{3,1},... | collective-permute-start | bytes 1572872 | tf_op jit(solution)/shard_map/ppermute | solution.py:280
  255.9 17.1 %collective-permute-start.36 = (bf16[256,4096]{1,0:T(8,128)(2,1)S(1)}, bf16[256,4096]{1,0:T(8,128)(2,1)S(1)}, u32[]{:S(2)}, u32[]{:S(2)}) collective-permute-start(bf16[256,4096]{1,0:T(8,128)(2,1)S(1)} %get-tuple-element.232), channel_id=1, source_target_pairs={{0,1},{1,0},{2,3},{3,2},{4,5},{5,4},{6,7},{7,6},{8,9},{9,8},{10,11... | collective-permute-start | bytes 6291464 | tf_op jit(solution)/shard_map/ppermute | solution.py:291
  257.9 7.9 %collective-permute-start.33 = (bf16[64,2048]{1,0:T(8,128)(2,1)S(1)}, bf16[64,2048]{1,0:T(8,128)(2,1)S(1)}, u32[]{:S(2)}, u32[]{:S(2)}) collective-permute-start(bf16[64,2048]{1,0:T(8,128)(2,1)S(1)} %get-tuple-element.233), channel_id=1, source_target_pairs={{0,4},{2,6},{4,0},{6,2},{8,12},{10,14},{12,8},{14,10},{1,5},{3,7},... | collective-permute-start | bytes 786440 | tf_op jit(solution)/shard_map/ppermute | solution.py:280
  259.5 13.2 %collective-permute-start.32 = (bf16[128,2048]{1,0:T(8,128)(2,1)S(1)}, bf16[128,2048]{1,0:T(8,128)(2,1)S(1)}, u32[]{:S(2)}, u32[]{:S(2)}) collective-permute-start(bf16[128,2048]{1,0:T(8,128)(2,1)S(1)} %get-tuple-element.228), channel_id=1, source_target_pairs={{0,2},{2,0},{4,6},{6,4},{8,10},{10,8},{12,14},{14,12},{1,3},{3,1},... | collective-permute-start | bytes 1572872 | tf_op jit(solution)/shard_map/ppermute | solution.py:280
  259.8 13.9 %collective-permute-start.37 = (bf16[64,2048]{1,0:T(8,128)(2,1)S(1)}, bf16[64,2048]{1,0:T(8,128)(2,1)S(1)}, u32[]{:S(2)}, u32[]{:S(2)}) collective-permute-start(bf16[64,2048]{1,0:T(8,128)(2,1)S(1)} %get-tuple-element.384), channel_id=1, source_target_pairs={{0,12},{2,14},{12,0},{14,2},{4,8},{6,10},{8,4},{10,6},{1,13},{3,15... | collective-permute-start | bytes 786440 | tf_op jit(solution)/shard_map/ppermute | solution.py:280
  261.1 73.3 %collective-permute-start.45 = (bf16[128,2048]{1,0:T(8,128)(2,1)S(1)}, bf16[128,2048]{1,0:T(8,128)(2,1)S(1)}, u32[]{:S(2)}, u32[]{:S(2)}) collective-permute-start(bf16[128,2048]{1,0:T(8,128)(2,1)S(1)} %constant_dynamic-update-slice_fusion.12.upper_ref.refs_4_), channel_id=1, source_target_pairs={{0,2},{2,0},{4,6},{6,4},{8,10},{10,8},{12,14},{14,12},{1,3},{3,1},... | collective-permute-start | bytes 1572872 | tf_op jit(solution)/shard_map/ppermute | solution.py:280
  272.8 5.9 %collective-permute-start.35 = (bf16[64,2048]{1,0:T(8,128)(2,1)S(1)}, bf16[64,2048]{1,0:T(8,128)(2,1)S(1)}, u32[]{:S(2)}, u32[]{:S(2)}) collective-permute-start(bf16[64,2048]{1,0:T(8,128)(2,1)S(1)} %get-tuple-element.379), channel_id=1, source_target_pairs={{0,4},{2,6},{4,0},{6,2},{8,12},{10,14},{12,8},{14,10},{1,5},{3,7},... | collective-permute-start | bytes 786440 | tf_op jit(solution)/shard_map/ppermute | solution.py:280
  279.9 75.4 %collective-permute-start.38 = (bf16[64,2048]{1,0:T(8,128)(2,1)}, bf16[64,2048]{1,0:T(8,128)(2,1)}, u32[]{:S(2)}, u32[]{:S(2)}) collective-permute-start(bf16[64,2048]{1,0:T(8,128)(2,1)} %get-tuple-element.242), channel_id=1, source_target_pairs={{0,12},{2,14},{12,0},{14,2},{4,8},{6,10},{8,4},{10,6},{1,13},{3,15... | collective-permute-start | bytes 786440 | tf_op jit(solution)/shard_map/ppermute | solution.py:280
  281.2 11.6 %collective-permute-start.39 = (bf16[64,4096]{1,0:T(8,128)(2,1)S(1)}, bf16[64,4096]{1,0:T(8,128)(2,1)S(1)}, u32[]{:S(2)}, u32[]{:S(2)}) collective-permute-start(bf16[64,4096]{1,0:T(8,128)(2,1)S(1)} %get-tuple-element.341), channel_id=1, source_target_pairs={{0,2},{2,0},{4,6},{6,4},{8,10},{10,8},{12,14},{14,12},{1,3},{3,1},... | collective-permute-start | bytes 1572872 | tf_op jit(solution)/shard_map/ppermute | solution.py:280
  285.2 20.2 %collective-permute-start.43 = (bf16[128,2048]{1,0:T(8,128)(2,1)S(1)}, bf16[128,2048]{1,0:T(8,128)(2,1)S(1)}, u32[]{:S(2)}, u32[]{:S(2)}) collective-permute-start(bf16[128,2048]{1,0:T(8,128)(2,1)S(1)} %pad_maximum_fusion.16.upper_ref.refs_10_), channel_id=1, source_target_pairs={{0,2},{2,0},{4,6},{6,4},{8,10},{10,8},{12,14},{14,12},{1,3},{3,1},... | collective-permute-start | bytes 1572872 | tf_op jit(solution)/shard_map/ppermute | solution.py:280
  285.5 42.9 %collective-permute-start.42 = (bf16[64,4096]{1,0:T(8,128)(2,1)S(1)}, bf16[64,4096]{1,0:T(8,128)(2,1)S(1)}, u32[]{:S(2)}, u32[]{:S(2)}) collective-permute-start(bf16[64,4096]{1,0:T(8,128)(2,1)S(1)} %get-tuple-element.245), channel_id=1, source_target_pairs={{0,2},{2,0},{4,6},{6,4},{8,10},{10,8},{12,14},{14,12},{1,3},{3,1},... | collective-permute-start | bytes 1572872 | tf_op jit(solution)/shard_map/ppermute | solution.py:280
  293.1 36.6 %collective-permute-start.41 = (bf16[2,64,4096]{2,1,0:T(8,128)(2,1)S(1)}, bf16[2,64,4096]{2,1,0:T(8,128)(2,1)S(1)}, u32[]{:S(2)}, u32[]{:S(2)}) collective-permute-start(bf16[2,64,4096]{2,1,0:T(8,128)(2,1)S(1)} %pad_maximum_fusion.5), channel_id=1, source_target_pairs={{0,4},{2,6},{12,8},{14,10},{1,5},{3,7},{13,9},{15,11},{16,20},{18,... | collective-permute-start | bytes 3145736 | tf_op jit(solution)/shard_map/ppermute | solution.py:280
  321.7 10.5 %collective-permute-start.46 = (bf16[256,4096]{1,0:T(8,128)(2,1)S(1)}, bf16[256,4096]{1,0:T(8,128)(2,1)S(1)}, u32[]{:S(2)}, u32[]{:S(2)}) collective-permute-start(bf16[256,4096]{1,0:T(8,128)(2,1)S(1)} %get-tuple-element.251), channel_id=1, source_target_pairs={{0,1},{1,0},{2,3},{3,2},{4,5},{5,4},{6,7},{7,6},{8,9},{9,8},{10,11... | collective-permute-start | bytes 6291464 | tf_op jit(solution)/shard_map/ppermute | solution.py:291
  330.9 25.6 %collective-permute-start.44 = (bf16[64,2048]{1,0:T(8,128)(2,1)}, bf16[64,2048]{1,0:T(8,128)(2,1)}, u32[]{:S(2)}, u32[]{:S(2)}) collective-permute-start(bf16[64,2048]{1,0:T(8,128)(2,1)} %get-tuple-element.256), channel_id=1, source_target_pairs={{0,12},{2,14},{12,0},{14,2},{4,8},{6,10},{8,4},{10,6},{1,13},{3,15... | collective-permute-start | bytes 786440 | tf_op jit(solution)/shard_map/ppermute | solution.py:280
  334.4 25.4 %collective-permute-start.48 = (bf16[64,4096]{1,0:T(8,128)(2,1)}, bf16[64,4096]{1,0:T(8,128)(2,1)}, u32[]{:S(2)}, u32[]{:S(2)}) collective-permute-start(bf16[64,4096]{1,0:T(8,128)(2,1)} %get-tuple-element.337), channel_id=1, source_target_pairs={{0,2},{2,0},{4,6},{6,4},{8,10},{10,8},{12,14},{14,12},{1,3},{3,1},... | collective-permute-start | bytes 1572872 | tf_op jit(solution)/shard_map/ppermute | solution.py:280
  353.3 9.7 %collective-permute-start.47 = (bf16[256,4096]{1,0:T(8,128)(2,1)}, bf16[256,4096]{1,0:T(8,128)(2,1)}, u32[]{:S(2)}, u32[]{:S(2)}) collective-permute-start(bf16[256,4096]{1,0:T(8,128)(2,1)} %get-tuple-element.262), channel_id=1, source_target_pairs={{0,1},{1,0},{2,3},{3,2},{4,5},{5,4},{6,7},{7,6},{8,9},{9,8},{10,11... | collective-permute-start | bytes 6291464 | tf_op jit(solution)/shard_map/ppermute | solution.py:291
  354.1 34.1 %collective-permute-start.49 = (bf16[128,2048]{1,0:T(8,128)(2,1)S(1)}, bf16[128,2048]{1,0:T(8,128)(2,1)S(1)}, u32[]{:S(2)}, u32[]{:S(2)}) collective-permute-start(bf16[128,2048]{1,0:T(8,128)(2,1)S(1)} %constant_dynamic-update-slice_fusion.14.upper_ref.refs_8_), channel_id=1, source_target_pairs={{0,2},{2,0},{4,6},{6,4},{8,10},{10,8},{12,14},{14,12},{1,3},{3,1},... | collective-permute-start | bytes 1572872 | tf_op jit(solution)/shard_map/ppermute | solution.py:280
  355.3 27.3 %collective-permute-start.50 = (bf16[2,64,4096]{2,1,0:T(8,128)(2,1)}, bf16[2,64,4096]{2,1,0:T(8,128)(2,1)S(1)}, u32[]{:S(2)}, u32[]{:S(2)}) collective-permute-start(bf16[2,64,4096]{2,1,0:T(8,128)(2,1)} %pad_maximum_fusion.6), channel_id=1, source_target_pairs={{0,4},{2,6},{12,8},{14,10},{1,5},{3,7},{13,9},{15,11},{16,20},{18,... | collective-permute-start | bytes 3145736 | tf_op jit(solution)/shard_map/ppermute | solution.py:280
  356.6 56.2 %collective-permute-start.55 = (bf16[2,64,4096]{2,1,0:T(8,128)(2,1)}, bf16[2,64,4096]{2,1,0:T(8,128)(2,1)}, u32[]{:S(2)}, u32[]{:S(2)}) collective-permute-start(bf16[2,64,4096]{2,1,0:T(8,128)(2,1)} %add_convert_fusion.11), channel_id=1, source_target_pairs={{4,8},{6,10},{8,4},{10,6},{5,9},{7,11},{9,5},{11,7},{20,24},{22,26... | collective-permute-start | bytes 3145736 | tf_op jit(solution)/shard_map/ppermute | solution.py:280
  361.5 55.4 %collective-permute-start.52 = (bf16[2,64,4096]{2,1,0:T(8,128)(2,1)S(1)}, bf16[2,64,4096]{2,1,0:T(8,128)(2,1)S(1)}, u32[]{:S(2)}, u32[]{:S(2)}) collective-permute-start(bf16[2,64,4096]{2,1,0:T(8,128)(2,1)S(1)} %pad_maximum_fusion.7), channel_id=1, source_target_pairs={{0,4},{2,6},{12,8},{14,10},{1,5},{3,7},{13,9},{15,11},{16,20},{18,... | collective-permute-start | bytes 3145736 | tf_op jit(solution)/shard_map/ppermute | solution.py:280
  383.8 62.4 %collective-permute-start.58 = (bf16[2,64,4096]{2,1,0:T(8,128)(2,1)}, bf16[2,64,4096]{2,1,0:T(8,128)(2,1)}, u32[]{:S(2)}, u32[]{:S(2)}) collective-permute-start(bf16[2,64,4096]{2,1,0:T(8,128)(2,1)} %add_convert_fusion.10), channel_id=1, source_target_pairs={{4,8},{6,10},{8,4},{10,6},{5,9},{7,11},{9,5},{11,7},{20,24},{22,26... | collective-permute-start | bytes 3145736 | tf_op jit(solution)/shard_map/ppermute | solution.py:280
  386.8 28.5 %collective-permute-start.53 = (bf16[64,4096]{1,0:T(8,128)(2,1)S(1)}, bf16[64,4096]{1,0:T(8,128)(2,1)S(1)}, u32[]{:S(2)}, u32[]{:S(2)}) collective-permute-start(bf16[64,4096]{1,0:T(8,128)(2,1)S(1)} %copy-done.18), channel_id=1, source_target_pairs={{0,2},{2,0},{4,6},{6,4},{8,10},{10,8},{12,14},{14,12},{1,3},{3,1},... | collective-permute-start | bytes 1572872 | tf_op jit(solution)/shard_map/ppermute | solution.py:280
  388.1 22.1 %collective-permute-start.54 = (bf16[64,4096]{1,0:T(8,128)(2,1)S(1)}, bf16[64,4096]{1,0:T(8,128)(2,1)S(1)}, u32[]{:S(2)}, u32[]{:S(2)}) collective-permute-start(bf16[64,4096]{1,0:T(8,128)(2,1)S(1)} %get-tuple-element.331), channel_id=1, source_target_pairs={{0,2},{2,0},{4,6},{6,4},{8,10},{10,8},{12,14},{14,12},{1,3},{3,1},... | collective-permute-start | bytes 1572872 | tf_op jit(solution)/shard_map/ppermute | solution.py:280
  410.3 10.2 %collective-permute-start.51 = (bf16[256,4096]{1,0:T(8,128)(2,1)S(1)}, bf16[256,4096]{1,0:T(8,128)(2,1)S(1)}, u32[]{:S(2)}, u32[]{:S(2)}) collective-permute-start(bf16[256,4096]{1,0:T(8,128)(2,1)S(1)} %get-tuple-element.273), channel_id=1, source_target_pairs={{0,1},{1,0},{2,3},{3,2},{4,5},{5,4},{6,7},{7,6},{8,9},{9,8},{10,11... | collective-permute-start | bytes 6291464 | tf_op jit(solution)/shard_map/ppermute | solution.py:291
  415.3 31.3 %collective-permute-start.57 = (bf16[2,64,4096]{2,1,0:T(8,128)(2,1)}, bf16[2,64,4096]{2,1,0:T(8,128)(2,1)}, u32[]{:S(2)}, u32[]{:S(2)}) collective-permute-start(bf16[2,64,4096]{2,1,0:T(8,128)(2,1)} %add_convert_fusion.9), channel_id=1, source_target_pairs={{0,4},{2,6},{4,0},{6,2},{8,12},{10,14},{12,8},{14,10},{1,5},{3,7},... | collective-permute-start | bytes 3145736 | tf_op jit(solution)/shard_map/ppermute | solution.py:280
  415.6 47.2 %collective-permute-start.61 = (bf16[2,64,4096]{2,1,0:T(8,128)(2,1)S(1)}, bf16[2,64,4096]{2,1,0:T(8,128)(2,1)}, u32[]{:S(2)}, u32[]{:S(2)}) collective-permute-start(bf16[2,64,4096]{2,1,0:T(8,128)(2,1)S(1)} %pad_maximum_fusion.9), channel_id=1, source_target_pairs={{0,4},{2,6},{12,8},{14,10},{1,5},{3,7},{13,9},{15,11},{16,20},{18,... | collective-permute-start | bytes 3145736 | tf_op jit(solution)/shard_map/ppermute | solution.py:280
  418.2 51.3 %collective-permute-start.62 = (bf16[2,64,4096]{2,1,0:T(8,128)(2,1)}, bf16[2,64,4096]{2,1,0:T(8,128)(2,1)}, u32[]{:S(2)}, u32[]{:S(2)}) collective-permute-start(bf16[2,64,4096]{2,1,0:T(8,128)(2,1)} %add_convert_fusion.8), channel_id=1, source_target_pairs={{4,8},{6,10},{8,4},{10,6},{5,9},{7,11},{9,5},{11,7},{20,24},{22,26... | collective-permute-start | bytes 3145736 | tf_op jit(solution)/shard_map/ppermute | solution.py:280
  422.3 22.4 %collective-permute-start.56 = (bf16[64,4096]{1,0:T(8,128)(2,1)S(1)}, bf16[64,4096]{1,0:T(8,128)(2,1)S(1)}, u32[]{:S(2)}, u32[]{:S(2)}) collective-permute-start(bf16[64,4096]{1,0:T(8,128)(2,1)S(1)} %copy-done.19), channel_id=1, source_target_pairs={{0,2},{2,0},{4,6},{6,4},{8,10},{10,8},{12,14},{14,12},{1,3},{3,1},... | collective-permute-start | bytes 1572872 | tf_op jit(solution)/shard_map/ppermute | solution.py:280
  444.7 56.7 %collective-permute-start.63 = (bf16[64,4096]{1,0:T(8,128)(2,1)}, bf16[64,4096]{1,0:T(8,128)(2,1)S(1)}, u32[]{:S(2)}, u32[]{:S(2)}) collective-permute-start(bf16[64,4096]{1,0:T(8,128)(2,1)} %get-tuple-element.285), channel_id=1, source_target_pairs={{0,2},{2,0},{4,6},{6,4},{8,10},{10,8},{12,14},{14,12},{1,3},{3,1},... | collective-permute-start | bytes 1572872 | tf_op jit(solution)/shard_map/ppermute | solution.py:280
  446.2 22.9 %collective-permute-start.60 = (bf16[64,4096]{1,0:T(8,128)(2,1)S(1)}, bf16[64,4096]{1,0:T(8,128)(2,1)S(1)}, u32[]{:S(2)}, u32[]{:S(2)}) collective-permute-start(bf16[64,4096]{1,0:T(8,128)(2,1)S(1)} %get-tuple-element.326), channel_id=1, source_target_pairs={{0,2},{2,0},{4,6},{6,4},{8,10},{10,8},{12,14},{14,12},{1,3},{3,1},... | collective-permute-start | bytes 1572872 | tf_op jit(solution)/shard_map/ppermute | solution.py:280
  470.9 30.8 %collective-permute-start.64 = (bf16[2,64,4096]{2,1,0:T(8,128)(2,1)S(1)}, bf16[2,64,4096]{2,1,0:T(8,128)(2,1)S(1)}, u32[]{:S(2)}, u32[]{:S(2)}) collective-permute-start(bf16[2,64,4096]{2,1,0:T(8,128)(2,1)S(1)} %add_convert_fusion.5), channel_id=1, source_target_pairs={{0,4},{2,6},{4,0},{6,2},{8,12},{10,14},{12,8},{14,10},{1,5},{3,7},... | collective-permute-start | bytes 3145736 | tf_op jit(solution)/shard_map/ppermute | solution.py:280
  473.4 28.4 %collective-permute-start.65 = (bf16[2,64,4096]{2,1,0:T(8,128)(2,1)S(1)}, bf16[2,64,4096]{2,1,0:T(8,128)(2,1)S(1)}, u32[]{:S(2)}, u32[]{:S(2)}) collective-permute-start(bf16[2,64,4096]{2,1,0:T(8,128)(2,1)S(1)} %add_convert_fusion.6), channel_id=1, source_target_pairs={{4,8},{6,10},{8,4},{10,6},{5,9},{7,11},{9,5},{11,7},{20,24},{22,26... | collective-permute-start | bytes 3145736 | tf_op jit(solution)/shard_map/ppermute | solution.py:280
  475.9 24.1 %collective-permute-start.59 = (bf16[2,64,4096]{2,1,0:T(8,128)(2,1)S(1)}, bf16[2,64,4096]{2,1,0:T(8,128)(2,1)S(1)}, u32[]{:S(2)}, u32[]{:S(2)}) collective-permute-start(bf16[2,64,4096]{2,1,0:T(8,128)(2,1)S(1)} %add_convert_fusion.7), channel_id=1, source_target_pairs={{0,1},{1,0},{2,3},{3,2},{4,5},{5,4},{6,7},{7,6},{8,9},{9,8},{10,11... | collective-permute-start | bytes 3145736 | tf_op jit(solution)/shard_map/ppermute | solution.py:291
  (24 other events, 265.1 us)

commit v2 on v1

--- a/solution.py
+++ b/solution.py
@@ -8,6 +8,7 @@
 PAIRS = 2
 SPLIT = (1, 1)
 STRIP = 1024
+DEEP = 2048
 VMEM_LIMIT = 48 * 1024 * 1024
 
 
@@ -100,7 +101,7 @@
 def rebuild(core, own, other, decoder):
     rows, half = own.shape
     depth = decoder.shape[1]
-    strips = half // min(STRIP, half)
+    strips = half // min(DEEP, half)
     kept = rows // 2
 
     def kernel(core_ref, own_ref, other_ref, decoder_ref, *rest):
@@ -138,9 +139,9 @@
         core,
         [own, other, decoder],
         [
-            pl.BlockSpec((rows, STRIP), lambda i, c: (0, jnp.minimum(i, strips - 1))),
-            pl.BlockSpec((rows, STRIP), lambda i, c: (0, jnp.maximum(i - strips, 0))),
-            pl.BlockSpec((STRIP, depth), strip),
+            pl.BlockSpec((rows, DEEP), lambda i, c: (0, jnp.minimum(i, strips - 1))),
+            pl.BlockSpec((rows, DEEP), lambda i, c: (0, jnp.maximum(i - strips, 0))),
+            pl.BlockSpec((DEEP, depth), strip),
         ],
         2 * strips,
         [out, out],

time: 522 us -> 519 us (level)
  waiting for transfers between devices: 164 us -> 178 us
  starting transfers between devices: 105 us -> 94 us
  Pallas kernels: 178 us -> 172 us
    ppermute x57, waiting for transfers between devices: 161 us -> 176 us  [feat(): return lax.ppermute(value, 'feat', perm)]
    ppermute x57, starting transfers between devices: 77.6 us -> 66.6 us  [feat(): return lax.ppermute(value, 'feat', perm)]
    pallas_call x10, Pallas kernels: 178 us -> 172 us  [call(): pl.pallas_call(kernel, grid_spec=pltpu.PrefetchScalarGridSpec(num_scalar_...]
  transfers between devices with their start and end apart: 67 -> 67, of which waited for: 26 -> 27; matrix products, arithmetic and copies ran while one was open for 9% -> 9% of each run, Pallas kernels for 32% -> 30%
where the time goes in v2:
time: 519 us; the launch traced here: 509 us
  waiting for transfers between devices  178 us (34%)
  Pallas kernels  172 us (33%)
  starting transfers between devices  94 us (18%)
  other arithmetic  32 us (6%)
  local copies, waits for them, and re-layouts  30.7 us (6%)
    ppermute x57, waiting for transfers between devices, feat(): return lax.ppermute(value, 'feat', perm)  176 us
    pallas_call x10, Pallas kernels, call(): pl.pallas_call(kernel, grid_spec=pltpu.PrefetchScalarGridSpec(num_scalar_...  172 us
    ppermute x57, starting transfers between devices, feat(): return lax.ppermute(value, 'feat', perm)  66.6 us
    ppermute x10, starting transfers between devices, other_core(): return lax.ppermute(value, 'pair', [(0, 1), (1, 0)])  27.4 us
    convert_element_type x16, other arithmetic, add(): sum((term.astype(jnp.float32) for term in terms)).astype(jnp.bfloat16)  16.8 us
    unnamed x55, local copies, waits for them, and re-layouts  14.4 us
  transfers between devices with their start and end apart: 67, of which 27 were waited for; matrix products, arithmetic and copies ran while one was open for 9% of the time, Pallas kernels for 30%

profile of v2, /device:TPU:9, one launch (start us, length us, event | category | flops | bytes accessed | tf_op | source)
XLA Modules:
  0.0 509.3 jit_solution(519102496921965376)
XLA Ops:
  0.6 2.1 constant_dynamic-slice_fusion
  3.4 3.2 collective-permute-start.1
  6.7 6.9 %copy.13 = bf16[128,2,8192]{2,0,1:T(8,128)(2,1)} copy(bf16[128,2,8192]{2,1,0:T(2,128)(2,1)} %param.4) | data formatting | bytes 8388608 | tf_op jit(solution)/shard_map/optimization_barrier | solution.py:313
  15.0 14.4 %collective-permute-done.1 = bf16[2,64,4096]{2,1,0:T(8,128)(2,1)} collective-permute-done((bf16[2,64,4096]{2,1,0:T(8,128)(2,1)S(1)}, bf16[2,64,4096]{2,1,0:T(8,128)(2,1)}, u32[]{:S(2)}, u32[]{:S(2)}) %collective-permute-start.1) | collective-permute-done | bytes 1048608 | tf_op jit(solution)/shard_map/ppermute | solution.py:281
  31.9 2.1 collective-permute-start.2
  34.0 2.1 collective-permute-start.7
  39.6 18.3 %collective-permute-done.7 = bf16[2,64,4096]{2,1,0:T(8,128)(2,1)S(1)} collective-permute-done((bf16[2,64,4096]{2,1,0:T(8,128)(2,1)S(1)}, bf16[2,64,4096]{2,1,0:T(8,128)(2,1)S(1)}, u32[]{:S(2)}, u32[]{:S(2)}) %collective-permute-start.7) | collective-permute-done | bytes 1048608 | tf_op jit(solution)/shard_map/ppermute | solution.py:281
  63.5 3.5 collective-permute-start.8
  67.1 1.5 collective-permute-start.12
  71.0 15.7 %shard_map.67 = (bf16[128,2048]{1,0:T(8,128)(2,1)S(1)}, bf16[128,2048]{1,0:T(8,128)(2,1)S(1)}) custom-call(s32[1]{0:T(128)} %bitcast.core_ref.side_ref, bf16[256,4096]{1,0:T(8,128)(2,1)} %constant_dynamic-update-slice_fusion.own_ref.refs_0_, bf16[256,4096]{1,0:T(8,128)(2,1)S(1)} %collective-permute-done.8.other_ref.refs_0_, bf16[8192,2048]{1,0:T(8,128)(2,1)} %decoder_ref.15), custom_call_target="tpu_custom_call" | custom-call | flops 8589934592 | bytes 33554432 | tf_op jit(solution)/shard_map/pallas_call | solution.py:83
  86.7 4.7 collective-permute-done.12
  93.0 3.1 collective-permute-start.11
  96.3 8.2 %collective-permute-done.14 = bf16[64,4096]{1,0:T(8,128)(2,1)S(1)} collective-permute-done((bf16[64,4096]{1,0:T(8,128)(2,1)S(1)}, bf16[64,4096]{1,0:T(8,128)(2,1)S(1)}, u32[]{:S(2)}, u32[]{:S(2)}) %collective-permute-start.14) | collective-permute-done | bytes 524320 | tf_op jit(solution)/shard_map/ppermute | solution.py:281
  104.7 1.7 collective-permute-start.17
  106.4 12.1 %collective-permute-done.11 = bf16[2,64,4096]{2,1,0:T(8,128)(2,1)S(1)} collective-permute-done((bf16[2,64,4096]{2,1,0:T(8,128)(2,1)S(1)}, bf16[2,64,4096]{2,1,0:T(8,128)(2,1)S(1)}, u32[]{:S(2)}, u32[]{:S(2)}) %collective-permute-start.11) | collective-permute-done | bytes 1048608 | tf_op jit(solution)/shard_map/ppermute | solution.py:281
  119.6 2.1 collective-permute-start.16
  121.7 1.7 collective-permute-start.15
  124.4 15.2 %shard_map.68 = (bf16[128,2048]{1,0:T(8,128)(2,1)S(1)}, bf16[128,2048]{1,0:T(8,128)(2,1)S(1)}) custom-call(s32[1]{0:T(128)} %bitcast.core_ref.side_ref, bf16[256,4096]{1,0:T(8,128)(2,1)S(1)} %constant_dynamic-update-slice_fusion.2.own_ref.refs_1_, bf16[256,4096]{1,0:T(8,128)(2,1)S(1)} %collective-permute-done.17.other_ref.refs_1_, ...), custom_call_target="tpu_custom_call" | custom-call | flops 8589934592 | bytes 33554432 | tf_op jit(solution)/shard_map/pallas_call | solution.py:83
  139.6 4.3 collective-permute-done.16
  146.3 3.5 collective-permute-start.20
  152.9 10.4 %collective-permute-done.21 = bf16[128,2048]{1,0:T(8,128)(2,1)S(1)} collective-permute-done((bf16[128,2048]{1,0:T(8,128)(2,1)S(1)}, bf16[128,2048]{1,0:T(8,128)(2,1)S(1)}, u32[]{:S(2)}, u32[]{:S(2)}) %collective-permute-start.21) | collective-permute-done | bytes 524320 | tf_op jit(solution)/shard_map/ppermute | solution.py:281
  163.4 2.6 collective-permute-start.18
  166.3 15.1 %shard_map.69 = (bf16[128,2048]{1,0:T(8,128)(2,1)S(1)}, bf16[128,2048]{1,0:T(8,128)(2,1)S(1)}) custom-call(s32[1]{0:T(128)} %bitcast.core_ref.side_ref, bf16[256,4096]{1,0:T(8,128)(2,1)S(1)} %constant_dynamic-update-slice_fusion.6.own_ref.refs_2_, bf16[256,4096]{1,0:T(8,128)(2,1)S(1)} %collective-permute-done.20.other_ref.refs_2_, ...), custom_call_target="tpu_custom_call" | custom-call | flops 8589934592 | bytes 33554432 | tf_op jit(solution)/shard_map/pallas_call | solution.py:83
  181.4 5.7 %collective-permute-done.18 = bf16[2,64,4096]{2,1,0:T(8,128)(2,1)S(1)} collective-permute-done((bf16[2,64,4096]{2,1,0:T(8,128)(2,1)S(1)}, bf16[2,64,4096]{2,1,0:T(8,128)(2,1)S(1)}, u32[]{:S(2)}, u32[]{:S(2)}) %collective-permute-start.18) | collective-permute-done | bytes 1048608 | tf_op jit(solution)/shard_map/ppermute | solution.py:281
  189.2 7.3 %collective-permute-done.24 = bf16[128,2048]{1,0:T(8,128)(2,1)S(1)} collective-permute-done((bf16[128,2048]{1,0:T(8,128)(2,1)S(1)}, bf16[128,2048]{1,0:T(8,128)(2,1)S(1)}, u32[]{:S(2)}, u32[]{:S(2)}) %collective-permute-start.24) | collective-permute-done | bytes 524320 | tf_op jit(solution)/shard_map/ppermute | solution.py:281
  196.4 2.2 collective-permute-start.22
  201.6 6.1 %collective-permute-done.28 = bf16[64,4096]{1,0:T(8,128)(2,1)S(1)} collective-permute-done((bf16[64,4096]{1,0:T(8,128)(2,1)S(1)}, bf16[64,4096]{1,0:T(8,128)(2,1)S(1)}, u32[]{:S(2)}, u32[]{:S(2)}) %collective-permute-start.28) | collective-permute-done | bytes 524320 | tf_op jit(solution)/shard_map/ppermute | solution.py:281
  207.9 5.0 collective-permute-start.30
  213.1 2.3 collective-permute-start.31
  216.5 5.8 %collective-permute-done.31 = bf16[64,2048]{1,0:T(8,128)(2,1)S(1)} collective-permute-done((bf16[64,2048]{1,0:T(8,128)(2,1)S(1)}, bf16[64,2048]{1,0:T(8,128)(2,1)S(1)}, u32[]{:S(2)}, u32[]{:S(2)}) %collective-permute-start.31) | collective-permute-done | bytes 262176 | tf_op jit(solution)/shard_map/ppermute | solution.py:281
  222.4 15.2 %shard_map.70 = (bf16[128,2048]{1,0:T(8,128)(2,1)S(1)}, bf16[128,2048]{1,0:T(8,128)(2,1)S(1)}) custom-call(s32[1]{0:T(128)} %bitcast.core_ref.side_ref, bf16[256,4096]{1,0:T(8,128)(2,1)S(1)} %constant_dynamic-update-slice_fusion.8.own_ref.refs_3_, bf16[256,4096]{1,0:T(8,128)(2,1)S(1)} %collective-permute-done.30.other_ref.refs_3_, ...), custom_call_target="tpu_custom_call" | custom-call | flops 8589934592 | bytes 33554432 | tf_op jit(solution)/shard_map/pallas_call | solution.py:83
  237.6 16.7 %shard_map.71 = (bf16[256,4096]{1,0:T(8,128)(2,1)S(1)}, bf16[256,4096]{1,0:T(8,128)(2,1)S(1)}) custom-call(s32[1]{0:T(128)} %bitcast.core_ref.side_ref, bf16[128,2048]{1,0:T(8,128)(2,1)S(1)} %pad_maximum_fusion.14.upper_ref.refs_6_, bf16[128,2048]{1,0:T(8,128)(2,1)S(1)} %collective-permute-done.34.lower_ref.refs_7_, bf16[8192,2048]{1,0:T(8,128)(2,1)} %decoder_ref.15), custom_call_target="tpu_custom_call" | custom-call | flops 8589934592 | bytes 33554432 | tf_op jit(solution)/shard_map/pallas_call | solution.py:83
  254.3 2.0 collective-permute-start.36
  256.4 1.5 collective-permute-start.33
  260.7 3.6 collective-permute-done.33
  264.3 6.8 %collective-permute-done.32 = bf16[128,2048]{1,0:T(8,128)(2,1)S(1)} collective-permute-done((bf16[128,2048]{1,0:T(8,128)(2,1)S(1)}, bf16[128,2048]{1,0:T(8,128)(2,1)S(1)}, u32[]{:S(2)}, u32[]{:S(2)}) %collective-permute-start.32) | collective-permute-done | bytes 524320 | tf_op jit(solution)/shard_map/ppermute | solution.py:281
  272.2 5.0 collective-permute-done.35
  279.9 3.7 collective-permute-done.40
  285.2 6.1 %collective-permute-done.39 = bf16[64,4096]{1,0:T(8,128)(2,1)S(1)} collective-permute-done((bf16[64,4096]{1,0:T(8,128)(2,1)S(1)}, bf16[64,4096]{1,0:T(8,128)(2,1)S(1)}, u32[]{:S(2)}, u32[]{:S(2)}) %collective-permute-start.39) | collective-permute-done | bytes 524320 | tf_op jit(solution)/shard_map/ppermute | solution.py:281
  292.9 9.6 %collective-permute-done.43.lower_ref.refs_11_ = bf16[128,2048]{1,0:T(8,128)(2,1)S(1)} collective-permute-done((bf16[128,2048]{1,0:T(8,128)(2,1)S(1)}, bf16[128,2048]{1,0:T(8,128)(2,1)S(1)}, u32[]{:S(2)}, u32[]{:S(2)}) %collective-permute-start.43) | collective-permute-done | bytes 524320 | tf_op jit(solution)/shard_map/ppermute | solution.py:281
  302.5 16.3 %shard_map.72 = (bf16[256,4096]{1,0:T(8,128)(2,1)S(1)}, bf16[256,4096]{1,0:T(8,128)(2,1)S(1)}) custom-call(s32[1]{0:T(128)} %bitcast.core_ref.side_ref, bf16[128,2048]{1,0:T(8,128)(2,1)S(1)} %pad_maximum_fusion.16.upper_ref.refs_10_, bf16[128,2048]{1,0:T(8,128)(2,1)S(1)} %collective-permute-done.43.lower_ref.refs_11_, bf16[8192,2048]{1,0:T(8,128)(2,1)} %decoder_ref.15), custom_call_target="tpu_custom_call" | custom-call | flops 8589934592 | bytes 33554432 | tf_op jit(solution)/shard_map/pallas_call | solution.py:83
  318.8 6.7 %collective-permute-start.46 = (bf16[256,4096]{1,0:T(8,128)(2,1)S(1)}, bf16[256,4096]{1,0:T(8,128)(2,1)S(1)}, u32[]{:S(2)}, u32[]{:S(2)}) collective-permute-start(bf16[256,4096]{1,0:T(8,128)(2,1)S(1)} %get-tuple-element.251), channel_id=1, source_target_pairs={{0,1},{1,0},{2,3},{3,2},{4,5},{5,4},{6,7},{7,6},{8,9},{9,8},{10,11... | collective-permute-start | bytes 6291464 | tf_op jit(solution)/shard_map/ppermute | solution.py:292
  331.7 17.3 %shard_map.73 = (bf16[256,4096]{1,0:T(8,128)(2,1)}, bf16[256,4096]{1,0:T(8,128)(2,1)S(1)}) custom-call(s32[1]{0:T(128)} %bitcast.core_ref.side_ref, bf16[128,2048]{1,0:T(8,128)(2,1)S(1)} %constant_dynamic-update-slice_fusion.12.upper_ref.refs_4_, bf16[128,2048]{1,0:T(8,128)(2,1)S(1)} %collective-permute-done.45.lower_ref.refs_5_, bf16[8192,2048]{1,0:T(8,128)(2,1)} %decoder_ref.15), custom_call_target="tpu_custom_call" | custom-call | flops 8589934592 | bytes 33554432 | tf_op jit(solution)/shard_map/pallas_call | solution.py:83
  353.7 2.1 collective-permute-start.55
  356.9 1.6 select_bitcast_fusion.13
  360.1 2.4 add_convert_fusion.1
  362.4 17.2 %collective-permute-done.50 = bf16[2,64,4096]{2,1,0:T(8,128)(2,1)S(1)} collective-permute-done((bf16[2,64,4096]{2,1,0:T(8,128)(2,1)}, bf16[2,64,4096]{2,1,0:T(8,128)(2,1)S(1)}, u32[]{:S(2)}, u32[]{:S(2)}) %collective-permute-start.50) | collective-permute-done | bytes 1048608 | tf_op jit(solution)/shard_map/ppermute | solution.py:281
  380.8 3.0 collective-permute-start.58
  386.4 16.3 %shard_map.74 = (bf16[256,4096]{1,0:T(8,128)(2,1)S(1)}, bf16[256,4096]{1,0:T(8,128)(2,1)S(1)}) custom-call(s32[1]{0:T(128)} %bitcast.core_ref.side_ref, bf16[128,2048]{1,0:T(8,128)(2,1)S(1)} %constant_dynamic-update-slice_fusion.14.upper_ref.refs_8_, bf16[128,2048]{1,0:T(8,128)(2,1)S(1)} %collective-permute-done.49.lower_ref.refs_9_, ...), custom_call_target="tpu_custom_call" | custom-call | flops 8589934592 | bytes 33554432 | tf_op jit(solution)/shard_map/pallas_call | solution.py:83
  402.7 4.6 collective-permute-done.54
  407.3 2.2 collective-permute-start.51
  409.8 2.5 add_convert_fusion.9
  412.7 1.5 collective-permute-start.61
  415.4 2.3 collective-permute-start.62
  419.9 22.1 %shard_map.75.refs_12_ = bf16[8192,2048]{1,0:T(8,128)(2,1)} custom-call(s32[1]{0:T(128)} %bitcast.core_ref.side_ref, bf16[256,4096]{1,0:T(8,128)(2,1)} %constant_dynamic-update-slice_fusion.own_ref.refs_0_, bf16[256,4096]{1,0:T(8,128)(2,1)} %copy-done.5, bf16[256,4096]{1,0:T(8,128)(2,1)} %copy-done.4, bf16[256,4096]{1,0:T(8,128)(2,1)} %copy-done.6, ...), custom_call_target="tpu_custom_call" | custom-call | flops 17179869184 | bytes 25165824 | tf_op jit(solution)/shard_map/pallas_call | solution.py:83
  443.8 2.0 add_convert_fusion.7
  445.8 14.1 %collective-permute-done.61 = bf16[2,64,4096]{2,1,0:T(8,128)(2,1)} collective-permute-done((bf16[2,64,4096]{2,1,0:T(8,128)(2,1)S(1)}, bf16[2,64,4096]{2,1,0:T(8,128)(2,1)}, u32[]{:S(2)}, u32[]{:S(2)}) %collective-permute-start.61) | collective-permute-done | bytes 1048608 | tf_op jit(solution)/shard_map/ppermute | solution.py:281
  461.4 5.0 collective-permute-done.60
  468.2 2.5 collective-permute-start.64
  470.6 2.3 collective-permute-start.65
  472.9 2.0 collective-permute-start.59
  474.9 22.1 %shard_map.76 = bf16[8192,2048]{1,0:T(8,128)(2,1)} custom-call(s32[1]{0:T(128)S(6)} %sub.33.side_ref, bf16[256,4096]{1,0:T(8,128)(2,1)} %copy-done, bf16[256,4096]{1,0:T(8,128)(2,1)} %copy-done.1, bf16[256,4096]{1,0:T(8,128)(2,1)} %copy-done.2, bf16[256,4096]{1,0:T(8,128)(2,1)} %copy-done.3, ...), custom_call_target="tpu_custom_call", output_to_operand_aliasing={{}: (13, {})} | custom-call | flops 17179869184 | bytes 25165824 | tf_op jit(solution)/shard_map/pallas_call | solution.py:83
  499.4 2.0 copy.16
  502.6 6.4 %copy.17 = bf16[128,2,8192]{2,1,0:T(2,128)(2,1)} copy(bf16[128,2,8192]{2,0,1:T(8,128)(2,1)S(1)} %pad_maximum_fusion) | data formatting | bytes 8388608
  (242 shorter events, 71.4 us)
Async XLA Ops:
  3.4 26.0 %collective-permute-start.1 = (bf16[2,64,4096]{2,1,0:T(8,128)(2,1)S(1)}, bf16[2,64,4096]{2,1,0:T(8,128)(2,1)}, u32[]{:S(2)}, u32[]{:S(2)}) collective-permute-start(bf16[2,64,4096]{2,1,0:T(8,128)(2,1)S(1)} %bitcast.302), channel_id=1, source_target_pairs={{4,8},{6,10},{8,4},{10,6},{5,9},{7,11},{9,5},{11,7},{20,24},{22,26... | collective-permute-start | bytes 3145736 | tf_op jit(solution)/shard_map/ppermute | solution.py:281
  6.6 23.9 %collective-permute-start = (bf16[2,64,4096]{2,1,0:T(8,128)(2,1)S(1)}, bf16[2,64,4096]{2,1,0:T(8,128)(2,1)S(1)}, u32[]{:S(2)}, u32[]{:S(2)}) collective-permute-start(bf16[2,64,4096]{2,1,0:T(8,128)(2,1)S(1)} %bitcast.303), channel_id=1, source_target_pairs={{0,4},{2,6},{4,0},{6,2},{8,12},{10,14},{12,8},{14,10},{1,5},{3,7},... | collective-permute-start | bytes 3145736 | tf_op jit(solution)/shard_map/ppermute | solution.py:281
  30.5 8.9 %collective-permute-start.5 = (s32[128,2]{0,1:T(2,128)S(1)}, s32[128,2]{0,1:T(2,128)S(1)}, u32[]{:S(2)}, u32[]{:S(2)}) collective-permute-start(s32[128,2]{0,1:T(2,128)S(1)} %copy-done.20), channel_id=1, source_target_pairs={{0,8},{2,10},{8,0},{10,2},{4,12},{6,14},{12,4},{14,6},{1,9},{3,11}... | collective-permute-start | bytes 3080 | tf_op jit(solution)/shard_map/ppermute | solution.py:281
  31.4 8.1 %collective-permute-start.4 = (s32[128,2]{0,1:T(2,128)S(1)}, s32[128,2]{0,1:T(2,128)S(1)}, u32[]{:S(2)}, u32[]{:S(2)}) collective-permute-start(s32[128,2]{0,1:T(2,128)S(1)} %copy-done.20), channel_id=1, source_target_pairs={{0,12},{2,14},{12,0},{14,2},{4,8},{6,10},{8,4},{10,6},{1,13},{3,15... | collective-permute-start | bytes 3080 | tf_op jit(solution)/shard_map/ppermute | solution.py:281
  34.0 23.9 %collective-permute-start.7 = (bf16[2,64,4096]{2,1,0:T(8,128)(2,1)S(1)}, bf16[2,64,4096]{2,1,0:T(8,128)(2,1)S(1)}, u32[]{:S(2)}, u32[]{:S(2)}) collective-permute-start(bf16[2,64,4096]{2,1,0:T(8,128)(2,1)S(1)} %collective-permute-done), channel_id=1, source_target_pairs={{4,8},{6,10},{8,4},{10,6},{5,9},{7,11},{9,5},{11,7},{20,24},{22,26... | collective-permute-start | bytes 3145736 | tf_op jit(solution)/shard_map/ppermute | solution.py:281
  36.1 22.8 %collective-permute-start.6 = (bf16[2,64,4096]{2,1,0:T(8,128)(2,1)}, bf16[2,64,4096]{2,1,0:T(8,128)(2,1)S(1)}, u32[]{:S(2)}, u32[]{:S(2)}) collective-permute-start(bf16[2,64,4096]{2,1,0:T(8,128)(2,1)} %collective-permute-done.1), channel_id=1, source_target_pairs={{4,0},{6,2},{8,12},{10,14},{5,1},{7,3},{9,13},{11,15},{20,16},{22,... | collective-permute-start | bytes 3145736 | tf_op jit(solution)/shard_map/ppermute | solution.py:281
  38.1 23.3 %collective-permute-start.3 = (bf16[128,4096]{1,0:T(8,128)(2,1)S(1)}, bf16[128,4096]{1,0:T(8,128)(2,1)S(1)}, u32[]{:S(2)}, u32[]{:S(2)}) collective-permute-start(bf16[128,4096]{1,0:T(8,128)(2,1)S(1)} %pad_maximum_fusion.2), channel_id=1, source_target_pairs={{0,2},{2,0},{4,6},{6,4},{8,10},{10,8},{12,14},{14,12},{1,3},{3,1},... | collective-permute-start | bytes 3145736 | tf_op jit(solution)/shard_map/ppermute | solution.py:281
  63.5 7.5 %collective-permute-start.8 = (bf16[256,4096]{1,0:T(8,128)(2,1)}, bf16[256,4096]{1,0:T(8,128)(2,1)S(1)}, u32[]{:S(2)}, u32[]{:S(2)}) collective-permute-start(bf16[256,4096]{1,0:T(8,128)(2,1)} %constant_dynamic-update-slice_fusion.own_ref.refs_0_), channel_id=1, source_target_pairs={{0,1},{1,0},{2,3},{3,2},{4,5},{5,4},{6,7},{7,6},{8,9},{9,8},{10,11... | collective-permute-start | bytes 6291464 | tf_op jit(solution)/shard_map/ppermute | solution.py:292
  67.1 24.4 %collective-permute-start.12 = (bf16[2,64,4096]{2,1,0:T(8,128)(2,1)}, bf16[2,64,4096]{2,1,0:T(8,128)(2,1)S(1)}, u32[]{:S(2)}, u32[]{:S(2)}) collective-permute-start(bf16[2,64,4096]{2,1,0:T(8,128)(2,1)} %copy-done.16), channel_id=1, source_target_pairs={{4,0},{6,2},{8,12},{10,14},{5,1},{7,3},{9,13},{11,15},{20,16},{22,... | collective-permute-start | bytes 3145736 | tf_op jit(solution)/shard_map/ppermute | solution.py:281
  68.6 27.7 %collective-permute-start.13 = (bf16[64,4096]{1,0:T(8,128)(2,1)}, bf16[64,4096]{1,0:T(8,128)(2,1)S(1)}, u32[]{:S(2)}, u32[]{:S(2)}) collective-permute-start(bf16[64,4096]{1,0:T(8,128)(2,1)} %get-tuple-element.372), channel_id=1, source_target_pairs={{0,2},{2,0},{4,6},{6,4},{8,10},{10,8},{12,14},{14,12},{1,3},{3,1},... | collective-permute-start | bytes 1572872 | tf_op jit(solution)/shard_map/ppermute | solution.py:281
  91.7 12.7 %collective-permute-start.14 = (bf16[64,4096]{1,0:T(8,128)(2,1)S(1)}, bf16[64,4096]{1,0:T(8,128)(2,1)S(1)}, u32[]{:S(2)}, u32[]{:S(2)}) collective-permute-start(bf16[64,4096]{1,0:T(8,128)(2,1)S(1)} %get-tuple-element.369), channel_id=1, source_target_pairs={{0,2},{2,0},{4,6},{6,4},{8,10},{10,8},{12,14},{14,12},{1,3},{3,1},... | collective-permute-start | bytes 1572872 | tf_op jit(solution)/shard_map/ppermute | solution.py:281
  93.0 25.5 %collective-permute-start.11 = (bf16[2,64,4096]{2,1,0:T(8,128)(2,1)S(1)}, bf16[2,64,4096]{2,1,0:T(8,128)(2,1)S(1)}, u32[]{:S(2)}, u32[]{:S(2)}) collective-permute-start(bf16[2,64,4096]{2,1,0:T(8,128)(2,1)S(1)} %dynamic-slice_bitcast_fusion), channel_id=1, source_target_pairs={{4,8},{6,10},{8,4},{10,6},{5,9},{7,11},{9,5},{11,7},{20,24},{22,26... | collective-permute-start | bytes 3145736 | tf_op jit(solution)/shard_map/ppermute | solution.py:281
  96.2 23.4 %collective-permute-start.10 = (bf16[2,64,4096]{2,1,0:T(8,128)(2,1)S(1)}, bf16[2,64,4096]{2,1,0:T(8,128)(2,1)S(1)}, u32[]{:S(2)}, u32[]{:S(2)}) collective-permute-start(bf16[2,64,4096]{2,1,0:T(8,128)(2,1)S(1)} %dynamic-slice_bitcast_fusion), channel_id=1, source_target_pairs={{0,4},{2,6},{4,0},{6,2},{8,12},{10,14},{12,8},{14,10},{1,5},{3,7},... | collective-permute-start | bytes 3145736 | tf_op jit(solution)/shard_map/ppermute | solution.py:281
  104.7 19.7 %collective-permute-start.17 = (bf16[256,4096]{1,0:T(8,128)(2,1)S(1)}, bf16[256,4096]{1,0:T(8,128)(2,1)S(1)}, u32[]{:S(2)}, u32[]{:S(2)}) collective-permute-start(bf16[256,4096]{1,0:T(8,128)(2,1)S(1)} %constant_dynamic-update-slice_fusion.2.own_ref.refs_1_), channel_id=1, source_target_pairs={{0,1},{1,0},{2,3},{3,2},{4,5},{5,4},{6,7},{7,6},{8,9},{9,8},{10,11... | collective-permute-start | bytes 6291464 | tf_op jit(solution)/shard_map/ppermute | solution.py:292
  119.6 24.3 %collective-permute-start.16 = (bf16[2,64,4096]{2,1,0:T(8,128)(2,1)S(1)}, bf16[2,64,4096]{2,1,0:T(8,128)(2,1)S(1)}, u32[]{:S(2)}, u32[]{:S(2)}) collective-permute-start(bf16[2,64,4096]{2,1,0:T(8,128)(2,1)S(1)} %collective-permute-done.10), channel_id=1, source_target_pairs={{4,8},{6,10},{8,4},{10,6},{5,9},{7,11},{9,5},{11,7},{20,24},{22,26... | collective-permute-start | bytes 3145736 | tf_op jit(solution)/shard_map/ppermute | solution.py:281
  121.7 22.1 %collective-permute-start.15 = (bf16[2,64,4096]{2,1,0:T(8,128)(2,1)S(1)}, bf16[2,64,4096]{2,1,0:T(8,128)(2,1)S(1)}, u32[]{:S(2)}, u32[]{:S(2)}) collective-permute-start(bf16[2,64,4096]{2,1,0:T(8,128)(2,1)S(1)} %collective-permute-done.11), channel_id=1, source_target_pairs={{4,0},{6,2},{8,12},{10,14},{5,1},{7,3},{9,13},{11,15},{20,16},{22,... | collective-permute-start | bytes 3145736 | tf_op jit(solution)/shard_map/ppermute | solution.py:281
  123.9 22.2 %collective-permute-start.19 = (bf16[128,4096]{1,0:T(8,128)(2,1)S(1)}, bf16[128,4096]{1,0:T(8,128)(2,1)S(1)}, u32[]{:S(2)}, u32[]{:S(2)}) collective-permute-start(bf16[128,4096]{1,0:T(8,128)(2,1)S(1)} %pad_maximum_fusion.3), channel_id=1, source_target_pairs={{0,2},{2,0},{4,6},{6,4},{8,10},{10,8},{12,14},{14,12},{1,3},{3,1},... | collective-permute-start | bytes 3145736 | tf_op jit(solution)/shard_map/ppermute | solution.py:281
  146.3 19.9 %collective-permute-start.20 = (bf16[256,4096]{1,0:T(8,128)(2,1)S(1)}, bf16[256,4096]{1,0:T(8,128)(2,1)S(1)}, u32[]{:S(2)}, u32[]{:S(2)}) collective-permute-start(bf16[256,4096]{1,0:T(8,128)(2,1)S(1)} %constant_dynamic-update-slice_fusion.6.own_ref.refs_2_), channel_id=1, source_target_pairs={{0,1},{1,0},{2,3},{3,2},{4,5},{5,4},{6,7},{7,6},{8,9},{9,8},{10,11... | collective-permute-start | bytes 6291464 | tf_op jit(solution)/shard_map/ppermute | solution.py:292
  149.8 13.5 %collective-permute-start.21 = (bf16[128,2048]{1,0:T(8,128)(2,1)S(1)}, bf16[128,2048]{1,0:T(8,128)(2,1)S(1)}, u32[]{:S(2)}, u32[]{:S(2)}) collective-permute-start(bf16[128,2048]{1,0:T(8,128)(2,1)S(1)} %get-tuple-element.188), channel_id=1, source_target_pairs={{0,2},{2,0},{4,6},{6,4},{8,10},{10,8},{12,14},{14,12},{1,3},{3,1},... | collective-permute-start | bytes 1572872 | tf_op jit(solution)/shard_map/ppermute | solution.py:281
  150.1 37.6 %collective-permute-start.9 = (bf16[128,2048]{1,0:T(8,128)(2,1)S(1)}, bf16[128,2048]{1,0:T(8,128)(2,1)S(1)}, u32[]{:S(2)}, u32[]{:S(2)}) collective-permute-start(bf16[128,2048]{1,0:T(8,128)(2,1)S(1)} %get-tuple-element.171), channel_id=1, source_target_pairs={{0,2},{2,0},{4,6},{6,4},{8,10},{10,8},{12,14},{14,12},{1,3},{3,1},... | collective-permute-start | bytes 1572872 | tf_op jit(solution)/shard_map/ppermute | solution.py:281
  151.4 50.2 %collective-permute-start.27 = (bf16[64,4096]{1,0:T(8,128)(2,1)S(1)}, bf16[64,4096]{1,0:T(8,128)(2,1)S(1)}, u32[]{:S(2)}, u32[]{:S(2)}) collective-permute-start(bf16[64,4096]{1,0:T(8,128)(2,1)S(1)} %get-tuple-element.364), channel_id=1, source_target_pairs={{0,2},{2,0},{4,6},{6,4},{8,10},{10,8},{12,14},{14,12},{1,3},{3,1},... | collective-permute-start | bytes 1572872 | tf_op jit(solution)/shard_map/ppermute | solution.py:281
  151.7 47.1 %collective-permute-start.25 = (bf16[64,2048]{1,0:T(8,128)(2,1)S(1)}, bf16[64,2048]{1,0:T(8,128)(2,1)S(1)}, u32[]{:S(2)}, u32[]{:S(2)}) collective-permute-start(bf16[64,2048]{1,0:T(8,128)(2,1)S(1)} %get-tuple-element.392), channel_id=1, source_target_pairs={{0,12},{2,14},{12,0},{14,2},{4,8},{6,10},{8,4},{10,6},{1,13},{3,15... | collective-permute-start | bytes 786440 | tf_op jit(solution)/shard_map/ppermute | solution.py:281
  163.4 23.7 %collective-permute-start.18 = (bf16[2,64,4096]{2,1,0:T(8,128)(2,1)S(1)}, bf16[2,64,4096]{2,1,0:T(8,128)(2,1)S(1)}, u32[]{:S(2)}, u32[]{:S(2)}) collective-permute-start(bf16[2,64,4096]{2,1,0:T(8,128)(2,1)S(1)} %collective-permute-done.16), channel_id=1, source_target_pairs={{4,0},{6,2},{8,12},{10,14},{5,1},{7,3},{9,13},{11,15},{20,16},{22,... | collective-permute-start | bytes 3145736 | tf_op jit(solution)/shard_map/ppermute | solution.py:281
  166.2 32.6 %collective-permute-start.23 = (bf16[64,2048]{1,0:T(8,128)(2,1)S(1)}, bf16[64,2048]{1,0:T(8,128)(2,1)S(1)}, u32[]{:S(2)}, u32[]{:S(2)}) collective-permute-start(bf16[64,2048]{1,0:T(8,128)(2,1)S(1)} %get-tuple-element.389), channel_id=1, source_target_pairs={{0,4},{2,6},{4,0},{6,2},{8,12},{10,14},{12,8},{14,10},{1,5},{3,7},... | collective-permute-start | bytes 786440 | tf_op jit(solution)/shard_map/ppermute | solution.py:281
  187.1 9.4 %collective-permute-start.24 = (bf16[128,2048]{1,0:T(8,128)(2,1)S(1)}, bf16[128,2048]{1,0:T(8,128)(2,1)S(1)}, u32[]{:S(2)}, u32[]{:S(2)}) collective-permute-start(bf16[128,2048]{1,0:T(8,128)(2,1)S(1)} %get-tuple-element.200), channel_id=1, source_target_pairs={{0,2},{2,0},{4,6},{6,4},{8,10},{10,8},{12,14},{14,12},{1,3},{3,1},... | collective-permute-start | bytes 1572872 | tf_op jit(solution)/shard_map/ppermute | solution.py:281
  187.7 20.0 %collective-permute-start.28 = (bf16[64,4096]{1,0:T(8,128)(2,1)S(1)}, bf16[64,4096]{1,0:T(8,128)(2,1)S(1)}, u32[]{:S(2)}, u32[]{:S(2)}) collective-permute-start(bf16[64,4096]{1,0:T(8,128)(2,1)S(1)} %get-tuple-element.362), channel_id=1, source_target_pairs={{0,2},{2,0},{4,6},{6,4},{8,10},{10,8},{12,14},{14,12},{1,3},{3,1},... | collective-permute-start | bytes 1572872 | tf_op jit(solution)/shard_map/ppermute | solution.py:281
  196.4 16.5 %collective-permute-start.22 = (bf16[64,2048]{1,0:T(8,128)(2,1)S(1)}, bf16[64,2048]{1,0:T(8,128)(2,1)S(1)}, u32[]{:S(2)}, u32[]{:S(2)}) collective-permute-start(bf16[64,2048]{1,0:T(8,128)(2,1)S(1)} %get-tuple-element.387), channel_id=1, source_target_pairs={{0,4},{2,6},{4,0},{6,2},{8,12},{10,14},{12,8},{14,10},{1,5},{3,7},... | collective-permute-start | bytes 786440 | tf_op jit(solution)/shard_map/ppermute | solution.py:281
  199.7 13.2 %collective-permute-start.26 = (bf16[64,2048]{1,0:T(8,128)(2,1)S(1)}, bf16[64,2048]{1,0:T(8,128)(2,1)S(1)}, u32[]{:S(2)}, u32[]{:S(2)}) collective-permute-start(bf16[64,2048]{1,0:T(8,128)(2,1)S(1)} %get-tuple-element.215), channel_id=1, source_target_pairs={{0,4},{2,6},{4,0},{6,2},{8,12},{10,14},{12,8},{14,10},{1,5},{3,7},... | collective-permute-start | bytes 786440 | tf_op jit(solution)/shard_map/ppermute | solution.py:281
  199.7 16.0 %collective-permute-start.29 = (bf16[64,2048]{1,0:T(8,128)(2,1)S(1)}, bf16[64,2048]{1,0:T(8,128)(2,1)S(1)}, u32[]{:S(2)}, u32[]{:S(2)}) collective-permute-start(bf16[64,2048]{1,0:T(8,128)(2,1)S(1)} %get-tuple-element.385), channel_id=1, source_target_pairs={{0,4},{2,6},{4,0},{6,2},{8,12},{10,14},{12,8},{14,10},{1,5},{3,7},... | collective-permute-start | bytes 786440 | tf_op jit(solution)/shard_map/ppermute | solution.py:281
  207.9 14.5 %collective-permute-start.30 = (bf16[256,4096]{1,0:T(8,128)(2,1)S(1)}, bf16[256,4096]{1,0:T(8,128)(2,1)S(1)}, u32[]{:S(2)}, u32[]{:S(2)}) collective-permute-start(bf16[256,4096]{1,0:T(8,128)(2,1)S(1)} %constant_dynamic-update-slice_fusion.8.own_ref.refs_3_), channel_id=1, source_target_pairs={{0,1},{1,0},{2,3},{3,2},{4,5},{5,4},{6,7},{7,6},{8,9},{9,8},{10,11... | collective-permute-start | bytes 6291464 | tf_op jit(solution)/shard_map/ppermute | solution.py:292
  213.1 9.2 %collective-permute-start.31 = (bf16[64,2048]{1,0:T(8,128)(2,1)S(1)}, bf16[64,2048]{1,0:T(8,128)(2,1)S(1)}, u32[]{:S(2)}, u32[]{:S(2)}) collective-permute-start(bf16[64,2048]{1,0:T(8,128)(2,1)S(1)} %get-tuple-element.223), channel_id=1, source_target_pairs={{0,4},{2,6},{4,0},{6,2},{8,12},{10,14},{12,8},{14,10},{1,5},{3,7},... | collective-permute-start | bytes 786440 | tf_op jit(solution)/shard_map/ppermute | solution.py:281
  215.4 22.2 %collective-permute-start.34 = (bf16[128,2048]{1,0:T(8,128)(2,1)S(1)}, bf16[128,2048]{1,0:T(8,128)(2,1)S(1)}, u32[]{:S(2)}, u32[]{:S(2)}) collective-permute-start(bf16[128,2048]{1,0:T(8,128)(2,1)S(1)} %pad_maximum_fusion.14.upper_ref.refs_6_), channel_id=1, source_target_pairs={{0,2},{2,0},{4,6},{6,4},{8,10},{10,8},{12,14},{14,12},{1,3},{3,1},... | collective-permute-start | bytes 1572872 | tf_op jit(solution)/shard_map/ppermute | solution.py:281
  254.3 17.1 %collective-permute-start.36 = (bf16[256,4096]{1,0:T(8,128)(2,1)S(1)}, bf16[256,4096]{1,0:T(8,128)(2,1)S(1)}, u32[]{:S(2)}, u32[]{:S(2)}) collective-permute-start(bf16[256,4096]{1,0:T(8,128)(2,1)S(1)} %get-tuple-element.232), channel_id=1, source_target_pairs={{0,1},{1,0},{2,3},{3,2},{4,5},{5,4},{6,7},{7,6},{8,9},{9,8},{10,11... | collective-permute-start | bytes 6291464 | tf_op jit(solution)/shard_map/ppermute | solution.py:292
  256.4 7.9 %collective-permute-start.33 = (bf16[64,2048]{1,0:T(8,128)(2,1)S(1)}, bf16[64,2048]{1,0:T(8,128)(2,1)S(1)}, u32[]{:S(2)}, u32[]{:S(2)}) collective-permute-start(bf16[64,2048]{1,0:T(8,128)(2,1)S(1)} %get-tuple-element.233), channel_id=1, source_target_pairs={{0,4},{2,6},{4,0},{6,2},{8,12},{10,14},{12,8},{14,10},{1,5},{3,7},... | collective-permute-start | bytes 786440 | tf_op jit(solution)/shard_map/ppermute | solution.py:281
  258.0 13.2 %collective-permute-start.32 = (bf16[128,2048]{1,0:T(8,128)(2,1)S(1)}, bf16[128,2048]{1,0:T(8,128)(2,1)S(1)}, u32[]{:S(2)}, u32[]{:S(2)}) collective-permute-start(bf16[128,2048]{1,0:T(8,128)(2,1)S(1)} %get-tuple-element.228), channel_id=1, source_target_pairs={{0,2},{2,0},{4,6},{6,4},{8,10},{10,8},{12,14},{14,12},{1,3},{3,1},... | collective-permute-start | bytes 1572872 | tf_op jit(solution)/shard_map/ppermute | solution.py:281
  258.3 13.9 %collective-permute-start.37 = (bf16[64,2048]{1,0:T(8,128)(2,1)S(1)}, bf16[64,2048]{1,0:T(8,128)(2,1)S(1)}, u32[]{:S(2)}, u32[]{:S(2)}) collective-permute-start(bf16[64,2048]{1,0:T(8,128)(2,1)S(1)} %get-tuple-element.384), channel_id=1, source_target_pairs={{0,12},{2,14},{12,0},{14,2},{4,8},{6,10},{8,4},{10,6},{1,13},{3,15... | collective-permute-start | bytes 786440 | tf_op jit(solution)/shard_map/ppermute | solution.py:281
  259.5 71.9 %collective-permute-start.45 = (bf16[128,2048]{1,0:T(8,128)(2,1)S(1)}, bf16[128,2048]{1,0:T(8,128)(2,1)S(1)}, u32[]{:S(2)}, u32[]{:S(2)}) collective-permute-start(bf16[128,2048]{1,0:T(8,128)(2,1)S(1)} %constant_dynamic-update-slice_fusion.12.upper_ref.refs_4_), channel_id=1, source_target_pairs={{0,2},{2,0},{4,6},{6,4},{8,10},{10,8},{12,14},{14,12},{1,3},{3,1},... | collective-permute-start | bytes 1572872 | tf_op jit(solution)/shard_map/ppermute | solution.py:281
  271.3 5.9 %collective-permute-start.35 = (bf16[64,2048]{1,0:T(8,128)(2,1)S(1)}, bf16[64,2048]{1,0:T(8,128)(2,1)S(1)}, u32[]{:S(2)}, u32[]{:S(2)}) collective-permute-start(bf16[64,2048]{1,0:T(8,128)(2,1)S(1)} %get-tuple-element.379), channel_id=1, source_target_pairs={{0,4},{2,6},{4,0},{6,2},{8,12},{10,14},{12,8},{14,10},{1,5},{3,7},... | collective-permute-start | bytes 786440 | tf_op jit(solution)/shard_map/ppermute | solution.py:281
  278.3 74.0 %collective-permute-start.38 = (bf16[64,2048]{1,0:T(8,128)(2,1)}, bf16[64,2048]{1,0:T(8,128)(2,1)}, u32[]{:S(2)}, u32[]{:S(2)}) collective-permute-start(bf16[64,2048]{1,0:T(8,128)(2,1)} %get-tuple-element.242), channel_id=1, source_target_pairs={{0,12},{2,14},{12,0},{14,2},{4,8},{6,10},{8,4},{10,6},{1,13},{3,15... | collective-permute-start | bytes 786440 | tf_op jit(solution)/shard_map/ppermute | solution.py:281
  279.6 11.6 %collective-permute-start.39 = (bf16[64,4096]{1,0:T(8,128)(2,1)S(1)}, bf16[64,4096]{1,0:T(8,128)(2,1)S(1)}, u32[]{:S(2)}, u32[]{:S(2)}) collective-permute-start(bf16[64,4096]{1,0:T(8,128)(2,1)S(1)} %get-tuple-element.341), channel_id=1, source_target_pairs={{0,2},{2,0},{4,6},{6,4},{8,10},{10,8},{12,14},{14,12},{1,3},{3,1},... | collective-permute-start | bytes 1572872 | tf_op jit(solution)/shard_map/ppermute | solution.py:281
  283.7 18.8 %collective-permute-start.43 = (bf16[128,2048]{1,0:T(8,128)(2,1)S(1)}, bf16[128,2048]{1,0:T(8,128)(2,1)S(1)}, u32[]{:S(2)}, u32[]{:S(2)}) collective-permute-start(bf16[128,2048]{1,0:T(8,128)(2,1)S(1)} %pad_maximum_fusion.16.upper_ref.refs_10_), channel_id=1, source_target_pairs={{0,2},{2,0},{4,6},{6,4},{8,10},{10,8},{12,14},{14,12},{1,3},{3,1},... | collective-permute-start | bytes 1572872 | tf_op jit(solution)/shard_map/ppermute | solution.py:281
  284.0 41.5 %collective-permute-start.42 = (bf16[64,4096]{1,0:T(8,128)(2,1)S(1)}, bf16[64,4096]{1,0:T(8,128)(2,1)S(1)}, u32[]{:S(2)}, u32[]{:S(2)}) collective-permute-start(bf16[64,4096]{1,0:T(8,128)(2,1)S(1)} %get-tuple-element.245), channel_id=1, source_target_pairs={{0,2},{2,0},{4,6},{6,4},{8,10},{10,8},{12,14},{14,12},{1,3},{3,1},... | collective-permute-start | bytes 1572872 | tf_op jit(solution)/shard_map/ppermute | solution.py:281
  291.6 35.2 %collective-permute-start.41 = (bf16[2,64,4096]{2,1,0:T(8,128)(2,1)S(1)}, bf16[2,64,4096]{2,1,0:T(8,128)(2,1)S(1)}, u32[]{:S(2)}, u32[]{:S(2)}) collective-permute-start(bf16[2,64,4096]{2,1,0:T(8,128)(2,1)S(1)} %pad_maximum_fusion.5), channel_id=1, source_target_pairs={{0,4},{2,6},{12,8},{14,10},{1,5},{3,7},{13,9},{15,11},{16,20},{18,... | collective-permute-start | bytes 3145736 | tf_op jit(solution)/shard_map/ppermute | solution.py:281
  318.8 10.5 %collective-permute-start.46 = (bf16[256,4096]{1,0:T(8,128)(2,1)S(1)}, bf16[256,4096]{1,0:T(8,128)(2,1)S(1)}, u32[]{:S(2)}, u32[]{:S(2)}) collective-permute-start(bf16[256,4096]{1,0:T(8,128)(2,1)S(1)} %get-tuple-element.251), channel_id=1, source_target_pairs={{0,1},{1,0},{2,3},{3,2},{4,5},{5,4},{6,7},{7,6},{8,9},{9,8},{10,11... | collective-permute-start | bytes 6291464 | tf_op jit(solution)/shard_map/ppermute | solution.py:292
  328.0 25.6 %collective-permute-start.44 = (bf16[64,2048]{1,0:T(8,128)(2,1)}, bf16[64,2048]{1,0:T(8,128)(2,1)}, u32[]{:S(2)}, u32[]{:S(2)}) collective-permute-start(bf16[64,2048]{1,0:T(8,128)(2,1)} %get-tuple-element.256), channel_id=1, source_target_pairs={{0,12},{2,14},{12,0},{14,2},{4,8},{6,10},{8,4},{10,6},{1,13},{3,15... | collective-permute-start | bytes 786440 | tf_op jit(solution)/shard_map/ppermute | solution.py:281
  331.5 25.4 %collective-permute-start.48 = (bf16[64,4096]{1,0:T(8,128)(2,1)}, bf16[64,4096]{1,0:T(8,128)(2,1)}, u32[]{:S(2)}, u32[]{:S(2)}) collective-permute-start(bf16[64,4096]{1,0:T(8,128)(2,1)} %get-tuple-element.337), channel_id=1, source_target_pairs={{0,2},{2,0},{4,6},{6,4},{8,10},{10,8},{12,14},{14,12},{1,3},{3,1},... | collective-permute-start | bytes 1572872 | tf_op jit(solution)/shard_map/ppermute | solution.py:281
  350.4 9.7 %collective-permute-start.47 = (bf16[256,4096]{1,0:T(8,128)(2,1)}, bf16[256,4096]{1,0:T(8,128)(2,1)}, u32[]{:S(2)}, u32[]{:S(2)}) collective-permute-start(bf16[256,4096]{1,0:T(8,128)(2,1)} %get-tuple-element.262), channel_id=1, source_target_pairs={{0,1},{1,0},{2,3},{3,2},{4,5},{5,4},{6,7},{7,6},{8,9},{9,8},{10,11... | collective-permute-start | bytes 6291464 | tf_op jit(solution)/shard_map/ppermute | solution.py:292
  351.2 34.0 %collective-permute-start.49 = (bf16[128,2048]{1,0:T(8,128)(2,1)S(1)}, bf16[128,2048]{1,0:T(8,128)(2,1)S(1)}, u32[]{:S(2)}, u32[]{:S(2)}) collective-permute-start(bf16[128,2048]{1,0:T(8,128)(2,1)S(1)} %constant_dynamic-update-slice_fusion.14.upper_ref.refs_8_), channel_id=1, source_target_pairs={{0,2},{2,0},{4,6},{6,4},{8,10},{10,8},{12,14},{14,12},{1,3},{3,1},... | collective-permute-start | bytes 1572872 | tf_op jit(solution)/shard_map/ppermute | solution.py:281
  352.4 27.2 %collective-permute-start.50 = (bf16[2,64,4096]{2,1,0:T(8,128)(2,1)}, bf16[2,64,4096]{2,1,0:T(8,128)(2,1)S(1)}, u32[]{:S(2)}, u32[]{:S(2)}) collective-permute-start(bf16[2,64,4096]{2,1,0:T(8,128)(2,1)} %pad_maximum_fusion.6), channel_id=1, source_target_pairs={{0,4},{2,6},{12,8},{14,10},{1,5},{3,7},{13,9},{15,11},{16,20},{18,... | collective-permute-start | bytes 3145736 | tf_op jit(solution)/shard_map/ppermute | solution.py:281
  353.7 56.1 %collective-permute-start.55 = (bf16[2,64,4096]{2,1,0:T(8,128)(2,1)}, bf16[2,64,4096]{2,1,0:T(8,128)(2,1)}, u32[]{:S(2)}, u32[]{:S(2)}) collective-permute-start(bf16[2,64,4096]{2,1,0:T(8,128)(2,1)} %add_convert_fusion.11), channel_id=1, source_target_pairs={{4,8},{6,10},{8,4},{10,6},{5,9},{7,11},{9,5},{11,7},{20,24},{22,26... | collective-permute-start | bytes 3145736 | tf_op jit(solution)/shard_map/ppermute | solution.py:281
  358.6 55.6 %collective-permute-start.52 = (bf16[2,64,4096]{2,1,0:T(8,128)(2,1)S(1)}, bf16[2,64,4096]{2,1,0:T(8,128)(2,1)S(1)}, u32[]{:S(2)}, u32[]{:S(2)}) collective-permute-start(bf16[2,64,4096]{2,1,0:T(8,128)(2,1)S(1)} %pad_maximum_fusion.7), channel_id=1, source_target_pairs={{0,4},{2,6},{12,8},{14,10},{1,5},{3,7},{13,9},{15,11},{16,20},{18,... | collective-permute-start | bytes 3145736 | tf_op jit(solution)/shard_map/ppermute | solution.py:281
  380.8 62.6 %collective-permute-start.58 = (bf16[2,64,4096]{2,1,0:T(8,128)(2,1)}, bf16[2,64,4096]{2,1,0:T(8,128)(2,1)}, u32[]{:S(2)}, u32[]{:S(2)}) collective-permute-start(bf16[2,64,4096]{2,1,0:T(8,128)(2,1)} %add_convert_fusion.10), channel_id=1, source_target_pairs={{4,8},{6,10},{8,4},{10,6},{5,9},{7,11},{9,5},{11,7},{20,24},{22,26... | collective-permute-start | bytes 3145736 | tf_op jit(solution)/shard_map/ppermute | solution.py:281
  383.8 28.5 %collective-permute-start.53 = (bf16[64,4096]{1,0:T(8,128)(2,1)S(1)}, bf16[64,4096]{1,0:T(8,128)(2,1)S(1)}, u32[]{:S(2)}, u32[]{:S(2)}) collective-permute-start(bf16[64,4096]{1,0:T(8,128)(2,1)S(1)} %copy-done.18), channel_id=1, source_target_pairs={{0,2},{2,0},{4,6},{6,4},{8,10},{10,8},{12,14},{14,12},{1,3},{3,1},... | collective-permute-start | bytes 1572872 | tf_op jit(solution)/shard_map/ppermute | solution.py:281
  385.1 22.1 %collective-permute-start.54 = (bf16[64,4096]{1,0:T(8,128)(2,1)S(1)}, bf16[64,4096]{1,0:T(8,128)(2,1)S(1)}, u32[]{:S(2)}, u32[]{:S(2)}) collective-permute-start(bf16[64,4096]{1,0:T(8,128)(2,1)S(1)} %get-tuple-element.331), channel_id=1, source_target_pairs={{0,2},{2,0},{4,6},{6,4},{8,10},{10,8},{12,14},{14,12},{1,3},{3,1},... | collective-permute-start | bytes 1572872 | tf_op jit(solution)/shard_map/ppermute | solution.py:281
  407.3 10.4 %collective-permute-start.51 = (bf16[256,4096]{1,0:T(8,128)(2,1)S(1)}, bf16[256,4096]{1,0:T(8,128)(2,1)S(1)}, u32[]{:S(2)}, u32[]{:S(2)}) collective-permute-start(bf16[256,4096]{1,0:T(8,128)(2,1)S(1)} %get-tuple-element.273), channel_id=1, source_target_pairs={{0,1},{1,0},{2,3},{3,2},{4,5},{5,4},{6,7},{7,6},{8,9},{9,8},{10,11... | collective-permute-start | bytes 6291464 | tf_op jit(solution)/shard_map/ppermute | solution.py:292
  412.3 31.5 %collective-permute-start.57 = (bf16[2,64,4096]{2,1,0:T(8,128)(2,1)}, bf16[2,64,4096]{2,1,0:T(8,128)(2,1)}, u32[]{:S(2)}, u32[]{:S(2)}) collective-permute-start(bf16[2,64,4096]{2,1,0:T(8,128)(2,1)} %add_convert_fusion.9), channel_id=1, source_target_pairs={{0,4},{2,6},{4,0},{6,2},{8,12},{10,14},{12,8},{14,10},{1,5},{3,7},... | collective-permute-start | bytes 3145736 | tf_op jit(solution)/shard_map/ppermute | solution.py:281
  412.7 47.2 %collective-permute-start.61 = (bf16[2,64,4096]{2,1,0:T(8,128)(2,1)S(1)}, bf16[2,64,4096]{2,1,0:T(8,128)(2,1)}, u32[]{:S(2)}, u32[]{:S(2)}) collective-permute-start(bf16[2,64,4096]{2,1,0:T(8,128)(2,1)S(1)} %pad_maximum_fusion.9), channel_id=1, source_target_pairs={{0,4},{2,6},{12,8},{14,10},{1,5},{3,7},{13,9},{15,11},{16,20},{18,... | collective-permute-start | bytes 3145736 | tf_op jit(solution)/shard_map/ppermute | solution.py:281
  415.4 51.3 %collective-permute-start.62 = (bf16[2,64,4096]{2,1,0:T(8,128)(2,1)}, bf16[2,64,4096]{2,1,0:T(8,128)(2,1)}, u32[]{:S(2)}, u32[]{:S(2)}) collective-permute-start(bf16[2,64,4096]{2,1,0:T(8,128)(2,1)} %add_convert_fusion.8), channel_id=1, source_target_pairs={{4,8},{6,10},{8,4},{10,6},{5,9},{7,11},{9,5},{11,7},{20,24},{22,26... | collective-permute-start | bytes 3145736 | tf_op jit(solution)/shard_map/ppermute | solution.py:281
  419.6 22.4 %collective-permute-start.56 = (bf16[64,4096]{1,0:T(8,128)(2,1)S(1)}, bf16[64,4096]{1,0:T(8,128)(2,1)S(1)}, u32[]{:S(2)}, u32[]{:S(2)}) collective-permute-start(bf16[64,4096]{1,0:T(8,128)(2,1)S(1)} %copy-done.19), channel_id=1, source_target_pairs={{0,2},{2,0},{4,6},{6,4},{8,10},{10,8},{12,14},{14,12},{1,3},{3,1},... | collective-permute-start | bytes 1572872 | tf_op jit(solution)/shard_map/ppermute | solution.py:281
  441.9 56.5 %collective-permute-start.63 = (bf16[64,4096]{1,0:T(8,128)(2,1)}, bf16[64,4096]{1,0:T(8,128)(2,1)S(1)}, u32[]{:S(2)}, u32[]{:S(2)}) collective-permute-start(bf16[64,4096]{1,0:T(8,128)(2,1)} %get-tuple-element.285), channel_id=1, source_target_pairs={{0,2},{2,0},{4,6},{6,4},{8,10},{10,8},{12,14},{14,12},{1,3},{3,1},... | collective-permute-start | bytes 1572872 | tf_op jit(solution)/shard_map/ppermute | solution.py:281
  443.4 22.9 %collective-permute-start.60 = (bf16[64,4096]{1,0:T(8,128)(2,1)S(1)}, bf16[64,4096]{1,0:T(8,128)(2,1)S(1)}, u32[]{:S(2)}, u32[]{:S(2)}) collective-permute-start(bf16[64,4096]{1,0:T(8,128)(2,1)S(1)} %get-tuple-element.326), channel_id=1, source_target_pairs={{0,2},{2,0},{4,6},{6,4},{8,10},{10,8},{12,14},{14,12},{1,3},{3,1},... | collective-permute-start | bytes 1572872 | tf_op jit(solution)/shard_map/ppermute | solution.py:281
  468.2 30.6 %collective-permute-start.64 = (bf16[2,64,4096]{2,1,0:T(8,128)(2,1)S(1)}, bf16[2,64,4096]{2,1,0:T(8,128)(2,1)S(1)}, u32[]{:S(2)}, u32[]{:S(2)}) collective-permute-start(bf16[2,64,4096]{2,1,0:T(8,128)(2,1)S(1)} %add_convert_fusion.5), channel_id=1, source_target_pairs={{0,4},{2,6},{4,0},{6,2},{8,12},{10,14},{12,8},{14,10},{1,5},{3,7},... | collective-permute-start | bytes 3145736 | tf_op jit(solution)/shard_map/ppermute | solution.py:281
  470.6 28.2 %collective-permute-start.65 = (bf16[2,64,4096]{2,1,0:T(8,128)(2,1)S(1)}, bf16[2,64,4096]{2,1,0:T(8,128)(2,1)S(1)}, u32[]{:S(2)}, u32[]{:S(2)}) collective-permute-start(bf16[2,64,4096]{2,1,0:T(8,128)(2,1)S(1)} %add_convert_fusion.6), channel_id=1, source_target_pairs={{4,8},{6,10},{8,4},{10,6},{5,9},{7,11},{9,5},{11,7},{20,24},{22,26... | collective-permute-start | bytes 3145736 | tf_op jit(solution)/shard_map/ppermute | solution.py:281
  472.9 24.0 %collective-permute-start.59 = (bf16[2,64,4096]{2,1,0:T(8,128)(2,1)S(1)}, bf16[2,64,4096]{2,1,0:T(8,128)(2,1)S(1)}, u32[]{:S(2)}, u32[]{:S(2)}) collective-permute-start(bf16[2,64,4096]{2,1,0:T(8,128)(2,1)S(1)} %add_convert_fusion.7), channel_id=1, source_target_pairs={{0,1},{1,0},{2,3},{3,2},{4,5},{5,4},{6,7},{7,6},{8,9},{9,8},{10,11... | collective-permute-start | bytes 3145736 | tf_op jit(solution)/shard_map/ppermute | solution.py:292
  (24 other events, 256.7 us)

commit v3 on v2

--- a/solution.py
+++ b/solution.py
@@ -155,7 +155,7 @@
 def code_terms(core, upper, lower, decoder):
     kept, depth = upper.shape
     half = decoder.shape[0] // 2
-    strips = half // min(STRIP, half)
+    strips = half // min(DEEP, half)
     rows = 2 * kept
 
     def kernel(core_ref, upper_ref, lower_ref, decoder_ref, give_ref, keep_ref, grads):
@@ -191,12 +191,12 @@
         core,
         [upper, lower, decoder],
         [pl.BlockSpec((kept, depth), lambda i, c: (0, 0))] * 2
-        + [pl.BlockSpec((STRIP, depth), strip)],
+        + [pl.BlockSpec((DEEP, depth), strip)],
         2 * strips,
         [out, out],
         [
-            pl.BlockSpec((rows, STRIP), lambda i, c: (0, jnp.minimum(i, strips - 1))),
-            pl.BlockSpec((rows, STRIP), lambda i, c: (0, jnp.maximum(i - strips, 0))),
+            pl.BlockSpec((rows, DEEP), lambda i, c: (0, jnp.minimum(i, strips - 1))),
+            pl.BlockSpec((rows, DEEP), lambda i, c: (0, jnp.maximum(i - strips, 0))),
         ],
         [pltpu.VMEM((rows, depth), jnp.bfloat16)],
         4 * rows * half * depth,

time: 519 us -> 524 us (level)
  transfers between devices with their start and end apart: 67 -> 67, of which waited for: 27 -> 27; matrix products, arithmetic and copies ran while one was open for 9% -> 9% of each run, Pallas kernels for 30% -> 29%
where the time goes in v3:
time: 524 us; the launch traced here: 514 us
  waiting for transfers between devices  180 us (34%)
  Pallas kernels  176 us (34%)
  starting transfers between devices  93.9 us (18%)
  other arithmetic  32 us (6%)
  local copies, waits for them, and re-layouts  30.7 us (6%)
    ppermute x57, waiting for transfers between devices, feat(): return lax.ppermute(value, 'feat', perm)  177 us
    pallas_call x10, Pallas kernels, call(): pl.pallas_call(kernel, grid_spec=pltpu.PrefetchScalarGridSpec(num_scalar_...  176 us
    ppermute x57, starting transfers between devices, feat(): return lax.ppermute(value, 'feat', perm)  66.4 us
    ppermute x10, starting transfers between devices, other_core(): return lax.ppermute(value, 'pair', [(0, 1), (1, 0)])  27.4 us
    convert_element_type x16, other arithmetic, add(): sum((term.astype(jnp.float32) for term in terms)).astype(jnp.bfloat16)  16.8 us
    unnamed x55, local copies, waits for them, and re-layouts  14.4 us
  transfers between devices with their start and end apart: 67, of which 27 were waited for; matrix products, arithmetic and copies ran while one was open for 9% of the time, Pallas kernels for 29%

profile of v3, /device:TPU:9, one launch (start us, length us, event | category | flops | bytes accessed | tf_op | source)
XLA Modules:
  0.0 514.5 jit_solution(6062169542773227827)
XLA Ops:
  0.6 2.1 constant_dynamic-slice_fusion
  3.4 3.2 collective-permute-start.1
  6.7 6.9 %copy.13 = bf16[128,2,8192]{2,0,1:T(8,128)(2,1)} copy(bf16[128,2,8192]{2,1,0:T(2,128)(2,1)} %param.4) | data formatting | bytes 8388608 | tf_op jit(solution)/shard_map/optimization_barrier | solution.py:313
  15.0 14.4 %collective-permute-done.1 = bf16[2,64,4096]{2,1,0:T(8,128)(2,1)} collective-permute-done((bf16[2,64,4096]{2,1,0:T(8,128)(2,1)S(1)}, bf16[2,64,4096]{2,1,0:T(8,128)(2,1)}, u32[]{:S(2)}, u32[]{:S(2)}) %collective-permute-start.1) | collective-permute-done | bytes 1048608 | tf_op jit(solution)/shard_map/ppermute | solution.py:281
  31.9 2.1 collective-permute-start.2
  34.0 2.1 collective-permute-start.7
  39.6 18.3 %collective-permute-done.7 = bf16[2,64,4096]{2,1,0:T(8,128)(2,1)S(1)} collective-permute-done((bf16[2,64,4096]{2,1,0:T(8,128)(2,1)S(1)}, bf16[2,64,4096]{2,1,0:T(8,128)(2,1)S(1)}, u32[]{:S(2)}, u32[]{:S(2)}) %collective-permute-start.7) | collective-permute-done | bytes 1048608 | tf_op jit(solution)/shard_map/ppermute | solution.py:281
  63.5 3.5 collective-permute-start.8
  67.1 1.5 collective-permute-start.12
  71.0 15.7 %shard_map.67 = (bf16[128,2048]{1,0:T(8,128)(2,1)S(1)}, bf16[128,2048]{1,0:T(8,128)(2,1)S(1)}) custom-call(s32[1]{0:T(128)} %bitcast.core_ref.side_ref, bf16[256,4096]{1,0:T(8,128)(2,1)} %constant_dynamic-update-slice_fusion.own_ref.refs_0_, bf16[256,4096]{1,0:T(8,128)(2,1)S(1)} %collective-permute-done.8.other_ref.refs_0_, bf16[8192,2048]{1,0:T(8,128)(2,1)} %decoder_ref.15), custom_call_target="tpu_custom_call" | custom-call | flops 8589934592 | bytes 33554432 | tf_op jit(solution)/shard_map/pallas_call | solution.py:83
  86.7 4.7 collective-permute-done.12
  93.0 3.1 collective-permute-start.11
  96.3 8.2 %collective-permute-done.14 = bf16[64,4096]{1,0:T(8,128)(2,1)S(1)} collective-permute-done((bf16[64,4096]{1,0:T(8,128)(2,1)S(1)}, bf16[64,4096]{1,0:T(8,128)(2,1)S(1)}, u32[]{:S(2)}, u32[]{:S(2)}) %collective-permute-start.14) | collective-permute-done | bytes 524320 | tf_op jit(solution)/shard_map/ppermute | solution.py:281
  104.7 1.7 collective-permute-start.17
  106.4 12.1 %collective-permute-done.11 = bf16[2,64,4096]{2,1,0:T(8,128)(2,1)S(1)} collective-permute-done((bf16[2,64,4096]{2,1,0:T(8,128)(2,1)S(1)}, bf16[2,64,4096]{2,1,0:T(8,128)(2,1)S(1)}, u32[]{:S(2)}, u32[]{:S(2)}) %collective-permute-start.11) | collective-permute-done | bytes 1048608 | tf_op jit(solution)/shard_map/ppermute | solution.py:281
  119.6 2.1 collective-permute-start.16
  121.7 1.6 collective-permute-start.15
  124.3 15.2 %shard_map.68 = (bf16[128,2048]{1,0:T(8,128)(2,1)S(1)}, bf16[128,2048]{1,0:T(8,128)(2,1)S(1)}) custom-call(s32[1]{0:T(128)} %bitcast.core_ref.side_ref, bf16[256,4096]{1,0:T(8,128)(2,1)S(1)} %constant_dynamic-update-slice_fusion.2.own_ref.refs_1_, bf16[256,4096]{1,0:T(8,128)(2,1)S(1)} %collective-permute-done.17.other_ref.refs_1_, ...), custom_call_target="tpu_custom_call" | custom-call | flops 8589934592 | bytes 33554432 | tf_op jit(solution)/shard_map/pallas_call | solution.py:83
  139.5 4.3 collective-permute-done.16
  146.2 3.5 collective-permute-start.20
  152.8 10.4 %collective-permute-done.21 = bf16[128,2048]{1,0:T(8,128)(2,1)S(1)} collective-permute-done((bf16[128,2048]{1,0:T(8,128)(2,1)S(1)}, bf16[128,2048]{1,0:T(8,128)(2,1)S(1)}, u32[]{:S(2)}, u32[]{:S(2)}) %collective-permute-start.21) | collective-permute-done | bytes 524320 | tf_op jit(solution)/shard_map/ppermute | solution.py:281
  163.3 2.7 collective-permute-start.18
  166.3 15.1 %shard_map.69 = (bf16[128,2048]{1,0:T(8,128)(2,1)S(1)}, bf16[128,2048]{1,0:T(8,128)(2,1)S(1)}) custom-call(s32[1]{0:T(128)} %bitcast.core_ref.side_ref, bf16[256,4096]{1,0:T(8,128)(2,1)S(1)} %constant_dynamic-update-slice_fusion.6.own_ref.refs_2_, bf16[256,4096]{1,0:T(8,128)(2,1)S(1)} %collective-permute-done.20.other_ref.refs_2_, ...), custom_call_target="tpu_custom_call" | custom-call | flops 8589934592 | bytes 33554432 | tf_op jit(solution)/shard_map/pallas_call | solution.py:83
  181.4 5.7 %collective-permute-done.18 = bf16[2,64,4096]{2,1,0:T(8,128)(2,1)S(1)} collective-permute-done((bf16[2,64,4096]{2,1,0:T(8,128)(2,1)S(1)}, bf16[2,64,4096]{2,1,0:T(8,128)(2,1)S(1)}, u32[]{:S(2)}, u32[]{:S(2)}) %collective-permute-start.18) | collective-permute-done | bytes 1048608 | tf_op jit(solution)/shard_map/ppermute | solution.py:281
  189.2 7.3 %collective-permute-done.24 = bf16[128,2048]{1,0:T(8,128)(2,1)S(1)} collective-permute-done((bf16[128,2048]{1,0:T(8,128)(2,1)S(1)}, bf16[128,2048]{1,0:T(8,128)(2,1)S(1)}, u32[]{:S(2)}, u32[]{:S(2)}) %collective-permute-start.24) | collective-permute-done | bytes 524320 | tf_op jit(solution)/shard_map/ppermute | solution.py:281
  196.4 2.2 collective-permute-start.22
  201.6 6.1 %collective-permute-done.28 = bf16[64,4096]{1,0:T(8,128)(2,1)S(1)} collective-permute-done((bf16[64,4096]{1,0:T(8,128)(2,1)S(1)}, bf16[64,4096]{1,0:T(8,128)(2,1)S(1)}, u32[]{:S(2)}, u32[]{:S(2)}) %collective-permute-start.28) | collective-permute-done | bytes 524320 | tf_op jit(solution)/shard_map/ppermute | solution.py:281
  207.9 5.0 collective-permute-start.30
  213.1 2.3 collective-permute-start.31
  216.5 5.8 %collective-permute-done.31 = bf16[64,2048]{1,0:T(8,128)(2,1)S(1)} collective-permute-done((bf16[64,2048]{1,0:T(8,128)(2,1)S(1)}, bf16[64,2048]{1,0:T(8,128)(2,1)S(1)}, u32[]{:S(2)}, u32[]{:S(2)}) %collective-permute-start.31) | collective-permute-done | bytes 262176 | tf_op jit(solution)/shard_map/ppermute | solution.py:281
  222.4 15.2 %shard_map.70 = (bf16[128,2048]{1,0:T(8,128)(2,1)S(1)}, bf16[128,2048]{1,0:T(8,128)(2,1)S(1)}) custom-call(s32[1]{0:T(128)} %bitcast.core_ref.side_ref, bf16[256,4096]{1,0:T(8,128)(2,1)S(1)} %constant_dynamic-update-slice_fusion.8.own_ref.refs_3_, bf16[256,4096]{1,0:T(8,128)(2,1)S(1)} %collective-permute-done.30.other_ref.refs_3_, ...), custom_call_target="tpu_custom_call" | custom-call | flops 8589934592 | bytes 33554432 | tf_op jit(solution)/shard_map/pallas_call | solution.py:83
  237.6 24.9 %shard_map.71 = (bf16[256,4096]{1,0:T(8,128)(2,1)S(1)}, bf16[256,4096]{1,0:T(8,128)(2,1)S(1)}) custom-call(s32[1]{0:T(128)} %bitcast.core_ref.side_ref, bf16[128,2048]{1,0:T(8,128)(2,1)S(1)} %pad_maximum_fusion.14.upper_ref.refs_6_, bf16[128,2048]{1,0:T(8,128)(2,1)S(1)} %collective-permute-done.34.lower_ref.refs_7_, bf16[8192,2048]{1,0:T(8,128)(2,1)} %decoder_ref.15), custom_call_target="tpu_custom_call" | custom-call | flops 8589934592 | bytes 33554432 | tf_op jit(solution)/shard_map/pallas_call | solution.py:83
  262.6 2.0 collective-permute-start.36
  264.6 1.5 collective-permute-start.33
  269.0 3.6 collective-permute-done.33
  272.6 6.8 %collective-permute-done.32 = bf16[128,2048]{1,0:T(8,128)(2,1)S(1)} collective-permute-done((bf16[128,2048]{1,0:T(8,128)(2,1)S(1)}, bf16[128,2048]{1,0:T(8,128)(2,1)S(1)}, u32[]{:S(2)}, u32[]{:S(2)}) %collective-permute-start.32) | collective-permute-done | bytes 524320 | tf_op jit(solution)/shard_map/ppermute | solution.py:281
  280.4 5.0 collective-permute-done.35
  288.1 3.7 collective-permute-done.40
  293.4 6.1 %collective-permute-done.39 = bf16[64,4096]{1,0:T(8,128)(2,1)S(1)} collective-permute-done((bf16[64,4096]{1,0:T(8,128)(2,1)S(1)}, bf16[64,4096]{1,0:T(8,128)(2,1)S(1)}, u32[]{:S(2)}, u32[]{:S(2)}) %collective-permute-start.39) | collective-permute-done | bytes 524320 | tf_op jit(solution)/shard_map/ppermute | solution.py:281
  301.1 9.6 %collective-permute-done.43.lower_ref.refs_11_ = bf16[128,2048]{1,0:T(8,128)(2,1)S(1)} collective-permute-done((bf16[128,2048]{1,0:T(8,128)(2,1)S(1)}, bf16[128,2048]{1,0:T(8,128)(2,1)S(1)}, u32[]{:S(2)}, u32[]{:S(2)}) %collective-permute-start.43) | collective-permute-done | bytes 524320 | tf_op jit(solution)/shard_map/ppermute | solution.py:281
  310.7 14.8 %shard_map.72 = (bf16[256,4096]{1,0:T(8,128)(2,1)S(1)}, bf16[256,4096]{1,0:T(8,128)(2,1)S(1)}) custom-call(s32[1]{0:T(128)} %bitcast.core_ref.side_ref, bf16[128,2048]{1,0:T(8,128)(2,1)S(1)} %pad_maximum_fusion.16.upper_ref.refs_10_, bf16[128,2048]{1,0:T(8,128)(2,1)S(1)} %collective-permute-done.43.lower_ref.refs_11_, bf16[8192,2048]{1,0:T(8,128)(2,1)} %decoder_ref.15), custom_call_target="tpu_custom_call" | custom-call | flops 8589934592 | bytes 33554432 | tf_op jit(solution)/shard_map/pallas_call | solution.py:83
  325.5 6.7 %collective-permute-start.46 = (bf16[256,4096]{1,0:T(8,128)(2,1)S(1)}, bf16[256,4096]{1,0:T(8,128)(2,1)S(1)}, u32[]{:S(2)}, u32[]{:S(2)}) collective-permute-start(bf16[256,4096]{1,0:T(8,128)(2,1)S(1)} %get-tuple-element.251), channel_id=1, source_target_pairs={{0,1},{1,0},{2,3},{3,2},{4,5},{5,4},{6,7},{7,6},{8,9},{9,8},{10,11... | collective-permute-start | bytes 6291464 | tf_op jit(solution)/shard_map/ppermute | solution.py:292
  338.4 15.8 %shard_map.73 = (bf16[256,4096]{1,0:T(8,128)(2,1)}, bf16[256,4096]{1,0:T(8,128)(2,1)S(1)}) custom-call(s32[1]{0:T(128)} %bitcast.core_ref.side_ref, bf16[128,2048]{1,0:T(8,128)(2,1)S(1)} %constant_dynamic-update-slice_fusion.12.upper_ref.refs_4_, bf16[128,2048]{1,0:T(8,128)(2,1)S(1)} %collective-permute-done.45.lower_ref.refs_5_, bf16[8192,2048]{1,0:T(8,128)(2,1)} %decoder_ref.15), custom_call_target="tpu_custom_call" | custom-call | flops 8589934592 | bytes 33554432 | tf_op jit(solution)/shard_map/pallas_call | solution.py:83
  358.7 2.1 collective-permute-start.55
  362.0 1.6 select_bitcast_fusion.13
  365.1 2.4 add_convert_fusion.1
  367.5 17.2 %collective-permute-done.50 = bf16[2,64,4096]{2,1,0:T(8,128)(2,1)S(1)} collective-permute-done((bf16[2,64,4096]{2,1,0:T(8,128)(2,1)}, bf16[2,64,4096]{2,1,0:T(8,128)(2,1)S(1)}, u32[]{:S(2)}, u32[]{:S(2)}) %collective-permute-start.50) | collective-permute-done | bytes 1048608 | tf_op jit(solution)/shard_map/ppermute | solution.py:281
  385.9 3.0 collective-permute-start.58
  391.4 15.0 %shard_map.74 = (bf16[256,4096]{1,0:T(8,128)(2,1)S(1)}, bf16[256,4096]{1,0:T(8,128)(2,1)S(1)}) custom-call(s32[1]{0:T(128)} %bitcast.core_ref.side_ref, bf16[128,2048]{1,0:T(8,128)(2,1)S(1)} %constant_dynamic-update-slice_fusion.14.upper_ref.refs_8_, bf16[128,2048]{1,0:T(8,128)(2,1)S(1)} %collective-permute-done.49.lower_ref.refs_9_, ...), custom_call_target="tpu_custom_call" | custom-call | flops 8589934592 | bytes 33554432 | tf_op jit(solution)/shard_map/pallas_call | solution.py:83
  406.4 6.0 %collective-permute-done.54 = bf16[64,4096]{1,0:T(8,128)(2,1)S(1)} collective-permute-done((bf16[64,4096]{1,0:T(8,128)(2,1)S(1)}, bf16[64,4096]{1,0:T(8,128)(2,1)S(1)}, u32[]{:S(2)}, u32[]{:S(2)}) %collective-permute-start.54) | collective-permute-done | bytes 524320 | tf_op jit(solution)/shard_map/ppermute | solution.py:281
  412.4 2.2 collective-permute-start.51
  414.9 2.5 add_convert_fusion.9
  420.3 2.3 collective-permute-start.62
  424.7 22.1 %shard_map.75.refs_12_ = bf16[8192,2048]{1,0:T(8,128)(2,1)} custom-call(s32[1]{0:T(128)} %bitcast.core_ref.side_ref, bf16[256,4096]{1,0:T(8,128)(2,1)} %constant_dynamic-update-slice_fusion.own_ref.refs_0_, bf16[256,4096]{1,0:T(8,128)(2,1)} %copy-done.5, bf16[256,4096]{1,0:T(8,128)(2,1)} %copy-done.4, bf16[256,4096]{1,0:T(8,128)(2,1)} %copy-done.6, ...), custom_call_target="tpu_custom_call" | custom-call | flops 17179869184 | bytes 25165824 | tf_op jit(solution)/shard_map/pallas_call | solution.py:83
  448.6 2.0 add_convert_fusion.7
  450.7 14.3 %collective-permute-done.61 = bf16[2,64,4096]{2,1,0:T(8,128)(2,1)} collective-permute-done((bf16[2,64,4096]{2,1,0:T(8,128)(2,1)S(1)}, bf16[2,64,4096]{2,1,0:T(8,128)(2,1)}, u32[]{:S(2)}, u32[]{:S(2)}) %collective-permute-start.61) | collective-permute-done | bytes 1048608 | tf_op jit(solution)/shard_map/ppermute | solution.py:281
  466.4 4.7 collective-permute-done.60
  471.5 1.5 add_convert_fusion.5
  473.0 2.5 collective-permute-start.64
  475.5 2.3 collective-permute-start.65
  477.8 2.0 collective-permute-start.59
  479.8 22.3 %shard_map.76 = bf16[8192,2048]{1,0:T(8,128)(2,1)} custom-call(s32[1]{0:T(128)S(6)} %sub.33.side_ref, bf16[256,4096]{1,0:T(8,128)(2,1)} %copy-done, bf16[256,4096]{1,0:T(8,128)(2,1)} %copy-done.1, bf16[256,4096]{1,0:T(8,128)(2,1)} %copy-done.2, bf16[256,4096]{1,0:T(8,128)(2,1)} %copy-done.3, ...), custom_call_target="tpu_custom_call", output_to_operand_aliasing={{}: (13, {})} | custom-call | flops 17179869184 | bytes 25165824 | tf_op jit(solution)/shard_map/pallas_call | solution.py:83
  504.5 2.0 copy.16
  507.7 6.4 %copy.17 = bf16[128,2,8192]{2,1,0:T(2,128)(2,1)} copy(bf16[128,2,8192]{2,0,1:T(8,128)(2,1)S(1)} %pad_maximum_fusion) | data formatting | bytes 8388608
  (242 shorter events, 71.2 us)
Async XLA Ops:
  3.4 26.0 %collective-permute-start.1 = (bf16[2,64,4096]{2,1,0:T(8,128)(2,1)S(1)}, bf16[2,64,4096]{2,1,0:T(8,128)(2,1)}, u32[]{:S(2)}, u32[]{:S(2)}) collective-permute-start(bf16[2,64,4096]{2,1,0:T(8,128)(2,1)S(1)} %bitcast.302), channel_id=1, source_target_pairs={{4,8},{6,10},{8,4},{10,6},{5,9},{7,11},{9,5},{11,7},{20,24},{22,26... | collective-permute-start | bytes 3145736 | tf_op jit(solution)/shard_map/ppermute | solution.py:281
  6.6 23.9 %collective-permute-start = (bf16[2,64,4096]{2,1,0:T(8,128)(2,1)S(1)}, bf16[2,64,4096]{2,1,0:T(8,128)(2,1)S(1)}, u32[]{:S(2)}, u32[]{:S(2)}) collective-permute-start(bf16[2,64,4096]{2,1,0:T(8,128)(2,1)S(1)} %bitcast.303), channel_id=1, source_target_pairs={{0,4},{2,6},{4,0},{6,2},{8,12},{10,14},{12,8},{14,10},{1,5},{3,7},... | collective-permute-start | bytes 3145736 | tf_op jit(solution)/shard_map/ppermute | solution.py:281
  30.5 8.9 %collective-permute-start.5 = (s32[128,2]{0,1:T(2,128)S(1)}, s32[128,2]{0,1:T(2,128)S(1)}, u32[]{:S(2)}, u32[]{:S(2)}) collective-permute-start(s32[128,2]{0,1:T(2,128)S(1)} %copy-done.20), channel_id=1, source_target_pairs={{0,8},{2,10},{8,0},{10,2},{4,12},{6,14},{12,4},{14,6},{1,9},{3,11}... | collective-permute-start | bytes 3080 | tf_op jit(solution)/shard_map/ppermute | solution.py:281
  31.4 8.1 %collective-permute-start.4 = (s32[128,2]{0,1:T(2,128)S(1)}, s32[128,2]{0,1:T(2,128)S(1)}, u32[]{:S(2)}, u32[]{:S(2)}) collective-permute-start(s32[128,2]{0,1:T(2,128)S(1)} %copy-done.20), channel_id=1, source_target_pairs={{0,12},{2,14},{12,0},{14,2},{4,8},{6,10},{8,4},{10,6},{1,13},{3,15... | collective-permute-start | bytes 3080 | tf_op jit(solution)/shard_map/ppermute | solution.py:281
  34.0 23.9 %collective-permute-start.7 = (bf16[2,64,4096]{2,1,0:T(8,128)(2,1)S(1)}, bf16[2,64,4096]{2,1,0:T(8,128)(2,1)S(1)}, u32[]{:S(2)}, u32[]{:S(2)}) collective-permute-start(bf16[2,64,4096]{2,1,0:T(8,128)(2,1)S(1)} %collective-permute-done), channel_id=1, source_target_pairs={{4,8},{6,10},{8,4},{10,6},{5,9},{7,11},{9,5},{11,7},{20,24},{22,26... | collective-permute-start | bytes 3145736 | tf_op jit(solution)/shard_map/ppermute | solution.py:281
  36.1 22.8 %collective-permute-start.6 = (bf16[2,64,4096]{2,1,0:T(8,128)(2,1)}, bf16[2,64,4096]{2,1,0:T(8,128)(2,1)S(1)}, u32[]{:S(2)}, u32[]{:S(2)}) collective-permute-start(bf16[2,64,4096]{2,1,0:T(8,128)(2,1)} %collective-permute-done.1), channel_id=1, source_target_pairs={{4,0},{6,2},{8,12},{10,14},{5,1},{7,3},{9,13},{11,15},{20,16},{22,... | collective-permute-start | bytes 3145736 | tf_op jit(solution)/shard_map/ppermute | solution.py:281
  38.1 23.3 %collective-permute-start.3 = (bf16[128,4096]{1,0:T(8,128)(2,1)S(1)}, bf16[128,4096]{1,0:T(8,128)(2,1)S(1)}, u32[]{:S(2)}, u32[]{:S(2)}) collective-permute-start(bf16[128,4096]{1,0:T(8,128)(2,1)S(1)} %pad_maximum_fusion.2), channel_id=1, source_target_pairs={{0,2},{2,0},{4,6},{6,4},{8,10},{10,8},{12,14},{14,12},{1,3},{3,1},... | collective-permute-start | bytes 3145736 | tf_op jit(solution)/shard_map/ppermute | solution.py:281
  63.5 7.5 %collective-permute-start.8 = (bf16[256,4096]{1,0:T(8,128)(2,1)}, bf16[256,4096]{1,0:T(8,128)(2,1)S(1)}, u32[]{:S(2)}, u32[]{:S(2)}) collective-permute-start(bf16[256,4096]{1,0:T(8,128)(2,1)} %constant_dynamic-update-slice_fusion.own_ref.refs_0_), channel_id=1, source_target_pairs={{0,1},{1,0},{2,3},{3,2},{4,5},{5,4},{6,7},{7,6},{8,9},{9,8},{10,11... | collective-permute-start | bytes 6291464 | tf_op jit(solution)/shard_map/ppermute | solution.py:292
  67.1 24.4 %collective-permute-start.12 = (bf16[2,64,4096]{2,1,0:T(8,128)(2,1)}, bf16[2,64,4096]{2,1,0:T(8,128)(2,1)S(1)}, u32[]{:S(2)}, u32[]{:S(2)}) collective-permute-start(bf16[2,64,4096]{2,1,0:T(8,128)(2,1)} %copy-done.16), channel_id=1, source_target_pairs={{4,0},{6,2},{8,12},{10,14},{5,1},{7,3},{9,13},{11,15},{20,16},{22,... | collective-permute-start | bytes 3145736 | tf_op jit(solution)/shard_map/ppermute | solution.py:281
  68.6 27.7 %collective-permute-start.13 = (bf16[64,4096]{1,0:T(8,128)(2,1)}, bf16[64,4096]{1,0:T(8,128)(2,1)S(1)}, u32[]{:S(2)}, u32[]{:S(2)}) collective-permute-start(bf16[64,4096]{1,0:T(8,128)(2,1)} %get-tuple-element.372), channel_id=1, source_target_pairs={{0,2},{2,0},{4,6},{6,4},{8,10},{10,8},{12,14},{14,12},{1,3},{3,1},... | collective-permute-start | bytes 1572872 | tf_op jit(solution)/shard_map/ppermute | solution.py:281
  91.7 12.7 %collective-permute-start.14 = (bf16[64,4096]{1,0:T(8,128)(2,1)S(1)}, bf16[64,4096]{1,0:T(8,128)(2,1)S(1)}, u32[]{:S(2)}, u32[]{:S(2)}) collective-permute-start(bf16[64,4096]{1,0:T(8,128)(2,1)S(1)} %get-tuple-element.369), channel_id=1, source_target_pairs={{0,2},{2,0},{4,6},{6,4},{8,10},{10,8},{12,14},{14,12},{1,3},{3,1},... | collective-permute-start | bytes 1572872 | tf_op jit(solution)/shard_map/ppermute | solution.py:281
  93.0 25.5 %collective-permute-start.11 = (bf16[2,64,4096]{2,1,0:T(8,128)(2,1)S(1)}, bf16[2,64,4096]{2,1,0:T(8,128)(2,1)S(1)}, u32[]{:S(2)}, u32[]{:S(2)}) collective-permute-start(bf16[2,64,4096]{2,1,0:T(8,128)(2,1)S(1)} %dynamic-slice_bitcast_fusion), channel_id=1, source_target_pairs={{4,8},{6,10},{8,4},{10,6},{5,9},{7,11},{9,5},{11,7},{20,24},{22,26... | collective-permute-start | bytes 3145736 | tf_op jit(solution)/shard_map/ppermute | solution.py:281
  96.2 23.4 %collective-permute-start.10 = (bf16[2,64,4096]{2,1,0:T(8,128)(2,1)S(1)}, bf16[2,64,4096]{2,1,0:T(8,128)(2,1)S(1)}, u32[]{:S(2)}, u32[]{:S(2)}) collective-permute-start(bf16[2,64,4096]{2,1,0:T(8,128)(2,1)S(1)} %dynamic-slice_bitcast_fusion), channel_id=1, source_target_pairs={{0,4},{2,6},{4,0},{6,2},{8,12},{10,14},{12,8},{14,10},{1,5},{3,7},... | collective-permute-start | bytes 3145736 | tf_op jit(solution)/shard_map/ppermute | solution.py:281
  104.7 19.6 %collective-permute-start.17 = (bf16[256,4096]{1,0:T(8,128)(2,1)S(1)}, bf16[256,4096]{1,0:T(8,128)(2,1)S(1)}, u32[]{:S(2)}, u32[]{:S(2)}) collective-permute-start(bf16[256,4096]{1,0:T(8,128)(2,1)S(1)} %constant_dynamic-update-slice_fusion.2.own_ref.refs_1_), channel_id=1, source_target_pairs={{0,1},{1,0},{2,3},{3,2},{4,5},{5,4},{6,7},{7,6},{8,9},{9,8},{10,11... | collective-permute-start | bytes 6291464 | tf_op jit(solution)/shard_map/ppermute | solution.py:292
  119.6 24.3 %collective-permute-start.16 = (bf16[2,64,4096]{2,1,0:T(8,128)(2,1)S(1)}, bf16[2,64,4096]{2,1,0:T(8,128)(2,1)S(1)}, u32[]{:S(2)}, u32[]{:S(2)}) collective-permute-start(bf16[2,64,4096]{2,1,0:T(8,128)(2,1)S(1)} %collective-permute-done.10), channel_id=1, source_target_pairs={{4,8},{6,10},{8,4},{10,6},{5,9},{7,11},{9,5},{11,7},{20,24},{22,26... | collective-permute-start | bytes 3145736 | tf_op jit(solution)/shard_map/ppermute | solution.py:281
  121.7 22.1 %collective-permute-start.15 = (bf16[2,64,4096]{2,1,0:T(8,128)(2,1)S(1)}, bf16[2,64,4096]{2,1,0:T(8,128)(2,1)S(1)}, u32[]{:S(2)}, u32[]{:S(2)}) collective-permute-start(bf16[2,64,4096]{2,1,0:T(8,128)(2,1)S(1)} %collective-permute-done.11), channel_id=1, source_target_pairs={{4,0},{6,2},{8,12},{10,14},{5,1},{7,3},{9,13},{11,15},{20,16},{22,... | collective-permute-start | bytes 3145736 | tf_op jit(solution)/shard_map/ppermute | solution.py:281
  123.8 22.2 %collective-permute-start.19 = (bf16[128,4096]{1,0:T(8,128)(2,1)S(1)}, bf16[128,4096]{1,0:T(8,128)(2,1)S(1)}, u32[]{:S(2)}, u32[]{:S(2)}) collective-permute-start(bf16[128,4096]{1,0:T(8,128)(2,1)S(1)} %pad_maximum_fusion.3), channel_id=1, source_target_pairs={{0,2},{2,0},{4,6},{6,4},{8,10},{10,8},{12,14},{14,12},{1,3},{3,1},... | collective-permute-start | bytes 3145736 | tf_op jit(solution)/shard_map/ppermute | solution.py:281
  146.2 20.0 %collective-permute-start.20 = (bf16[256,4096]{1,0:T(8,128)(2,1)S(1)}, bf16[256,4096]{1,0:T(8,128)(2,1)S(1)}, u32[]{:S(2)}, u32[]{:S(2)}) collective-permute-start(bf16[256,4096]{1,0:T(8,128)(2,1)S(1)} %constant_dynamic-update-slice_fusion.6.own_ref.refs_2_), channel_id=1, source_target_pairs={{0,1},{1,0},{2,3},{3,2},{4,5},{5,4},{6,7},{7,6},{8,9},{9,8},{10,11... | collective-permute-start | bytes 6291464 | tf_op jit(solution)/shard_map/ppermute | solution.py:292
  149.8 13.5 %collective-permute-start.21 = (bf16[128,2048]{1,0:T(8,128)(2,1)S(1)}, bf16[128,2048]{1,0:T(8,128)(2,1)S(1)}, u32[]{:S(2)}, u32[]{:S(2)}) collective-permute-start(bf16[128,2048]{1,0:T(8,128)(2,1)S(1)} %get-tuple-element.188), channel_id=1, source_target_pairs={{0,2},{2,0},{4,6},{6,4},{8,10},{10,8},{12,14},{14,12},{1,3},{3,1},... | collective-permute-start | bytes 1572872 | tf_op jit(solution)/shard_map/ppermute | solution.py:281
  150.0 37.7 %collective-permute-start.9 = (bf16[128,2048]{1,0:T(8,128)(2,1)S(1)}, bf16[128,2048]{1,0:T(8,128)(2,1)S(1)}, u32[]{:S(2)}, u32[]{:S(2)}) collective-permute-start(bf16[128,2048]{1,0:T(8,128)(2,1)S(1)} %get-tuple-element.171), channel_id=1, source_target_pairs={{0,2},{2,0},{4,6},{6,4},{8,10},{10,8},{12,14},{14,12},{1,3},{3,1},... | collective-permute-start | bytes 1572872 | tf_op jit(solution)/shard_map/ppermute | solution.py:281
  151.3 50.3 %collective-permute-start.27 = (bf16[64,4096]{1,0:T(8,128)(2,1)S(1)}, bf16[64,4096]{1,0:T(8,128)(2,1)S(1)}, u32[]{:S(2)}, u32[]{:S(2)}) collective-permute-start(bf16[64,4096]{1,0:T(8,128)(2,1)S(1)} %get-tuple-element.364), channel_id=1, source_target_pairs={{0,2},{2,0},{4,6},{6,4},{8,10},{10,8},{12,14},{14,12},{1,3},{3,1},... | collective-permute-start | bytes 1572872 | tf_op jit(solution)/shard_map/ppermute | solution.py:281
  151.6 47.2 %collective-permute-start.25 = (bf16[64,2048]{1,0:T(8,128)(2,1)S(1)}, bf16[64,2048]{1,0:T(8,128)(2,1)S(1)}, u32[]{:S(2)}, u32[]{:S(2)}) collective-permute-start(bf16[64,2048]{1,0:T(8,128)(2,1)S(1)} %get-tuple-element.392), channel_id=1, source_target_pairs={{0,12},{2,14},{12,0},{14,2},{4,8},{6,10},{8,4},{10,6},{1,13},{3,15... | collective-permute-start | bytes 786440 | tf_op jit(solution)/shard_map/ppermute | solution.py:281
  163.3 23.8 %collective-permute-start.18 = (bf16[2,64,4096]{2,1,0:T(8,128)(2,1)S(1)}, bf16[2,64,4096]{2,1,0:T(8,128)(2,1)S(1)}, u32[]{:S(2)}, u32[]{:S(2)}) collective-permute-start(bf16[2,64,4096]{2,1,0:T(8,128)(2,1)S(1)} %collective-permute-done.16), channel_id=1, source_target_pairs={{4,0},{6,2},{8,12},{10,14},{5,1},{7,3},{9,13},{11,15},{20,16},{22,... | collective-permute-start | bytes 3145736 | tf_op jit(solution)/shard_map/ppermute | solution.py:281
  166.2 32.6 %collective-permute-start.23 = (bf16[64,2048]{1,0:T(8,128)(2,1)S(1)}, bf16[64,2048]{1,0:T(8,128)(2,1)S(1)}, u32[]{:S(2)}, u32[]{:S(2)}) collective-permute-start(bf16[64,2048]{1,0:T(8,128)(2,1)S(1)} %get-tuple-element.389), channel_id=1, source_target_pairs={{0,4},{2,6},{4,0},{6,2},{8,12},{10,14},{12,8},{14,10},{1,5},{3,7},... | collective-permute-start | bytes 786440 | tf_op jit(solution)/shard_map/ppermute | solution.py:281
  187.1 9.4 %collective-permute-start.24 = (bf16[128,2048]{1,0:T(8,128)(2,1)S(1)}, bf16[128,2048]{1,0:T(8,128)(2,1)S(1)}, u32[]{:S(2)}, u32[]{:S(2)}) collective-permute-start(bf16[128,2048]{1,0:T(8,128)(2,1)S(1)} %get-tuple-element.200), channel_id=1, source_target_pairs={{0,2},{2,0},{4,6},{6,4},{8,10},{10,8},{12,14},{14,12},{1,3},{3,1},... | collective-permute-start | bytes 1572872 | tf_op jit(solution)/shard_map/ppermute | solution.py:281
  187.7 20.0 %collective-permute-start.28 = (bf16[64,4096]{1,0:T(8,128)(2,1)S(1)}, bf16[64,4096]{1,0:T(8,128)(2,1)S(1)}, u32[]{:S(2)}, u32[]{:S(2)}) collective-permute-start(bf16[64,4096]{1,0:T(8,128)(2,1)S(1)} %get-tuple-element.362), channel_id=1, source_target_pairs={{0,2},{2,0},{4,6},{6,4},{8,10},{10,8},{12,14},{14,12},{1,3},{3,1},... | collective-permute-start | bytes 1572872 | tf_op jit(solution)/shard_map/ppermute | solution.py:281
  196.4 16.5 %collective-permute-start.22 = (bf16[64,2048]{1,0:T(8,128)(2,1)S(1)}, bf16[64,2048]{1,0:T(8,128)(2,1)S(1)}, u32[]{:S(2)}, u32[]{:S(2)}) collective-permute-start(bf16[64,2048]{1,0:T(8,128)(2,1)S(1)} %get-tuple-element.387), channel_id=1, source_target_pairs={{0,4},{2,6},{4,0},{6,2},{8,12},{10,14},{12,8},{14,10},{1,5},{3,7},... | collective-permute-start | bytes 786440 | tf_op jit(solution)/shard_map/ppermute | solution.py:281
  199.7 13.2 %collective-permute-start.26 = (bf16[64,2048]{1,0:T(8,128)(2,1)S(1)}, bf16[64,2048]{1,0:T(8,128)(2,1)S(1)}, u32[]{:S(2)}, u32[]{:S(2)}) collective-permute-start(bf16[64,2048]{1,0:T(8,128)(2,1)S(1)} %get-tuple-element.215), channel_id=1, source_target_pairs={{0,4},{2,6},{4,0},{6,2},{8,12},{10,14},{12,8},{14,10},{1,5},{3,7},... | collective-permute-start | bytes 786440 | tf_op jit(solution)/shard_map/ppermute | solution.py:281
  199.7 16.0 %collective-permute-start.29 = (bf16[64,2048]{1,0:T(8,128)(2,1)S(1)}, bf16[64,2048]{1,0:T(8,128)(2,1)S(1)}, u32[]{:S(2)}, u32[]{:S(2)}) collective-permute-start(bf16[64,2048]{1,0:T(8,128)(2,1)S(1)} %get-tuple-element.385), channel_id=1, source_target_pairs={{0,4},{2,6},{4,0},{6,2},{8,12},{10,14},{12,8},{14,10},{1,5},{3,7},... | collective-permute-start | bytes 786440 | tf_op jit(solution)/shard_map/ppermute | solution.py:281
  207.9 14.5 %collective-permute-start.30 = (bf16[256,4096]{1,0:T(8,128)(2,1)S(1)}, bf16[256,4096]{1,0:T(8,128)(2,1)S(1)}, u32[]{:S(2)}, u32[]{:S(2)}) collective-permute-start(bf16[256,4096]{1,0:T(8,128)(2,1)S(1)} %constant_dynamic-update-slice_fusion.8.own_ref.refs_3_), channel_id=1, source_target_pairs={{0,1},{1,0},{2,3},{3,2},{4,5},{5,4},{6,7},{7,6},{8,9},{9,8},{10,11... | collective-permute-start | bytes 6291464 | tf_op jit(solution)/shard_map/ppermute | solution.py:292
  213.1 9.2 %collective-permute-start.31 = (bf16[64,2048]{1,0:T(8,128)(2,1)S(1)}, bf16[64,2048]{1,0:T(8,128)(2,1)S(1)}, u32[]{:S(2)}, u32[]{:S(2)}) collective-permute-start(bf16[64,2048]{1,0:T(8,128)(2,1)S(1)} %get-tuple-element.223), channel_id=1, source_target_pairs={{0,4},{2,6},{4,0},{6,2},{8,12},{10,14},{12,8},{14,10},{1,5},{3,7},... | collective-permute-start | bytes 786440 | tf_op jit(solution)/shard_map/ppermute | solution.py:281
  215.4 22.2 %collective-permute-start.34 = (bf16[128,2048]{1,0:T(8,128)(2,1)S(1)}, bf16[128,2048]{1,0:T(8,128)(2,1)S(1)}, u32[]{:S(2)}, u32[]{:S(2)}) collective-permute-start(bf16[128,2048]{1,0:T(8,128)(2,1)S(1)} %pad_maximum_fusion.14.upper_ref.refs_6_), channel_id=1, source_target_pairs={{0,2},{2,0},{4,6},{6,4},{8,10},{10,8},{12,14},{14,12},{1,3},{3,1},... | collective-permute-start | bytes 1572872 | tf_op jit(solution)/shard_map/ppermute | solution.py:281
  262.6 17.0 %collective-permute-start.36 = (bf16[256,4096]{1,0:T(8,128)(2,1)S(1)}, bf16[256,4096]{1,0:T(8,128)(2,1)S(1)}, u32[]{:S(2)}, u32[]{:S(2)}) collective-permute-start(bf16[256,4096]{1,0:T(8,128)(2,1)S(1)} %get-tuple-element.232), channel_id=1, source_target_pairs={{0,1},{1,0},{2,3},{3,2},{4,5},{5,4},{6,7},{7,6},{8,9},{9,8},{10,11... | collective-permute-start | bytes 6291464 | tf_op jit(solution)/shard_map/ppermute | solution.py:292
  264.6 7.9 %collective-permute-start.33 = (bf16[64,2048]{1,0:T(8,128)(2,1)S(1)}, bf16[64,2048]{1,0:T(8,128)(2,1)S(1)}, u32[]{:S(2)}, u32[]{:S(2)}) collective-permute-start(bf16[64,2048]{1,0:T(8,128)(2,1)S(1)} %get-tuple-element.233), channel_id=1, source_target_pairs={{0,4},{2,6},{4,0},{6,2},{8,12},{10,14},{12,8},{14,10},{1,5},{3,7},... | collective-permute-start | bytes 786440 | tf_op jit(solution)/shard_map/ppermute | solution.py:281
  266.2 13.2 %collective-permute-start.32 = (bf16[128,2048]{1,0:T(8,128)(2,1)S(1)}, bf16[128,2048]{1,0:T(8,128)(2,1)S(1)}, u32[]{:S(2)}, u32[]{:S(2)}) collective-permute-start(bf16[128,2048]{1,0:T(8,128)(2,1)S(1)} %get-tuple-element.228), channel_id=1, source_target_pairs={{0,2},{2,0},{4,6},{6,4},{8,10},{10,8},{12,14},{14,12},{1,3},{3,1},... | collective-permute-start | bytes 1572872 | tf_op jit(solution)/shard_map/ppermute | solution.py:281
  266.5 13.9 %collective-permute-start.37 = (bf16[64,2048]{1,0:T(8,128)(2,1)S(1)}, bf16[64,2048]{1,0:T(8,128)(2,1)S(1)}, u32[]{:S(2)}, u32[]{:S(2)}) collective-permute-start(bf16[64,2048]{1,0:T(8,128)(2,1)S(1)} %get-tuple-element.384), channel_id=1, source_target_pairs={{0,12},{2,14},{12,0},{14,2},{4,8},{6,10},{8,4},{10,6},{1,13},{3,15... | collective-permute-start | bytes 786440 | tf_op jit(solution)/shard_map/ppermute | solution.py:281
  267.7 70.4 %collective-permute-start.45 = (bf16[128,2048]{1,0:T(8,128)(2,1)S(1)}, bf16[128,2048]{1,0:T(8,128)(2,1)S(1)}, u32[]{:S(2)}, u32[]{:S(2)}) collective-permute-start(bf16[128,2048]{1,0:T(8,128)(2,1)S(1)} %constant_dynamic-update-slice_fusion.12.upper_ref.refs_4_), channel_id=1, source_target_pairs={{0,2},{2,0},{4,6},{6,4},{8,10},{10,8},{12,14},{14,12},{1,3},{3,1},... | collective-permute-start | bytes 1572872 | tf_op jit(solution)/shard_map/ppermute | solution.py:281
  279.5 5.9 %collective-permute-start.35 = (bf16[64,2048]{1,0:T(8,128)(2,1)S(1)}, bf16[64,2048]{1,0:T(8,128)(2,1)S(1)}, u32[]{:S(2)}, u32[]{:S(2)}) collective-permute-start(bf16[64,2048]{1,0:T(8,128)(2,1)S(1)} %get-tuple-element.379), channel_id=1, source_target_pairs={{0,4},{2,6},{4,0},{6,2},{8,12},{10,14},{12,8},{14,10},{1,5},{3,7},... | collective-permute-start | bytes 786440 | tf_op jit(solution)/shard_map/ppermute | solution.py:281
  286.6 70.9 %collective-permute-start.38 = (bf16[64,2048]{1,0:T(8,128)(2,1)}, bf16[64,2048]{1,0:T(8,128)(2,1)}, u32[]{:S(2)}, u32[]{:S(2)}) collective-permute-start(bf16[64,2048]{1,0:T(8,128)(2,1)} %get-tuple-element.242), channel_id=1, source_target_pairs={{0,12},{2,14},{12,0},{14,2},{4,8},{6,10},{8,4},{10,6},{1,13},{3,15... | collective-permute-start | bytes 786440 | tf_op jit(solution)/shard_map/ppermute | solution.py:281
  287.8 11.6 %collective-permute-start.39 = (bf16[64,4096]{1,0:T(8,128)(2,1)S(1)}, bf16[64,4096]{1,0:T(8,128)(2,1)S(1)}, u32[]{:S(2)}, u32[]{:S(2)}) collective-permute-start(bf16[64,4096]{1,0:T(8,128)(2,1)S(1)} %get-tuple-element.341), channel_id=1, source_target_pairs={{0,2},{2,0},{4,6},{6,4},{8,10},{10,8},{12,14},{14,12},{1,3},{3,1},... | collective-permute-start | bytes 1572872 | tf_op jit(solution)/shard_map/ppermute | solution.py:281
  291.9 18.8 %collective-permute-start.43 = (bf16[128,2048]{1,0:T(8,128)(2,1)S(1)}, bf16[128,2048]{1,0:T(8,128)(2,1)S(1)}, u32[]{:S(2)}, u32[]{:S(2)}) collective-permute-start(bf16[128,2048]{1,0:T(8,128)(2,1)S(1)} %pad_maximum_fusion.16.upper_ref.refs_10_), channel_id=1, source_target_pairs={{0,2},{2,0},{4,6},{6,4},{8,10},{10,8},{12,14},{14,12},{1,3},{3,1},... | collective-permute-start | bytes 1572872 | tf_op jit(solution)/shard_map/ppermute | solution.py:281
  292.2 40.0 %collective-permute-start.42 = (bf16[64,4096]{1,0:T(8,128)(2,1)S(1)}, bf16[64,4096]{1,0:T(8,128)(2,1)S(1)}, u32[]{:S(2)}, u32[]{:S(2)}) collective-permute-start(bf16[64,4096]{1,0:T(8,128)(2,1)S(1)} %get-tuple-element.245), channel_id=1, source_target_pairs={{0,2},{2,0},{4,6},{6,4},{8,10},{10,8},{12,14},{14,12},{1,3},{3,1},... | collective-permute-start | bytes 1572872 | tf_op jit(solution)/shard_map/ppermute | solution.py:281
  299.8 33.6 %collective-permute-start.41 = (bf16[2,64,4096]{2,1,0:T(8,128)(2,1)S(1)}, bf16[2,64,4096]{2,1,0:T(8,128)(2,1)S(1)}, u32[]{:S(2)}, u32[]{:S(2)}) collective-permute-start(bf16[2,64,4096]{2,1,0:T(8,128)(2,1)S(1)} %pad_maximum_fusion.5), channel_id=1, source_target_pairs={{0,4},{2,6},{12,8},{14,10},{1,5},{3,7},{13,9},{15,11},{16,20},{18,... | collective-permute-start | bytes 3145736 | tf_op jit(solution)/shard_map/ppermute | solution.py:281
  325.5 10.5 %collective-permute-start.46 = (bf16[256,4096]{1,0:T(8,128)(2,1)S(1)}, bf16[256,4096]{1,0:T(8,128)(2,1)S(1)}, u32[]{:S(2)}, u32[]{:S(2)}) collective-permute-start(bf16[256,4096]{1,0:T(8,128)(2,1)S(1)} %get-tuple-element.251), channel_id=1, source_target_pairs={{0,1},{1,0},{2,3},{3,2},{4,5},{5,4},{6,7},{7,6},{8,9},{9,8},{10,11... | collective-permute-start | bytes 6291464 | tf_op jit(solution)/shard_map/ppermute | solution.py:292
  334.7 24.1 %collective-permute-start.44 = (bf16[64,2048]{1,0:T(8,128)(2,1)}, bf16[64,2048]{1,0:T(8,128)(2,1)}, u32[]{:S(2)}, u32[]{:S(2)}) collective-permute-start(bf16[64,2048]{1,0:T(8,128)(2,1)} %get-tuple-element.256), channel_id=1, source_target_pairs={{0,12},{2,14},{12,0},{14,2},{4,8},{6,10},{8,4},{10,6},{1,13},{3,15... | collective-permute-start | bytes 786440 | tf_op jit(solution)/shard_map/ppermute | solution.py:281
  338.1 23.9 %collective-permute-start.48 = (bf16[64,4096]{1,0:T(8,128)(2,1)}, bf16[64,4096]{1,0:T(8,128)(2,1)}, u32[]{:S(2)}, u32[]{:S(2)}) collective-permute-start(bf16[64,4096]{1,0:T(8,128)(2,1)} %get-tuple-element.337), channel_id=1, source_target_pairs={{0,2},{2,0},{4,6},{6,4},{8,10},{10,8},{12,14},{14,12},{1,3},{3,1},... | collective-permute-start | bytes 1572872 | tf_op jit(solution)/shard_map/ppermute | solution.py:281
  355.4 9.7 %collective-permute-start.47 = (bf16[256,4096]{1,0:T(8,128)(2,1)}, bf16[256,4096]{1,0:T(8,128)(2,1)}, u32[]{:S(2)}, u32[]{:S(2)}) collective-permute-start(bf16[256,4096]{1,0:T(8,128)(2,1)} %get-tuple-element.262), channel_id=1, source_target_pairs={{0,1},{1,0},{2,3},{3,2},{4,5},{5,4},{6,7},{7,6},{8,9},{9,8},{10,11... | collective-permute-start | bytes 6291464 | tf_op jit(solution)/shard_map/ppermute | solution.py:292
  356.2 34.0 %collective-permute-start.49 = (bf16[128,2048]{1,0:T(8,128)(2,1)S(1)}, bf16[128,2048]{1,0:T(8,128)(2,1)S(1)}, u32[]{:S(2)}, u32[]{:S(2)}) collective-permute-start(bf16[128,2048]{1,0:T(8,128)(2,1)S(1)} %constant_dynamic-update-slice_fusion.14.upper_ref.refs_8_), channel_id=1, source_target_pairs={{0,2},{2,0},{4,6},{6,4},{8,10},{10,8},{12,14},{14,12},{1,3},{3,1},... | collective-permute-start | bytes 1572872 | tf_op jit(solution)/shard_map/ppermute | solution.py:281
  357.4 27.2 %collective-permute-start.50 = (bf16[2,64,4096]{2,1,0:T(8,128)(2,1)}, bf16[2,64,4096]{2,1,0:T(8,128)(2,1)S(1)}, u32[]{:S(2)}, u32[]{:S(2)}) collective-permute-start(bf16[2,64,4096]{2,1,0:T(8,128)(2,1)} %pad_maximum_fusion.6), channel_id=1, source_target_pairs={{0,4},{2,6},{12,8},{14,10},{1,5},{3,7},{13,9},{15,11},{16,20},{18,... | collective-permute-start | bytes 3145736 | tf_op jit(solution)/shard_map/ppermute | solution.py:281
  358.7 56.1 %collective-permute-start.55 = (bf16[2,64,4096]{2,1,0:T(8,128)(2,1)}, bf16[2,64,4096]{2,1,0:T(8,128)(2,1)}, u32[]{:S(2)}, u32[]{:S(2)}) collective-permute-start(bf16[2,64,4096]{2,1,0:T(8,128)(2,1)} %add_convert_fusion.11), channel_id=1, source_target_pairs={{4,8},{6,10},{8,4},{10,6},{5,9},{7,11},{9,5},{11,7},{20,24},{22,26... | collective-permute-start | bytes 3145736 | tf_op jit(solution)/shard_map/ppermute | solution.py:281
  363.7 55.3 %collective-permute-start.52 = (bf16[2,64,4096]{2,1,0:T(8,128)(2,1)S(1)}, bf16[2,64,4096]{2,1,0:T(8,128)(2,1)S(1)}, u32[]{:S(2)}, u32[]{:S(2)}) collective-permute-start(bf16[2,64,4096]{2,1,0:T(8,128)(2,1)S(1)} %pad_maximum_fusion.7), channel_id=1, source_target_pairs={{0,4},{2,6},{12,8},{14,10},{1,5},{3,7},{13,9},{15,11},{16,20},{18,... | collective-permute-start | bytes 3145736 | tf_op jit(solution)/shard_map/ppermute | solution.py:281
  385.9 62.4 %collective-permute-start.58 = (bf16[2,64,4096]{2,1,0:T(8,128)(2,1)}, bf16[2,64,4096]{2,1,0:T(8,128)(2,1)}, u32[]{:S(2)}, u32[]{:S(2)}) collective-permute-start(bf16[2,64,4096]{2,1,0:T(8,128)(2,1)} %add_convert_fusion.10), channel_id=1, source_target_pairs={{4,8},{6,10},{8,4},{10,6},{5,9},{7,11},{9,5},{11,7},{20,24},{22,26... | collective-permute-start | bytes 3145736 | tf_op jit(solution)/shard_map/ppermute | solution.py:281
  388.9 28.5 %collective-permute-start.53 = (bf16[64,4096]{1,0:T(8,128)(2,1)S(1)}, bf16[64,4096]{1,0:T(8,128)(2,1)S(1)}, u32[]{:S(2)}, u32[]{:S(2)}) collective-permute-start(bf16[64,4096]{1,0:T(8,128)(2,1)S(1)} %copy-done.18), channel_id=1, source_target_pairs={{0,2},{2,0},{4,6},{6,4},{8,10},{10,8},{12,14},{14,12},{1,3},{3,1},... | collective-permute-start | bytes 1572872 | tf_op jit(solution)/shard_map/ppermute | solution.py:281
  390.2 22.1 %collective-permute-start.54 = (bf16[64,4096]{1,0:T(8,128)(2,1)S(1)}, bf16[64,4096]{1,0:T(8,128)(2,1)S(1)}, u32[]{:S(2)}, u32[]{:S(2)}) collective-permute-start(bf16[64,4096]{1,0:T(8,128)(2,1)S(1)} %get-tuple-element.331), channel_id=1, source_target_pairs={{0,2},{2,0},{4,6},{6,4},{8,10},{10,8},{12,14},{14,12},{1,3},{3,1},... | collective-permute-start | bytes 1572872 | tf_op jit(solution)/shard_map/ppermute | solution.py:281
  412.4 10.2 %collective-permute-start.51 = (bf16[256,4096]{1,0:T(8,128)(2,1)S(1)}, bf16[256,4096]{1,0:T(8,128)(2,1)S(1)}, u32[]{:S(2)}, u32[]{:S(2)}) collective-permute-start(bf16[256,4096]{1,0:T(8,128)(2,1)S(1)} %get-tuple-element.273), channel_id=1, source_target_pairs={{0,1},{1,0},{2,3},{3,2},{4,5},{5,4},{6,7},{7,6},{8,9},{9,8},{10,11... | collective-permute-start | bytes 6291464 | tf_op jit(solution)/shard_map/ppermute | solution.py:292
  417.4 31.3 %collective-permute-start.57 = (bf16[2,64,4096]{2,1,0:T(8,128)(2,1)}, bf16[2,64,4096]{2,1,0:T(8,128)(2,1)}, u32[]{:S(2)}, u32[]{:S(2)}) collective-permute-start(bf16[2,64,4096]{2,1,0:T(8,128)(2,1)} %add_convert_fusion.9), channel_id=1, source_target_pairs={{0,4},{2,6},{4,0},{6,2},{8,12},{10,14},{12,8},{14,10},{1,5},{3,7},... | collective-permute-start | bytes 3145736 | tf_op jit(solution)/shard_map/ppermute | solution.py:281
  417.7 47.2 %collective-permute-start.61 = (bf16[2,64,4096]{2,1,0:T(8,128)(2,1)S(1)}, bf16[2,64,4096]{2,1,0:T(8,128)(2,1)}, u32[]{:S(2)}, u32[]{:S(2)}) collective-permute-start(bf16[2,64,4096]{2,1,0:T(8,128)(2,1)S(1)} %pad_maximum_fusion.9), channel_id=1, source_target_pairs={{0,4},{2,6},{12,8},{14,10},{1,5},{3,7},{13,9},{15,11},{16,20},{18,... | collective-permute-start | bytes 3145736 | tf_op jit(solution)/shard_map/ppermute | solution.py:281
  420.3 51.2 %collective-permute-start.62 = (bf16[2,64,4096]{2,1,0:T(8,128)(2,1)}, bf16[2,64,4096]{2,1,0:T(8,128)(2,1)}, u32[]{:S(2)}, u32[]{:S(2)}) collective-permute-start(bf16[2,64,4096]{2,1,0:T(8,128)(2,1)} %add_convert_fusion.8), channel_id=1, source_target_pairs={{4,8},{6,10},{8,4},{10,6},{5,9},{7,11},{9,5},{11,7},{20,24},{22,26... | collective-permute-start | bytes 3145736 | tf_op jit(solution)/shard_map/ppermute | solution.py:281
  424.4 22.4 %collective-permute-start.56 = (bf16[64,4096]{1,0:T(8,128)(2,1)S(1)}, bf16[64,4096]{1,0:T(8,128)(2,1)S(1)}, u32[]{:S(2)}, u32[]{:S(2)}) collective-permute-start(bf16[64,4096]{1,0:T(8,128)(2,1)S(1)} %copy-done.19), channel_id=1, source_target_pairs={{0,2},{2,0},{4,6},{6,4},{8,10},{10,8},{12,14},{14,12},{1,3},{3,1},... | collective-permute-start | bytes 1572872 | tf_op jit(solution)/shard_map/ppermute | solution.py:281
  446.8 56.7 %collective-permute-start.63 = (bf16[64,4096]{1,0:T(8,128)(2,1)}, bf16[64,4096]{1,0:T(8,128)(2,1)S(1)}, u32[]{:S(2)}, u32[]{:S(2)}) collective-permute-start(bf16[64,4096]{1,0:T(8,128)(2,1)} %get-tuple-element.285), channel_id=1, source_target_pairs={{0,2},{2,0},{4,6},{6,4},{8,10},{10,8},{12,14},{14,12},{1,3},{3,1},... | collective-permute-start | bytes 1572872 | tf_op jit(solution)/shard_map/ppermute | solution.py:281
  448.3 22.9 %collective-permute-start.60 = (bf16[64,4096]{1,0:T(8,128)(2,1)S(1)}, bf16[64,4096]{1,0:T(8,128)(2,1)S(1)}, u32[]{:S(2)}, u32[]{:S(2)}) collective-permute-start(bf16[64,4096]{1,0:T(8,128)(2,1)S(1)} %get-tuple-element.326), channel_id=1, source_target_pairs={{0,2},{2,0},{4,6},{6,4},{8,10},{10,8},{12,14},{14,12},{1,3},{3,1},... | collective-permute-start | bytes 1572872 | tf_op jit(solution)/shard_map/ppermute | solution.py:281
  473.0 30.8 %collective-permute-start.64 = (bf16[2,64,4096]{2,1,0:T(8,128)(2,1)S(1)}, bf16[2,64,4096]{2,1,0:T(8,128)(2,1)S(1)}, u32[]{:S(2)}, u32[]{:S(2)}) collective-permute-start(bf16[2,64,4096]{2,1,0:T(8,128)(2,1)S(1)} %add_convert_fusion.5), channel_id=1, source_target_pairs={{0,4},{2,6},{4,0},{6,2},{8,12},{10,14},{12,8},{14,10},{1,5},{3,7},... | collective-permute-start | bytes 3145736 | tf_op jit(solution)/shard_map/ppermute | solution.py:281
  475.5 28.4 %collective-permute-start.65 = (bf16[2,64,4096]{2,1,0:T(8,128)(2,1)S(1)}, bf16[2,64,4096]{2,1,0:T(8,128)(2,1)S(1)}, u32[]{:S(2)}, u32[]{:S(2)}) collective-permute-start(bf16[2,64,4096]{2,1,0:T(8,128)(2,1)S(1)} %add_convert_fusion.6), channel_id=1, source_target_pairs={{4,8},{6,10},{8,4},{10,6},{5,9},{7,11},{9,5},{11,7},{20,24},{22,26... | collective-permute-start | bytes 3145736 | tf_op jit(solution)/shard_map/ppermute | solution.py:281
  477.8 24.3 %collective-permute-start.59 = (bf16[2,64,4096]{2,1,0:T(8,128)(2,1)S(1)}, bf16[2,64,4096]{2,1,0:T(8,128)(2,1)S(1)}, u32[]{:S(2)}, u32[]{:S(2)}) collective-permute-start(bf16[2,64,4096]{2,1,0:T(8,128)(2,1)S(1)} %add_convert_fusion.7), channel_id=1, source_target_pairs={{0,1},{1,0},{2,3},{3,2},{4,5},{5,4},{6,7},{7,6},{8,9},{9,8},{10,11... | collective-permute-start | bytes 3145736 | tf_op jit(solution)/shard_map/ppermute | solution.py:292
  (24 other events, 264.9 us)
